TPU v7x, 128 devices: a whole 4x4x4 slice. The times are simulated.
128 devices in a mesh: row: 16 (over x_lo, y, core), col: 8 (over x_hi, z).
Axes of the slice: x: 4 (x_hi: 2, x_lo: 2; x = x_hi * 2 + x_lo), y: 4, z: 4, core: 2. Of those that a mesh axis runs over, the one named last changes fastest.
Arguments:
- atom_state: bfloat16 [49152, 128], P(('row', 'col')), may hold values from -6 to 6
- token_input: bfloat16 [6144, 768], P(('row', 'col')), may hold values from -6 to 6
- atom_owner: int32 [128, 384], P(('row', 'col')), may hold values from 0 to 47, never falling along the last dimension, each value on 1 to 24 neighbouring positions
- atom_bias: bfloat16 [4, 49152, 128], P(None, ('row', 'col')), may hold values from -6 to 350
- pair_bias: bfloat16 [16, 6144, 6144], P(None, 'row', 'col'), may hold values from -6 to 350
- atom_proj: bfloat16 [4, 128, 128], replicated, may hold values from -0.5 to 0.5
- atom_output: bfloat16 [128, 128], replicated, may hold values from -0.5 to 0.5
- pool_weight: bfloat16 [128, 768], replicated, may hold values from -0.5 to 0.5
- token_proj: bfloat16 [4, 768, 768], replicated, may hold values from -0.21875 to 0.21875
- token_output: bfloat16 [768, 768], replicated, may hold values from -0.21875 to 0.21875
- back_weight: bfloat16 [768, 128], replicated, may hold values from -0.21875 to 0.21875
Outputs:
- atom_result: bfloat16 [49152, 128], P(('row', 'col'))
- token_state: bfloat16 [6144, 768], P(('row', 'col'))
Inputs may be any that keep to these rules, and one draw needn't show every extreme that they name: `atom_owner`: in each row the token number never falls; every number 0 to 47 owns 1 to 24 consecutive slots, and some token owns exactly 24.
All inputs are finite; a program needn't handle non-finite values.
Results may differ from a plain program's by a relative error of at most 0.008.
Values may be sent and summed in bfloat16 or wider, within the bound.
No kernel may reach another device: no remote copies, remote signals or barrier semaphores. Data moves between devices by JAX's collectives and lax.ppermute only.
A program may use at most 192 MiB of HBM per device.

v0:
```python
import math

import jax
import jax.numpy as jnp
from jax import lax
from jax.sharding import PartitionSpec as P

HEADS = 16
ATOM_HEADS = 4
WIN_Q = 32
WIN_K = 128
REACH = 48


EPSILON = 1e-05


def padded(cells, sides, width):
    for axis, dim in sides:
        count = lax.axis_size(axis)
        ends = count - 1
        head = lax.slice_in_dim(cells, 0, width, axis=dim)
        tail = lax.slice_in_dim(cells, cells.shape[dim] - width, cells.shape[dim], axis=dim)
        cells = jnp.concatenate(
            [
                lax.ppermute(tail, axis, [(i, (i + 1) % count) for i in range(ends)]),
                cells,
                lax.ppermute(head, axis, [((i + 1) % count, i) for i in range(ends)]),
            ],
            axis=dim,
        )
    return cells


def layer_norm(values):
    centred = values - jnp.mean(values, axis=-1, keepdims=True)
    spread = jnp.mean(centred * centred, axis=-1, keepdims=True)
    return centred * lax.rsqrt(spread + EPSILON)


def make_absorb(queries, bias_rows, head_count, head_dim):
    query_count = queries.shape[0]
    query_heads = queries.reshape(query_count, head_count, head_dim)

    def absorb(running_state, pieces, first_row):
        running, denominator, numerator = running_state
        key_piece, value_piece = pieces
        length = key_piece.shape[0]
        key_heads = key_piece.reshape(length, head_count, head_dim)
        value_heads = value_piece.reshape(length, head_count, head_dim)
        scores = jnp.einsum(
            "qhd,khd->hqk", query_heads, key_heads, preferred_element_type=jnp.float32
        ) / math.sqrt(head_dim)
        scores = scores + bias_rows.astype(jnp.float32)
        newest = jnp.maximum(running, jnp.max(scores, axis=-1))
        weights = jnp.exp(scores - newest[..., None])
        denominator = jnp.sum(weights, axis=-1)
        numerator = jnp.einsum(
            "hqk,khd->hqd",
            weights.astype(jnp.bfloat16),
            value_heads,
            preferred_element_type=jnp.float32,
        )
        return (newest, denominator, numerator)

    initial = (
        jnp.full((head_count, query_count), -1e30, jnp.float32),
        jnp.zeros((head_count, query_count), jnp.float32),
        jnp.zeros((head_count, query_count, head_dim), jnp.float32),
    )
    return (absorb, initial)


def finish(running_state, head_count, head_dim):
    running, denominator, numerator = running_state
    result = numerator / denominator[..., None]
    return result.transpose(1, 0, 2).reshape(numerator.shape[1], head_count * head_dim)


def per_device(
    atom_state,
    token_input,
    atom_owner,
    atom_bias,
    pair_bias,
    atom_proj,
    atom_output,
    pool_weight,
    token_proj,
    token_output,
    back_weight,
):
    atom_count, atom_width = atom_state.shape
    head_width = atom_width // ATOM_HEADS
    windows = atom_count // WIN_Q
    window_span = WIN_K // WIN_Q
    devices = lax.axis_size("row") * lax.axis_size("col")
    first_atom = lax.axis_index(("row", "col")) * atom_count
    atom_norm = layer_norm(atom_state.astype(jnp.float32)).astype(jnp.bfloat16)
    atom_query = jnp.dot(atom_norm, atom_proj[0], preferred_element_type=jnp.float32).astype(
        jnp.bfloat16
    )
    atom_gates = jax.nn.sigmoid(
        jnp.dot(atom_norm, atom_proj[3], preferred_element_type=jnp.float32)
    )
    pair_weight = jnp.concatenate([atom_proj[1], atom_proj[2]], axis=1)
    keyvals = jnp.dot(atom_norm, pair_weight, preferred_element_type=jnp.float32).astype(
        jnp.bfloat16
    )
    extended = padded(keyvals, ((("row", "col"), 0),), REACH)
    blocks = extended.reshape(windows + window_span - 1, WIN_Q, 2 * atom_width)
    window_pairs = jnp.concatenate(
        [blocks[offset_block : offset_block + windows] for offset_block in range(window_span)],
        axis=1,
    )
    window_keys = window_pairs[:, :, :atom_width].reshape(windows, WIN_K, ATOM_HEADS, head_width)
    window_values = window_pairs[:, :, atom_width:].reshape(windows, WIN_K, ATOM_HEADS, head_width)
    query_blocks = atom_query.reshape(windows, WIN_Q, ATOM_HEADS, head_width)
    scores = jnp.einsum(
        "wqhd,wkhd->whqk", query_blocks, window_keys, preferred_element_type=jnp.float32
    ) / math.sqrt(head_width)
    scores = scores + atom_bias.reshape(ATOM_HEADS, windows, WIN_Q, WIN_K).transpose(
        1, 0, 2, 3
    ).astype(jnp.float32)
    position = (
        first_atom
        + WIN_Q * jnp.arange(windows, dtype=jnp.int32)[:, None]
        - REACH
        + jnp.arange(WIN_K, dtype=jnp.int32)[None, :]
    )
    usable = (position >= 0) & (position < atom_count * devices)
    scores = jnp.where(usable[:, None, None, :], scores, -1e30)
    weights = jax.nn.softmax(scores, axis=-1).astype(jnp.bfloat16)
    blended = jnp.einsum(
        "whqk,wkhd->wqhd", weights, window_values, preferred_element_type=jnp.float32
    ).reshape(atom_count, atom_width)
    gated_atoms = (blended * atom_gates).astype(jnp.bfloat16)
    atom_mid = atom_state.astype(jnp.float32) + jnp.dot(
        gated_atoms, atom_output, preferred_element_type=jnp.float32
    )
    owners = atom_owner[0]
    token_count = token_input.shape[0]
    onehot = (jnp.arange(token_count, dtype=jnp.int32)[:, None] == owners[None, :]).astype(
        jnp.bfloat16
    )
    lifted = jax.nn.relu(
        jnp.dot(atom_mid.astype(jnp.bfloat16), pool_weight, preferred_element_type=jnp.float32)
    ).astype(jnp.bfloat16)
    pooled_sums = jnp.dot(onehot, lifted, preferred_element_type=jnp.float32)
    counts = jnp.sum(onehot.astype(jnp.float32), axis=1)
    single = token_input.astype(jnp.float32) + pooled_sums / counts[:, None]
    token_norm = layer_norm(single).astype(jnp.bfloat16)
    width = token_proj.shape[1]
    head_dim = width // HEADS
    token_query = jnp.dot(token_norm, token_proj[0], preferred_element_type=jnp.float32).astype(
        jnp.bfloat16
    )
    token_key = jnp.dot(token_norm, token_proj[1], preferred_element_type=jnp.float32).astype(
        jnp.bfloat16
    )
    token_value = jnp.dot(token_norm, token_proj[2], preferred_element_type=jnp.float32).astype(
        jnp.bfloat16
    )
    token_gate = jax.nn.sigmoid(
        jnp.dot(token_norm, token_proj[3], preferred_element_type=jnp.float32)
    )
    bias_here = lax.all_to_all(pair_bias, "col", split_axis=1, concat_axis=2, tiled=True)
    absorb, initial = make_absorb(token_query, bias_here, HEADS, head_dim)
    final_state = absorb(
        initial,
        (
            lax.all_gather(token_key, ("row", "col"), axis=0, tiled=True),
            lax.all_gather(token_value, ("row", "col"), axis=0, tiled=True),
        ),
        jnp.int32(0),
    )
    token_gated = (finish(final_state, HEADS, head_dim) * token_gate).astype(jnp.bfloat16)
    update = jnp.dot(token_gated, token_output, preferred_element_type=jnp.float32)
    token_state = (single + update).astype(jnp.bfloat16)
    returned = jnp.dot(token_state, back_weight, preferred_element_type=jnp.float32)
    atom_result = (atom_mid + jnp.take(returned, owners, axis=0)).astype(jnp.bfloat16)
    return (atom_result, token_state)


def solution(mesh):
    placed = (
        P(("row", "col"), None),
        P(("row", "col"), None),
        P(("row", "col"), None),
        P(None, ("row", "col"), None),
        P(None, "row", "col"),
        P(),
        P(),
        P(),
        P(),
        P(),
        P(),
    )
    return jax.shard_map(
        per_device,
        mesh=mesh,
        in_specs=placed,
        out_specs=(P(("row", "col"), None), P(("row", "col"), None)),
        check_vma=False,
    )
```

profile of v0, /device:TPU:0, one launch (start us, length us, event | category | flops | bytes accessed | tf_op | source)
XLA Modules:
  0.0 800.8 jit_solution(14318995543512058665)
XLA Ops:
  10.3 1.2 convolution_convert_fusion
  11.5 3.9 collective-permute-start
  15.4 1.3 collective-permute-start.1
  16.7 1.2 convolution_convert_fusion.1
  19.0 2.1 collective-permute-done.1
  21.9 1.2 fusion.10
  23.7 2.7 convolution_bitcast_fusion
  27.1 1.2 convolution_add_fusion
  29.1 2.3 fusion.52
  31.5 2.3 fusion.55
  33.8 12.6 %copy.48 = bf16[16,384,768]{2,0,1:T(8,128)(2,1)} copy(bf16[16,384,768]{2,1,0:T(8,128)(2,1)} %param.15) | data formatting | bytes 18874368 | tf_op args[4]
  46.4 9.0 %all-to-all-start = ((bf16[16,384,768]{2,0,1:T(8,128)(2,1)}), bf16[16,384,768]{2,0,1:T(8,128)(2,1)}, u32[]{:S(2)}, u32[]{:S(2)}) async-start(bf16[16,384,768]{2,0,1:T(8,128)(2,1)} %copy.48), calls=%async_computation | async-start | bytes 18874368 | tf_op jit(solution)/shard_map/all_to_all | solution.py:167
  55.5 1.6 fusion.49
  57.4 107.3 %all-to-all-done = bf16[16,384,768]{2,0,1:T(8,128)(2,1)} async-done(((bf16[16,384,768]{2,0,1:T(8,128)(2,1)}), bf16[16,384,768]{2,0,1:T(8,128)(2,1)}, u32[]{:S(2)}, u32[]{:S(2)}) %all-to-all-start) | async-done | bytes 9437216 | tf_op jit(solution)/shard_map/all_to_all | solution.py:167
  164.7 15.6 %copy.60 = f32[16,8,48,768]{3,1,2,0:T(8,128)} copy(bf16[16,8,48,768]{3,0,2,1:T(8,128)(2,1)} %bitcast.25) | data formatting | bytes 28311552 | tf_op jit(solution)/shard_map/convert_element_type | solution.py:54
  180.3 19.3 %reshape.142 = f32[16,48,6144]{2,1,0:T(8,128)} reshape(f32[16,48,8,768]{3,2,1,0:T(8,128)} %bitcast.82) | data formatting | bytes 37748736 | tf_op jit(solution)/shard_map/convert_element_type | solution.py:54
  199.7 244.8 %all-gather.3.cloned.1.call-done = bf16[6144,768]{1,0:T(8,128)(2,1)} async-done(((bf16[48,768]{1,0:T(8,128)(2,1)}), bf16[6144,768]{1,0:T(8,128)(2,1)}) %all-gather.3.cloned.1.call-update) | async-done | bytes 9437200 | tf_op jit(solution)/shard_map/all_gather | solution.py:172
  444.5 12.7 %copy.46 = bf16[6144,768]{0,1:T(8,128)(2,1)} copy(bf16[6144,768]{1,0:T(8,128)(2,1)} %all-gather.3.cloned.1.call-done) | data formatting | bytes 18874368 | tf_op jit(solution)/shard_map/all_gather | solution.py:172
  457.2 18.6 %fusion.119 = (f32[16,48]{1,0:T(8,128)S(1)}, f32[16,48,6144]{2,1,0:T(8,128)}) fusion(f32[16,48,6144]{2,1,0:T(8,128)} %reshape.142, bf16[6144,16,48]{0,2,1:T(8,128)(2,1)} %bitcast.83, bf16[48,16,48]{2,1,0:T(8,128)(2,1)S(1)} %reshape.138), kind=kOutput, calls=%fused_computation.123 | convolution fusion | flops 467139840 | bytes 47262720 | tf_op jit(solution)/shard_map/qhd,khd->hqk/dot_general | solution.py:51
  475.8 9.0 %fusion.1 = f32[16,48]{1,0:T(8,128)S(1)} fusion(f32[16,48,6144]{2,1,0:T(8,128)} %get-tuple-element.17, f32[16,48]{1,0:T(8,128)S(1)} %broadcast_maximum_fusion), kind=kLoop, calls=%fused_computation.5 | loop fusion | flops 9436416 | bytes 18880512 | tf_op jit(solution)/shard_map/reduce_sum | solution.py:57
  484.8 280.2 %all-gather.5.cloned.1.call-done = bf16[6144,768]{1,0:T(8,128)(2,1)} async-done(((bf16[48,768]{1,0:T(8,128)(2,1)}), bf16[6144,768]{1,0:T(8,128)(2,1)}) %all-gather.5.cloned.1.call-update) | async-done | bytes 9437200 | tf_op jit(solution)/shard_map/all_gather | solution.py:173
  765.1 12.7 %copy.50 = bf16[6144,768]{0,1:T(8,128)(2,1)} copy(bf16[6144,768]{1,0:T(8,128)(2,1)} %all-gather.5.cloned.1.call-done) | data formatting | bytes 18874368 | tf_op jit(solution)/shard_map/all_gather | solution.py:173
  777.8 11.9 %fusion.64 = f32[48,16,48]{2,0,1:T(8,128)S(1)} fusion(bf16[6144,16,48]{0,2,1:T(8,128)(2,1)} %bitcast.84, f32[16,48,6144]{2,1,0:T(8,128)} %get-tuple-element.17, f32[16,48]{1,0:T(8,128)S(1)} %broadcast_maximum_fusion, f32[48,16]{0,1:T(8,128)S(1)} %bitcast.92), kind=kOutput, calls=%fused_computation.53 | convolution fusion | flops 462458880 | bytes 28465152 | tf_op jit(solution)/shard_map/hqk,khd->hqd/dot_general | solution.py:58
  790.0 1.9 fusion.58
  (52 shorter events, 9.6 us)
Async XLA Ops:
  7.2 782.8 %copy-start = (bf16[768,768]{1,0:T(8,128)(2,1)S(1)}, bf16[768,768]{1,0:T(8,128)(2,1)}, u32[]{:S(2)}) copy-start(bf16[768,768]{1,0:T(8,128)(2,1)} %param.20) | copy-start | bytes 3538948
  7.2 20.0 %copy-start.1 = (bf16[384,128]{1,0:T(8,128)(2,1)S(1)}, bf16[384,128]{1,0:T(8,128)(2,1)}, u32[]{:S(2)}) copy-start(bf16[384,128]{1,0:T(8,128)(2,1)} %param.11) | copy-start | bytes 294916
  7.2 21.1 %copy-start.5 = (bf16[128,768]{1,0:T(8,128)(2,1)S(1)}, bf16[128,768]{1,0:T(8,128)(2,1)}, u32[]{:S(2)}) copy-start(bf16[128,768]{1,0:T(8,128)(2,1)} %param.18) | copy-start | bytes 589828
  7.2 21.1 %copy-start.6 = (bf16[48,768]{1,0:T(8,128)(2,1)S(1)}, bf16[48,768]{1,0:T(8,128)(2,1)}, u32[]{:S(2)}) copy-start(bf16[48,768]{1,0:T(8,128)(2,1)} %param.12) | copy-start | bytes 221188
  7.2 437.3 %all-gather.3.cloned.1.call-start = ((), (), s32[]{:S(2)}) async-start(), calls=%async_computation.1 | async-start | bytes 9510912 | tf_op jit(solution)/shard_map/all_gather | solution.py:172
  11.5 7.5 collective-permute-start
  15.4 5.7 collective-permute-start.1
  31.4 733.6 %all-gather.5.cloned.1.call-start = ((), (), s32[]{:S(2)}) async-start(), calls=%async_computation.2 | async-start | bytes 9510912 | tf_op jit(solution)/shard_map/all_gather | solution.py:173
  46.4 9.0 %copy-start.4 = (s32[1,384]{1,0:T(1,128)S(1)}, s32[1,384]{1,0:T(1,128)}, u32[]{:S(2)}) copy-start(s32[1,384]{1,0:T(1,128)} %param.13) | copy-start | bytes 4612
  46.4 118.3 %all-to-all-start = ((bf16[16,384,768]{2,0,1:T(8,128)(2,1)}), bf16[16,384,768]{2,0,1:T(8,128)(2,1)}, u32[]{:S(2)}, u32[]{:S(2)}) async-start(bf16[16,384,768]{2,0,1:T(8,128)(2,1)} %copy.48), calls=%async_computation | async-start | bytes 18874368 | tf_op jit(solution)/shard_map/all_to_all | solution.py:167
  777.8 14.1 %copy-start.2 = (bf16[768,128]{1,0:T(8,128)(2,1)S(1)}, bf16[768,128]{1,0:T(8,128)(2,1)}, u32[]{:S(2)}) copy-start(bf16[768,128]{1,0:T(8,128)(2,1)} %param.21) | copy-start | bytes 589828
  791.9 2.1 copy-start.3
Sparse Core Ops, SparseCore 0:
  31.6 412.9 all-gather.2
  446.8 318.2 all-gather.4
where the time goes:
time: 805 us; the launch traced here: 801 us
  waiting for transfers between devices  635 us (79%)
  local copies, waits for them, and re-layouts  77 us (10%)
  matrix products  46.8 us (6%)
  starting transfers between devices  14.3 us (2%)
  between operations  14.3 us (2%)
  other arithmetic  13.8 us (2%)
    all_gather x1, waiting for transfers between devices, per_device(): lax.all_gather(token_value, ('row', 'col'), axis=0, tiled=True)  280 us
    all_gather x1, waiting for transfers between devices, per_device(): lax.all_gather(token_key, ('row', 'col'), axis=0, tiled=True)  245 us
    all_to_all x1, waiting for transfers between devices, per_device(): lax.all_to_all(pair_bias, 'col', split_axis=1, concat_axis=2, tiled=True)  107 us
    convert_element_type x2, local copies, waits for them, and re-layouts, absorb(): scores = scores + bias_rows.astype(jnp.float32)  34.9 us
    dot_general x1, matrix products, absorb(): jnp.einsum('qhd,khd->hqk', query_heads, key_heads, preferred_element_type...  18.6 us
  transfers between devices with their start and end apart: 5, of which 4 were waited for; matrix products, arithmetic and copies ran while one was open for 12% of the time, Pallas kernels for 0%

commit v1 on v0

v1 whole, which is shorter than its diff:
```python
import math

import jax
import jax.numpy as jnp
from jax import lax
from jax.experimental import pallas as pl
from jax.experimental.pallas import tpu as pltpu
from jax.sharding import PartitionSpec as P

HEADS = 16
HEAD_DIM = 48
SLOT = 64
PAIRS = HEADS // 2
ATOM_HEADS = 4
WIN_Q = 32
WIN_K = 128
REACH = 48
EPSILON = 1e-05

BOTH = ("row", "col")
F32 = jnp.float32
BF16 = jnp.bfloat16
VMEM_LIMIT = 56 * 1024 * 1024


def dot(a, b, contract=((1,), (0,))):
    return lax.dot_general(a, b, (contract, ((), ())), preferred_element_type=F32)


def layer_norm(values):
    centred = values - jnp.mean(values, axis=-1, keepdims=True)
    spread = jnp.mean(centred * centred, axis=-1, keepdims=True)
    return centred * lax.rsqrt(spread + EPSILON)


def lanes(shape, axis):
    return lax.broadcasted_iota(jnp.int32, shape, axis)


def spread_weights(proj_ref, out_ref, proj_wide, out_wide):
    width = HEADS * HEAD_DIM
    wide = HEADS * SLOT
    source = lanes((width, wide), 0)
    target = lanes((width, wide), 1)
    place = (
        (source // HEAD_DIM == target // SLOT) & (source % HEAD_DIM == target % SLOT)
    ).astype(BF16)
    for i in range(4):
        proj_wide[i] = dot(proj_ref[i], place).astype(BF16)
    out_wide[...] = dot(place, out_ref[...], ((0,), (0,))).astype(BF16)


def atom_step(
    left_ref, state_ref, right_ref, input_ref, owner_ref, bias_ref, proj_ref, output_ref,
    pool_ref, mid_ref, single_ref, norm_ref,
):
    count = state_ref.shape[0]
    windows = count // WIN_Q
    rows, cols = lax.axis_size("row"), lax.axis_size("col")
    first = (lax.axis_index("row") * cols + lax.axis_index("col")) * count
    total = count * rows * cols
    state = state_ref[...].astype(F32)
    extended = jnp.concatenate(
        [left_ref[...].astype(F32), state, right_ref[...].astype(F32)], axis=0
    )
    normed = layer_norm(extended).astype(BF16)
    keys = dot(normed, proj_ref[1]).astype(BF16)
    values = dot(normed, proj_ref[2]).astype(BF16)
    own = normed[REACH : REACH + count]
    queries = dot(own, proj_ref[0]).astype(BF16)
    gates = jax.nn.sigmoid(dot(own, proj_ref[3]))
    width = state_ref.shape[1]
    head_width = width // ATOM_HEADS
    head_of = lanes((WIN_Q, width), 1) // head_width
    factor = 1.0 / math.sqrt(head_width)
    gated = []
    for w in range(windows):
        start = w * WIN_Q
        query = queries[start : start + WIN_Q]
        stacked = jnp.concatenate(
            [jnp.where(head_of == h, query, jnp.zeros_like(query)) for h in range(ATOM_HEADS)],
            axis=0,
        )
        scores = dot(stacked, keys[start : start + WIN_K], ((1,), (1,))) * factor
        scores = scores + jnp.concatenate(
            [bias_ref[h, start : start + WIN_Q, :] for h in range(ATOM_HEADS)], axis=0
        ).astype(F32)
        if start < REACH or start + WIN_K > count + REACH:
            position = first + (start - REACH) + lanes(scores.shape, 1)
            scores = jnp.where((position >= 0) & (position < total), scores, -1e30)
        top = jnp.max(scores, axis=-1, keepdims=True)
        weights = jnp.exp(scores - top)
        weights = (weights / jnp.sum(weights, axis=-1, keepdims=True)).astype(BF16)
        mixed = dot(weights, values[start : start + WIN_K])
        mix = jnp.zeros((WIN_Q, width), F32)
        for h in range(ATOM_HEADS):
            mix = jnp.where(head_of == h, mixed[h * WIN_Q : (h + 1) * WIN_Q], mix)
        gated.append((mix * gates[start : start + WIN_Q]).astype(BF16))
    gated = jnp.concatenate(gated, axis=0)
    mid = state + dot(gated, output_ref[...])
    mid_ref[...] = mid
    lifted = jnp.maximum(dot(mid.astype(BF16), pool_ref[...]), 0.0).astype(BF16)
    tokens = input_ref.shape[0]
    owned = (lanes((tokens, count), 0) == owner_ref[...]).astype(F32)
    counts = jnp.sum(owned, axis=1, keepdims=True)
    pooled = dot(owned.astype(BF16), lifted)
    single = input_ref[...].astype(F32) + pooled / counts
    single_ref[...] = single
    norm_ref[...] = layer_norm(single).astype(BF16)


def token_step(query_ref, key_ref, bias_ref, proj_ref, part_ref, q_ref, k_ref, v_ref):
    pair = pl.program_id(0)
    lane = 2 * SLOT

    @pl.when(pair == 0)
    def _():
        wide = HEADS * SLOT
        q = dot(query_ref[...], proj_ref[0]).astype(BF16)
        k = dot(key_ref[...], proj_ref[1]).astype(BF16)
        v = dot(key_ref[...], proj_ref[2])
        v = jnp.where(lanes((1, wide), 1) % SLOT == HEAD_DIM, 1.0, v).astype(BF16)
        for p in range(PAIRS):
            q_ref[p] = q[:, p * lane : (p + 1) * lane]
            k_ref[p] = k[:, p * lane : (p + 1) * lane]
            v_ref[p] = v[:, p * lane : (p + 1) * lane]

    query = q_ref[pair]
    key = k_ref[pair]
    value = v_ref[pair]
    count = query.shape[0]
    at = lanes((count, lane), 1)
    factor = 1.0 / math.sqrt(HEAD_DIM)
    result = jnp.zeros((count, lane), F32)
    for a in range(2):
        mine = jnp.where(at // SLOT == a, query, jnp.zeros_like(query))
        scores = dot(mine, key, ((1,), (1,))) * factor + bias_ref[a].astype(F32)
        top = jnp.max(scores, axis=-1, keepdims=True)
        weights = jnp.exp(scores - top).astype(BF16)
        mixed = dot(weights, value)
        base = a * SLOT + HEAD_DIM
        mass = mixed[:, base : base + 1]
        level = top + jnp.log(mass)
        high = level.astype(BF16).astype(F32)
        middle = (level - high).astype(BF16).astype(F32)
        low = level - high - middle
        part = mixed / mass
        part = jnp.where(at == base, high, part)
        part = jnp.where(at == base + 1, middle, part)
        part = jnp.where(at == base + 2, low, part)
        result = jnp.where(at // SLOT == a, part, result)
    part_ref[...] = result.astype(BF16)


def last_step(
    part_ref, norm_ref, single_ref, mid_ref, owner_ref, proj_ref, output_ref, back_ref,
    atom_ref, token_ref,
):
    lane = 2 * SLOT
    shares, tokens, _ = part_ref.shape
    here, there = lanes((lane, lane), 0), lanes((lane, lane), 1)
    level_of = (
        (here // SLOT == there // SLOT)
        & (here % SLOT >= HEAD_DIM)
        & (here % SLOT < HEAD_DIM + 3)
    ).astype(BF16)
    gates = jax.nn.sigmoid(dot(norm_ref[...], proj_ref[0]))
    gated = []
    for p in range(PAIRS):
        span = slice(p * lane, (p + 1) * lane)
        parts = [part_ref[c, :, span] for c in range(shares)]
        levels = [dot(part, level_of) for part in parts]
        top = levels[0]
        for level in levels[1:]:
            top = jnp.maximum(top, level)
        mass = jnp.zeros((tokens, lane), F32)
        mix = jnp.zeros((tokens, lane), F32)
        for part, level in zip(parts, levels):
            weight = jnp.exp(level - top)
            mass = mass + weight
            mix = mix + weight * part.astype(F32)
        gated.append((mix / mass * gates[:, span]).astype(BF16))
    update = dot(jnp.concatenate(gated, axis=1), output_ref[...])
    token_state = (single_ref[...] + update).astype(BF16)
    token_ref[...] = token_state
    returned = dot(token_state, back_ref[...])
    high = returned.astype(BF16)
    low = (returned - high.astype(F32)).astype(BF16)
    count = mid_ref.shape[0]
    owned = (lanes((tokens, count), 0) == owner_ref[...]).astype(F32).T.astype(BF16)
    atom_ref[...] = (mid_ref[...] + dot(owned, high) + dot(owned, low)).astype(BF16)


def call(kernel, out, cost, **more):
    flops, size = cost
    return pl.pallas_call(
        kernel,
        out_shape=out,
        compiler_params=pltpu.CompilerParams(vmem_limit_bytes=VMEM_LIMIT),
        cost_estimate=pl.CostEstimate(flops=flops, bytes_accessed=size, transcendentals=0),
        **more,
    )


def shape(dims, kind):
    return jax.ShapeDtypeStruct(dims, kind)


def per_device(
    atom_state, token_input, atom_owner, atom_bias, pair_bias, atom_proj, atom_output,
    pool_weight, token_proj, token_output, back_weight,
):
    rows, cols = lax.axis_size("row"), lax.axis_size("col")
    devices = rows * cols
    count, width = atom_state.shape
    tokens, depth = token_input.shape
    wide = HEADS * SLOT
    ends = devices - 1
    left = lax.ppermute(
        atom_state[count - REACH :], BOTH, [(i, i + 1) for i in range(ends)]
    )
    right = lax.ppermute(atom_state[:REACH], BOTH, [(i + 1, i) for i in range(ends)])
    proj_wide, output_wide = call(
        spread_weights,
        (shape((4, depth, wide), BF16), shape((wide, depth), BF16)),
        (10 * depth * depth * wide, 14_000_000),
    )(token_proj, token_output)
    mid, single, norm = call(
        atom_step,
        (
            shape((count, width), F32),
            shape((tokens, depth), F32),
            shape((tokens, depth), BF16),
        ),
        (400_000_000, 2_000_000),
    )(
        left, atom_state, right, token_input, atom_owner, atom_bias, atom_proj, atom_output,
        pool_weight,
    )
    half = rows // cols
    turn = []
    for r in range(rows):
        for c in range(cols):
            turn.append((r * cols + c, ((r % half) * cols + c) * cols + r // half))
    turned = lax.ppermute(norm, BOTH, turn)
    queries = lax.all_to_all(
        jnp.broadcast_to(norm[None], (cols, tokens, depth)), "col", 0, 0
    ).reshape(cols * tokens, depth)
    keys = lax.all_to_all(
        jnp.broadcast_to(turned[None], (rows, tokens, depth)), "row", 0, 0
    ).reshape(rows * tokens, depth)
    q_count, k_count = cols * tokens, rows * tokens
    lane = 2 * SLOT
    whole = lambda *dims: pl.BlockSpec(dims, lambda p: (0,) * len(dims))
    parts = call(
        token_step,
        shape((q_count, wide), BF16),
        (8_000_000_000, 14_000_000),
        grid=(PAIRS,),
        in_specs=[
            whole(q_count, depth),
            whole(k_count, depth),
            pl.BlockSpec((2, q_count, k_count), lambda p: (p, 0, 0)),
            whole(3, depth, wide),
        ],
        out_specs=pl.BlockSpec((q_count, lane), lambda p: (0, p)),
        scratch_shapes=[
            pltpu.VMEM((PAIRS, q_count, lane), BF16),
            pltpu.VMEM((PAIRS, k_count, lane), BF16),
            pltpu.VMEM((PAIRS, k_count, lane), BF16),
        ],
    )(queries, keys, pair_bias, proj_wide)
    parts = lax.all_to_all(parts.reshape(cols, tokens, wide), "col", 0, 0)
    full = lambda *dims: pl.BlockSpec(dims, lambda i: (0,) * len(dims))
    return call(
        last_step,
        (shape((count, width), BF16), shape((tokens, depth), BF16)),
        (400_000_000, 5_000_000),
        grid=(1,),
        in_specs=[
            full(cols, tokens, wide),
            full(tokens, depth),
            full(tokens, depth),
            full(count, width),
            full(1, count),
            pl.BlockSpec((1, depth, wide), lambda i: (3, 0, 0)),
            full(wide, depth),
            full(depth, width),
        ],
        out_specs=(full(count, width), full(tokens, depth)),
    )(parts, norm, single, mid, atom_owner, proj_wide, output_wide, back_weight)


def solution(mesh):
    split = P(BOTH, None)
    placed = (
        split, split, split, P(None, BOTH, None), P(None, "row", "col"),
        P(), P(), P(), P(), P(), P(),
    )
    return jax.shard_map(
        per_device, mesh=mesh, in_specs=placed, out_specs=(split, split), check_vma=False
    )
```

time: 805 us -> 113 us (0.14)
  waiting for transfers between devices: 635 us -> 19.8 us
  local copies, waits for them, and re-layouts: 77 us -> 5.51 us
  matrix products: 46.8 us -> 0 us
  Pallas kernels: 0 us -> 40.7 us
  blocking collectives: 0 us -> 19.6 us
  other arithmetic: 13.8 us -> 0 us
  between operations: 14.3 us -> 0.7 us
  starting transfers between devices: 14.3 us -> 26.2 us
    all_gather x2 -> x0, waiting for transfers between devices: 525 us -> none  [the longest x1 280 us: per_device(): lax.all_gather(token_value, ('row', 'col'), axis=0, tiled=True)]
    all_to_all x1 -> x2, waiting for transfers between devices: 107 us -> 18.5 us  [the longest x1 11.5 us: per_device(): lax.all_to_all(jnp.broadcast_to(norm[None], (cols, tokens, depth)), 'col'...]
    dot_general x13 -> x0, matrix products: 46.8 us -> none  [the longest x1 18.6 us: absorb(): jnp.einsum('qhd,khd->hqk', query_heads, key_heads, preferred_element_type...]
    pallas_call x0 -> x4, Pallas kernels: none -> 40.7 us  [the longest x1 18.4 us: per_device(): call(token_step, shape((q_count, wide), BF16), (8000000000, 14000000), gr...]
    convert_element_type x2 -> x0, local copies, waits for them, and re-layouts: 34.9 us -> none  [absorb(): scores = scores + bias_rows.astype(jnp.float32)]
    all_gather x2 -> x0, local copies, waits for them, and re-layouts: 25.4 us -> none  [the longest x1 12.7 us: per_device(): lax.all_gather(token_value, ('row', 'col'), axis=0, tiled=True)]
    all_to_all x0 -> x1, blocking collectives: none -> 19.6 us  [per_device(): parts = lax.all_to_all(parts.reshape(cols, tokens, wide), 'col', 0, 0)]
    reduce_sum x5 -> x0, other arithmetic: 11.6 us -> none  [the longest x1 9.03 us: absorb(): denominator = jnp.sum(weights, axis=-1)]
  transfers between devices with their start and end apart: 5 -> 5, of which waited for: 4 -> 3; matrix products, arithmetic and copies ran while one was open for 12% -> 0% of each run, Pallas kernels for 0% -> 10%
where the time goes in v1:
time: 113 us
  Pallas kernels  40.7 us (36%)
  starting transfers between devices  26.2 us (23%)
  waiting for transfers between devices  19.8 us (18%)
  blocking collectives  19.6 us (17%)
  local copies, waits for them, and re-layouts  5.51 us (5%)
    all_to_all x1, blocking collectives, per_device(): parts = lax.all_to_all(parts.reshape(cols, tokens, wide), 'col', 0, 0)  19.6 us
    pallas_call x1, Pallas kernels, per_device(): call(token_step, shape((q_count, wide), BF16), (8000000000, 14000000), gr...  18.4 us
    all_to_all x1, starting transfers between devices, per_device(): lax.all_to_all(jnp.broadcast_to(norm[None], (cols, tokens, depth)), 'col'...  12.2 us
    all_to_all x1, waiting for transfers between devices, per_device(): lax.all_to_all(jnp.broadcast_to(norm[None], (cols, tokens, depth)), 'col'...  11.5 us
    pallas_call x1, Pallas kernels, per_device(): call(spread_weights, (shape((4, depth, wide), BF16), shape((wide, depth),...  11.1 us
    all_to_all x1, starting transfers between devices, per_device(): lax.all_to_all(jnp.broadcast_to(turned[None], (rows, tokens, depth)), 'ro...  7.47 us
    all_to_all x1, waiting for transfers between devices, per_device(): lax.all_to_all(jnp.broadcast_to(turned[None], (rows, tokens, depth)), 'ro...  7 us
    pallas_call x1, Pallas kernels, per_device(): call(atom_step, (shape((count, width), F32), shape((tokens, depth), F32),...  6.58 us
  transfers between devices with their start and end apart: 5, of which 3 were waited for; matrix products, arithmetic and copies ran while one was open for 0% of the time, Pallas kernels for 10%

profile of v1, /device:TPU:0, one launch (start us, length us, event | category | flops | bytes accessed | tf_op | source)
XLA Modules:
  0.0 112.5 jit_solution(428533111750300544)
XLA Ops:
  0.6 0.7 fusion
  1.4 1.3 %collective-permute-start.1 = (bf16[48,128]{1,0:T(8,128)(2,1)S(1)}, bf16[48,128]{1,0:T(8,128)(2,1)S(1)}, u32[]{:S(2)}, u32[]{:S(2)}) collective-permute-start(bf16[48,128]{1,0:T(8,128)(2,1)S(1)} %get-tuple-element.12), channel_id=1, source_target_pairs={{1,0},{2,1},{3,2},{4,3},{5,4},{6,5},{7,6},{8,7},{9,8},{10,9},{11,1... | collective-permute-start | bytes 36872 | tf_op jit(solution)/shard_map/ppermute | solution.py:222
  2.6 4.5 %collective-permute-start = (bf16[48,128]{1,0:T(8,128)(2,1)S(1)}, bf16[48,128]{1,0:T(8,128)(2,1)S(1)}, u32[]{:S(2)}, u32[]{:S(2)}) collective-permute-start(bf16[48,128]{1,0:T(8,128)(2,1)S(1)} %get-tuple-element.13), channel_id=1, source_target_pairs={{0,1},{1,2},{2,3},{3,4},{4,5},{5,6},{6,7},{7,8},{8,9},{9,10},{10,1... | collective-permute-start | bytes 36872 | tf_op jit(solution)/shard_map/ppermute | solution.py:219
  7.2 0.0 collective-permute-done.1.right_ref
  7.2 0.0 copy-start.3
  7.2 1.4 %collective-permute-done.left_ref = bf16[48,128]{1,0:T(8,128)(2,1)S(1)} collective-permute-done((bf16[48,128]{1,0:T(8,128)(2,1)S(1)}, bf16[48,128]{1,0:T(8,128)(2,1)S(1)}, u32[]{:S(2)}, u32[]{:S(2)}) %collective-permute-start) | collective-permute-done | bytes 12320 | tf_op jit(solution)/shard_map/ppermute | solution.py:219
  8.6 0.0 copy-done.3
  8.6 0.6 copy-done.4
  9.2 6.6 %shard_map.122 = (f32[384,128]{1,0:T(8,128)}, f32[48,768]{1,0:T(8,128)}, bf16[48,768]{1,0:T(8,128)(2,1)}) custom-call(bf16[48,128]{1,0:T(8,128)(2,1)} %copy-done.4, bf16[384,128]{1,0:T(8,128)(2,1)} %state_ref.1, bf16[48,128]{1,0:T(8,128)(2,1)} %copy-done.3, bf16[48,768]{1,0:T(8,128)(2,1)} %input_ref.1, s32[1,384]{1,0:T(1,128)} %owner_ref.3, ...), custom_call_target="tpu_custom_call" | custom-call | flops 400000000 | bytes 2000000 | tf_op jit(solution)/shard_map/pallas_call | solution.py:228
  15.8 1.8 %broadcast_in_dim.4 = bf16[8,48,768]{2,1,0:T(8,128)(2,1)} broadcast(bf16[48,768]{1,0:T(8,128)(2,1)} %get-tuple-element.7.norm_ref), dimensions={1,2} | broadcast | bytes 663552 | tf_op jit(solution)/shard_map/broadcast_in_dim | solution.py:247
  17.6 12.2 %all-to-all-start = ((bf16[8,48,768]{2,1,0:T(8,128)(2,1)}), bf16[8,48,768]{2,1,0:T(8,128)(2,1)S(1)}, u32[]{:S(2)}, u32[]{:S(2)}) async-start(bf16[8,48,768]{2,1,0:T(8,128)(2,1)} %broadcast_in_dim.4), calls=%async_computation | async-start | bytes 1179648 | tf_op jit(solution)/shard_map/all_to_all | solution.py:246
  29.8 0.0 copy-done.2
  29.8 0.7 collective-permute-start.2
  30.5 0.0 collective-permute-done.2
  30.5 11.5 %all-to-all-done = bf16[8,48,768]{2,1,0:T(8,128)(2,1)S(1)} async-done(((bf16[8,48,768]{2,1,0:T(8,128)(2,1)}), bf16[8,48,768]{2,1,0:T(8,128)(2,1)S(1)}, u32[]{:S(2)}, u32[]{:S(2)}) %all-to-all-start) | async-done | bytes 589856 | tf_op jit(solution)/shard_map/all_to_all | solution.py:246
  42.0 1.2 %broadcast_in_dim.5 = bf16[16,48,768]{2,1,0:T(8,128)(2,1)} broadcast(bf16[48,768]{1,0:T(8,128)(2,1)S(1)} %collective-permute-done.2), dimensions={1,2} | broadcast | bytes 1253376 | tf_op jit(solution)/shard_map/broadcast_in_dim | solution.py:250
  43.2 0.1 copy-done.1
  43.3 7.5 %all-to-all-start.1 = ((bf16[16,48,768]{2,1,0:T(8,128)(2,1)}), bf16[16,48,768]{2,1,0:T(8,128)(2,1)S(1)}, u32[]{:S(2)}, u32[]{:S(2)}) async-start(bf16[16,48,768]{2,1,0:T(8,128)(2,1)} %broadcast_in_dim.5), calls=%async_computation.1 | async-start | bytes 2359296 | tf_op jit(solution)/shard_map/all_to_all | solution.py:249
  50.7 11.1 %shard_map.123 = (bf16[4,768,1024]{2,1,0:T(8,128)(2,1)}, bf16[1024,768]{1,0:T(8,128)(2,1)}) custom-call(bf16[4,768,768]{2,1,0:T(8,128)(2,1)} %proj_ref.3, bf16[768,768]{1,0:T(8,128)(2,1)} %out_ref.1), custom_call_target="tpu_custom_call" | custom-call | flops 6039797760 | bytes 14000000 | tf_op jit(solution)/shard_map/pallas_call | solution.py:223
  61.8 7.0 %all-to-all-done.1 = bf16[16,48,768]{2,1,0:T(8,128)(2,1)S(1)} async-done(((bf16[16,48,768]{2,1,0:T(8,128)(2,1)}), bf16[16,48,768]{2,1,0:T(8,128)(2,1)S(1)}, u32[]{:S(2)}, u32[]{:S(2)}) %all-to-all-start.1) | async-done | bytes 1179680 | tf_op jit(solution)/shard_map/all_to_all | solution.py:249
  68.8 1.1 copy-done
  69.9 18.4 %shard_map.124 = bf16[384,1024]{1,0:T(8,128)(2,1)} custom-call(bf16[384,768]{1,0:T(8,128)(2,1)} %bitcast.5, bf16[768,768]{1,0:T(8,128)(2,1)} %bitcast.3, bf16[16,384,768]{2,1,0:T(8,128)(2,1)} %bias_ref.3, bf16[4,768,1024]{2,1,0:T(8,128)(2,1)} %get-tuple-element.8.proj_ref), custom_call_target="tpu_custom_call" | custom-call | flops 8000000000 | bytes 14000000 | tf_op jit(solution)/shard_map/pallas_call | solution.py:255
  88.3 19.6 %all_to_all.15.part_ref = bf16[8,48,1024]{2,1,0:T(8,128)(2,1)} all-to-all(bf16[8,48,1024]{2,1,0:T(8,128)(2,1)} %bitcast.4), channel_id=1, replica_groups=mesh['row'=16,'col'=8] {'col'}, dimensions={0} | all-to-all | bytes 1572864 | tf_op jit(solution)/shard_map/all_to_all | solution.py:273
  107.9 4.7 %shard_map.125 = (bf16[384,128]{1,0:T(8,128)(2,1)}, bf16[48,768]{1,0:T(8,128)(2,1)}) custom-call(bf16[8,48,1024]{2,1,0:T(8,128)(2,1)} %all_to_all.15.part_ref, bf16[48,768]{1,0:T(8,128)(2,1)} %get-tuple-element.7.norm_ref, f32[48,768]{1,0:T(8,128)} %get-tuple-element.9.single_ref, f32[384,128]{1,0:T(8,128)} %get-tuple-element.10.mid_ref, ...), custom_call_target="tpu_custom_call" | custom-call | flops 400000000 | bytes 5000000 | tf_op jit(solution)/shard_map/pallas_call | solution.py:275
  (4 shorter events, 0.0 us)
Async XLA Ops:
  1.4 5.8 %collective-permute-start.1 = (bf16[48,128]{1,0:T(8,128)(2,1)S(1)}, bf16[48,128]{1,0:T(8,128)(2,1)S(1)}, u32[]{:S(2)}, u32[]{:S(2)}) collective-permute-start(bf16[48,128]{1,0:T(8,128)(2,1)S(1)} %get-tuple-element.12), channel_id=1, source_target_pairs={{1,0},{2,1},{3,2},{4,3},{5,4},{6,5},{7,6},{8,7},{9,8},{10,9},{11,1... | collective-permute-start | bytes 36872 | tf_op jit(solution)/shard_map/ppermute | solution.py:222
  2.6 5.9 %collective-permute-start = (bf16[48,128]{1,0:T(8,128)(2,1)S(1)}, bf16[48,128]{1,0:T(8,128)(2,1)S(1)}, u32[]{:S(2)}, u32[]{:S(2)}) collective-permute-start(bf16[48,128]{1,0:T(8,128)(2,1)S(1)} %get-tuple-element.13), channel_id=1, source_target_pairs={{0,1},{1,2},{2,3},{3,4},{4,5},{5,6},{6,7},{7,8},{8,9},{9,10},{10,1... | collective-permute-start | bytes 36872 | tf_op jit(solution)/shard_map/ppermute | solution.py:219
  7.2 1.4 %copy-start.3 = (bf16[48,128]{1,0:T(8,128)(2,1)}, bf16[48,128]{1,0:T(8,128)(2,1)S(1)}, u32[]{:S(2)}) copy-start(bf16[48,128]{1,0:T(8,128)(2,1)S(1)} %collective-permute-done.1.right_ref) | copy-start | bytes 36868
  8.6 0.6 copy-start.4
  15.8 14.1 %copy-start.2 = (bf16[48,768]{1,0:T(8,128)(2,1)S(1)}, bf16[48,768]{1,0:T(8,128)(2,1)}, u32[]{:S(2)}) copy-start(bf16[48,768]{1,0:T(8,128)(2,1)} %get-tuple-element.7.norm_ref) | copy-start | bytes 221188
  17.6 24.4 %all-to-all-start = ((bf16[8,48,768]{2,1,0:T(8,128)(2,1)}), bf16[8,48,768]{2,1,0:T(8,128)(2,1)S(1)}, u32[]{:S(2)}, u32[]{:S(2)}) async-start(bf16[8,48,768]{2,1,0:T(8,128)(2,1)} %broadcast_in_dim.4), calls=%async_computation | async-start | bytes 1179648 | tf_op jit(solution)/shard_map/all_to_all | solution.py:246
  29.8 0.7 collective-permute-start.2
  42.0 1.3 %copy-start.1 = (bf16[8,48,768]{2,1,0:T(8,128)(2,1)}, bf16[8,48,768]{2,1,0:T(8,128)(2,1)S(1)}, u32[]{:S(2)}) copy-start(bf16[8,48,768]{2,1,0:T(8,128)(2,1)S(1)} %all-to-all-done) | copy-start | bytes 1769476
  43.3 25.5 %all-to-all-start.1 = ((bf16[16,48,768]{2,1,0:T(8,128)(2,1)}), bf16[16,48,768]{2,1,0:T(8,128)(2,1)S(1)}, u32[]{:S(2)}, u32[]{:S(2)}) async-start(bf16[16,48,768]{2,1,0:T(8,128)(2,1)} %broadcast_in_dim.5), calls=%async_computation.1 | async-start | bytes 2359296 | tf_op jit(solution)/shard_map/all_to_all | solution.py:249
  68.8 1.1 copy-start

commit v2 on v1

v2 whole, which is shorter than its diff:
```python
import math

import jax
import jax.numpy as jnp
from jax import lax
from jax.experimental import pallas as pl
from jax.experimental.pallas import tpu as pltpu
from jax.sharding import PartitionSpec as P

HEADS = 16
HEAD_DIM = 48
SLOT = 64
PAIRS = HEADS // 2
ATOM_HEADS = 4
WIN_Q = 32
WIN_K = 128
REACH = 48
EPSILON = 1e-05

BOTH = ("row", "col")
F32 = jnp.float32
BF16 = jnp.bfloat16
ORDER = (2, 3, 0, 1, 6, 7, 4, 5)


def dot(a, b, contract=((1,), (0,))):
    return lax.dot_general(a, b, (contract, ((), ())), preferred_element_type=F32)


def layer_norm(values):
    centred = values - jnp.mean(values, axis=-1, keepdims=True)
    spread = jnp.mean(centred * centred, axis=-1, keepdims=True)
    return centred * lax.rsqrt(spread + EPSILON)


def lanes(shape, axis):
    return lax.broadcasted_iota(jnp.int32, shape, axis)


BAND = 2 * 2 * SLOT
STARTS = (0, 128, 384, 512)


def band_place(group, back=False):
    near = lanes((BAND, BAND), 1 if back else 0) + STARTS[group]
    far = lanes((BAND, BAND), 0 if back else 1) + group * BAND
    return ((near // HEAD_DIM == far // SLOT) & (near % HEAD_DIM == far % SLOT)).astype(BF16)


def spread(values):
    return [
        dot(values[:, STARTS[g] : STARTS[g] + BAND], band_place(g)) for g in range(HEADS // 4)
    ]


def gather_lanes(values):
    parts = [dot(values[g], band_place(g, True)) for g in range(HEADS // 4)]
    lane = 2 * SLOT
    return jnp.concatenate(
        [
            parts[0][:, :lane],
            parts[0][:, lane:] + parts[1][:, :lane],
            parts[1][:, lane:],
            parts[2][:, :lane],
            parts[2][:, lane:] + parts[3][:, :lane],
            parts[3][:, lane:],
        ],
        axis=1,
    )


def store_pairs(ref, bands):
    lane = 2 * SLOT
    for g, band in enumerate(bands):
        ref[2 * g] = band[:, :lane].astype(BF16)
        ref[2 * g + 1] = band[:, lane:].astype(BF16)


def atom_step(
    left_ref, state_ref, right_ref, input_ref, owner_ref, bias_ref, proj_ref, output_ref,
    pool_ref, mid_ref, single_ref, norm_ref,
):
    count = state_ref.shape[0]
    windows = count // WIN_Q
    rows, cols = lax.axis_size("row"), lax.axis_size("col")
    first = (lax.axis_index("row") * cols + lax.axis_index("col")) * count
    total = count * rows * cols
    state = state_ref[...].astype(F32)
    extended = jnp.concatenate(
        [left_ref[...].astype(F32), state, right_ref[...].astype(F32)], axis=0
    )
    normed = layer_norm(extended).astype(BF16)
    keys = dot(normed, proj_ref[1]).astype(BF16)
    values = dot(normed, proj_ref[2]).astype(BF16)
    own = normed[REACH : REACH + count]
    queries = dot(own, proj_ref[0]).astype(BF16)
    gates = jax.nn.sigmoid(dot(own, proj_ref[3]))
    width = state_ref.shape[1]
    head_width = width // ATOM_HEADS
    head_of = lanes((WIN_Q, width), 1) // head_width
    factor = 1.0 / math.sqrt(head_width)
    gated = []
    for w in range(windows):
        start = w * WIN_Q
        query = queries[start : start + WIN_Q]
        stacked = jnp.concatenate(
            [jnp.where(head_of == h, query, jnp.zeros_like(query)) for h in range(ATOM_HEADS)],
            axis=0,
        )
        scores = dot(stacked, keys[start : start + WIN_K], ((1,), (1,))) * factor
        scores = scores + jnp.concatenate(
            [bias_ref[h, start : start + WIN_Q, :] for h in range(ATOM_HEADS)], axis=0
        ).astype(F32)
        if start < REACH or start + WIN_K > count + REACH:
            position = first + (start - REACH) + lanes(scores.shape, 1)
            scores = jnp.where((position >= 0) & (position < total), scores, -1e30)
        top = jnp.max(scores, axis=-1, keepdims=True)
        weights = jnp.exp(scores - top)
        weights = (weights / jnp.sum(weights, axis=-1, keepdims=True)).astype(BF16)
        mixed = dot(weights, values[start : start + WIN_K])
        mix = jnp.zeros((WIN_Q, width), F32)
        for h in range(ATOM_HEADS):
            mix = jnp.where(head_of == h, mixed[h * WIN_Q : (h + 1) * WIN_Q], mix)
        gated.append((mix * gates[start : start + WIN_Q]).astype(BF16))
    gated = jnp.concatenate(gated, axis=0)
    mid = state + dot(gated, output_ref[...])
    mid_ref[...] = mid
    lifted = jnp.maximum(dot(mid.astype(BF16), pool_ref[...]), 0.0).astype(BF16)
    tokens = input_ref.shape[0]
    owned = (lanes((tokens, count), 0) == owner_ref[...]).astype(F32)
    counts = jnp.sum(owned, axis=1, keepdims=True)
    pooled = dot(owned.astype(BF16), lifted)
    single = input_ref[...].astype(F32) + pooled / counts
    single_ref[...] = single
    norm_ref[...] = layer_norm(single).astype(BF16)


def query_step(own_ref, after_ref, before_ref, far_ref, norm_ref, proj_ref, q_ref, gate_ref):
    tokens = norm_ref.shape[0]
    lane = 2 * SLOT
    rows = jnp.concatenate(
        [own_ref[...], after_ref[...], before_ref[...], far_ref[...]], axis=0
    )
    bands = spread(dot(rows, proj_ref[0]).astype(BF16))
    ring = lax.axis_size("col") // 2
    me = lax.axis_index("col")
    high, low = me // ring, me % ring
    for i, step in enumerate((0, ring - 1, 1, 2)):
        for j in range(2):
            source = lax.rem(high + j, 2) * ring + lax.rem(low + step, ring)
            at = pl.ds(pl.multiple_of(source * tokens, 16), tokens)
            first = (2 * i + j) * tokens
            for g, band in enumerate(bands):
                block = band[first : first + tokens].astype(BF16)
                q_ref[2 * g, at, :] = block[:, :lane]
                q_ref[2 * g + 1, at, :] = block[:, lane:]
    gates = jax.nn.sigmoid(dot(norm_ref[...], proj_ref[3]))
    top = gates.astype(BF16)
    rest = (gates - top.astype(F32)).astype(BF16)
    for g, (a, b) in enumerate(zip(spread(top), spread(rest))):
        gate_ref[:, g * BAND : (g + 1) * BAND] = a + b


def project(blocks_ref, proj_ref, k_ref, v_ref):
    rows = jnp.concatenate([blocks_ref[i] for i in ORDER], axis=0)
    store_pairs(k_ref, spread(dot(rows, proj_ref[1]).astype(BF16)))
    mass = lanes((1, BAND), 1) % SLOT == HEAD_DIM
    bands = spread(dot(rows, proj_ref[2]).astype(BF16))
    store_pairs(v_ref, [jnp.where(mass, 1.0, band) for band in bands])


def token_step(
    q_ref, k_ref, v_ref, blocks_ref, proj_ref, bias_hbm, part_ref, bias_ref, other_k, other_v,
    sems,
):
    lane = 2 * SLOT
    copies = [
        pltpu.make_async_copy(bias_hbm.at[h], bias_ref.at[h], sems.at[h]) for h in range(HEADS)
    ]
    for copy in copies:
        copy.start()
    project(blocks_ref, proj_ref, other_k, other_v)
    core = lax.rem(lax.axis_index("row"), 2)
    count, half = q_ref.shape[1], k_ref.shape[1]
    mine_at = pl.ds(pl.multiple_of(core * half, lane), half)
    other_at = pl.ds(pl.multiple_of((1 - core) * half, lane), half)
    at = lanes((count, lane), 1)
    factor = 1.0 / math.sqrt(HEAD_DIM)
    for pair in range(PAIRS):
        query = q_ref[pair]
        result = jnp.zeros((count, lane), F32)
        for a in range(2):
            head = 2 * pair + a
            copies[head].wait()
            mine = jnp.where(at // SLOT == a, query, jnp.zeros_like(query))
            near = dot(mine, k_ref[pair], ((1,), (1,))) * factor
            near = near + bias_ref[head, :, mine_at].astype(F32)
            far = dot(mine, other_k[pair], ((1,), (1,))) * factor
            far = far + bias_ref[head, :, other_at].astype(F32)
            top = jnp.maximum(
                jnp.max(near, axis=-1, keepdims=True), jnp.max(far, axis=-1, keepdims=True)
            )
            mixed = dot(jnp.exp(near - top).astype(BF16), v_ref[pair])
            mixed = mixed + dot(jnp.exp(far - top).astype(BF16), other_v[pair])
            base = a * SLOT + HEAD_DIM
            mass = mixed[:, base : base + 1]
            level = top + jnp.log(mass)
            high = level.astype(BF16).astype(F32)
            middle = (level - high).astype(BF16).astype(F32)
            low = level - high - middle
            part = mixed / mass
            part = jnp.where(at == base, high, part)
            part = jnp.where(at == base + 1, middle, part)
            part = jnp.where(at == base + 2, low, part)
            result = jnp.where(at // SLOT == a, part, result)
        part_ref[:, pair * lane : (pair + 1) * lane] = result.astype(BF16)


def last_step(
    part_ref, gate_ref, single_ref, mid_ref, owner_ref, output_ref, back_ref, atom_ref,
    token_ref,
):
    lane = 2 * SLOT
    shares, tokens, _ = part_ref.shape
    here, there = lanes((lane, lane), 0), lanes((lane, lane), 1)
    level_of = (
        (here // SLOT == there // SLOT)
        & (here % SLOT >= HEAD_DIM)
        & (here % SLOT < HEAD_DIM + 3)
    ).astype(BF16)
    gated = []
    for p in range(PAIRS):
        span = slice(p * lane, (p + 1) * lane)
        parts = [part_ref[c, :, span] for c in range(shares)]
        levels = [dot(part, level_of) for part in parts]
        top = levels[0]
        for level in levels[1:]:
            top = jnp.maximum(top, level)
        mass = jnp.zeros((tokens, lane), F32)
        mix = jnp.zeros((tokens, lane), F32)
        for part, level in zip(parts, levels):
            weight = jnp.exp(level - top)
            mass = mass + weight
            mix = mix + weight * part.astype(F32)
        gated.append((mix / mass * gate_ref[:, span]).astype(BF16))
    gated = [jnp.concatenate(gated[g : g + 2], axis=1) for g in range(0, PAIRS, 2)]
    update = dot(gather_lanes(gated).astype(BF16), output_ref[...])
    token_state = (single_ref[...] + update).astype(BF16)
    token_ref[...] = token_state
    returned = dot(token_state, back_ref[...])
    high = returned.astype(BF16)
    low = (returned - high.astype(F32)).astype(BF16)
    count = mid_ref.shape[0]
    owned = (lanes((tokens, count), 0) == owner_ref[...]).astype(F32).T.astype(BF16)
    atom_ref[...] = (mid_ref[...] + dot(owned, high) + dot(owned, low)).astype(BF16)


def call(kernel, out, megabytes, cost, **more):
    flops, size = cost
    return pl.pallas_call(
        kernel,
        out_shape=out,
        compiler_params=pltpu.CompilerParams(vmem_limit_bytes=megabytes * 1024 * 1024),
        cost_estimate=pl.CostEstimate(flops=flops, bytes_accessed=size, transcendentals=0),
        **more,
    )


def shape(dims, kind):
    return jax.ShapeDtypeStruct(dims, kind)


def per_device(
    atom_state, token_input, atom_owner, atom_bias, pair_bias, atom_proj, atom_output,
    pool_weight, token_proj, token_output, back_weight,
):
    rows, cols = lax.axis_size("row"), lax.axis_size("col")
    devices = rows * cols
    count, width = atom_state.shape
    tokens, depth = token_input.shape
    wide = HEADS * SLOT
    ends = devices - 1
    left = lax.ppermute(
        atom_state[count - REACH :], BOTH, [(i, i + 1) for i in range(ends)]
    )
    right = lax.ppermute(atom_state[:REACH], BOTH, [(i + 1, i) for i in range(ends)])
    mid, single, norm = call(
        atom_step,
        (
            shape((count, width), F32),
            shape((tokens, depth), F32),
            shape((tokens, depth), BF16),
        ),
        12,
        (400_000_000, 2_000_000),
    )(
        left, atom_state, right, token_input, atom_owner, atom_bias, atom_proj, atom_output,
        pool_weight,
    )
    ring = cols // 2
    turn = []
    for r in range(rows):
        for c in range(cols):
            to_row = (c // ring) * cols + 2 * ((c % ring + 2) % ring) + r % 2
            turn.append((r * cols + c, to_row * cols + r // 2))
    turned = lax.ppermute(norm, BOTH, turn)
    across = lax.ppermute(norm, "col", [(i, (i + ring) % cols) for i in range(cols)])
    own = jnp.concatenate([norm, across], axis=0)
    turned, own = lax.optimization_barrier((turned, own))
    same_core = [[i for i in range(rows) if i % 2 == e] for e in range(2)]
    near = lax.all_to_all(
        jnp.broadcast_to(turned[None], (rows // 2, tokens, depth)), "row", 0, 0,
        axis_index_groups=same_core,
    )
    along = [
        lax.ppermute(
            own, "col", [(i, i // ring * ring + (i + step) % ring) for i in range(cols)]
        )
        for step in (1, ring - 1, 2)
    ]
    far = lax.ppermute(near, "row", [(i, i ^ 1) for i in range(rows)])
    q_count, half = cols * tokens, rows * tokens // 2
    lane = 2 * SLOT
    queries, gates = call(
        query_step,
        (shape((PAIRS, q_count, lane), BF16), shape((tokens, wide), F32)),
        14,
        (900_000_000, 5_000_000),
    )(own, *along, norm, token_proj)
    near_k, near_v = call(
        project,
        (shape((PAIRS, half, lane), BF16), shape((PAIRS, half, lane), BF16)),
        14,
        (1_400_000_000, 5_000_000),
    )(near, token_proj)
    parts = call(
        token_step,
        shape((q_count, wide), BF16),
        32,
        (6_000_000_000, 14_000_000),
        in_specs=[pl.BlockSpec(memory_space=pltpu.VMEM)] * 5
        + [pl.BlockSpec(memory_space=pl.ANY)],
        scratch_shapes=[
            pltpu.VMEM((HEADS, q_count, 2 * half), BF16),
            pltpu.VMEM((PAIRS, half, lane), BF16),
            pltpu.VMEM((PAIRS, half, lane), BF16),
            pltpu.SemaphoreType.DMA((HEADS,)),
        ],
    )(queries, near_k, near_v, far, token_proj, pair_bias)
    parts = lax.all_to_all(parts.reshape(cols, tokens, wide), "col", 0, 0)
    return call(
        last_step,
        (shape((count, width), BF16), shape((tokens, depth), BF16)),
        12,
        (400_000_000, 5_000_000),
    )(parts, gates, single, mid, atom_owner, token_output, back_weight)


def solution(mesh):
    split = P(BOTH, None)
    placed = (
        split, split, split, P(None, BOTH, None), P(None, "row", "col"),
        P(), P(), P(), P(), P(), P(),
    )
    return jax.shard_map(
        per_device, mesh=mesh, in_specs=placed, out_specs=(split, split), check_vma=False
    )
```

time: 113 us -> 113 us (level)
  blocking collectives: 19.6 us -> 34.5 us
  Pallas kernels: 40.7 us -> 28 us
  waiting for transfers between devices: 19.8 us -> 11.4 us
  local copies, waits for them, and re-layouts: 5.51 us -> 13.8 us
  starting transfers between devices: 26.2 us -> 24.3 us
    all_to_all x2 -> x0, starting transfers between devices: 19.7 us -> none  [the longest x1 12.2 us: per_device(): lax.all_to_all(jnp.broadcast_to(norm[None], (cols, tokens, depth)), 'col'...]
    all_to_all x2 -> x0, waiting for transfers between devices: 18.5 us -> none  [the longest x1 11.5 us: per_device(): lax.all_to_all(jnp.broadcast_to(norm[None], (cols, tokens, depth)), 'col'...]
    ppermute x0 -> x5, starting transfers between devices: none -> 15.2 us  [the longest x1 11 us: per_device(): lax.ppermute(norm, 'col', [(i, (i + ring) % cols) for i in range(cols)])]
    all_to_all x0 -> x1, blocking collectives: none -> 15.1 us  [per_device(): lax.all_to_all(jnp.broadcast_to(turned[None], (rows // 2, tokens, depth))...]
    unnamed x10 -> x26, local copies, waits for them, and re-layouts: 1.75 us -> 13 us
    pallas_call x2 -> x3, Pallas kernels: 29.5 us -> 21 us  [the longest x1 17.9 us: per_device(): call(token_step, shape((q_count, wide), BF16), 32, (6000000000, 14000000)...]
    ppermute x0 -> x5, waiting for transfers between devices: none -> 6.73 us  [the longest x3 6.72 us: per_device(): lax.ppermute(own, 'col', [(i, i // ring * ring + (i + step) % ring) for i...]
    ppermute x1, waiting for transfers between devices: 0.01 us -> 3.25 us  [per_device(): turned = lax.ppermute(norm, BOTH, turn)]
  transfers between devices with their start and end apart: 5 -> 8, of which waited for: 3 -> 5; matrix products, arithmetic and copies ran while one was open for 0% -> 0% of each run, Pallas kernels for 10% -> 3%
where the time goes in v2:
time: 113 us
  blocking collectives  34.5 us (31%)
  Pallas kernels  28 us (25%)
  starting transfers between devices  24.3 us (22%)
  local copies, waits for them, and re-layouts  13.8 us (12%)
  waiting for transfers between devices  11.4 us (10%)
    all_to_all x1, blocking collectives, per_device(): parts = lax.all_to_all(parts.reshape(cols, tokens, wide), 'col', 0, 0)  19.4 us
    pallas_call x1, Pallas kernels, per_device(): call(token_step, shape((q_count, wide), BF16), 32, (6000000000, 14000000)...  17.9 us
    all_to_all x1, blocking collectives, per_device(): lax.all_to_all(jnp.broadcast_to(turned[None], (rows // 2, tokens, depth))...  15.1 us
    unnamed x26, local copies, waits for them, and re-layouts  13 us
    ppermute x1, starting transfers between devices, per_device(): lax.ppermute(norm, 'col', [(i, (i + ring) % cols) for i in range(cols)])  11 us
    ppermute x3, waiting for transfers between devices, per_device(): lax.ppermute(own, 'col', [(i, i // ring * ring + (i + step) % ring) for i...  6.72 us
    pallas_call x1, Pallas kernels, per_device(): call(atom_step, (shape((count, width), F32), shape((tokens, depth), F32),...  4.75 us
    ppermute x1, starting transfers between devices, per_device(): lax.ppermute(atom_state[count - REACH:], BOTH, [(i, i + 1) for i in range...  4.55 us
  transfers between devices with their start and end apart: 8, of which 5 were waited for; matrix products, arithmetic and copies ran while one was open for 0% of the time, Pallas kernels for 3%

profile of v2, /device:TPU:0, one launch (start us, length us, event | category | flops | bytes accessed | tf_op | source)
XLA Modules:
  0.0 112.6 jit_solution(14465778706781914442)
XLA Ops:
  1.4 1.3 %collective-permute-start.1 = (bf16[48,128]{1,0:T(8,128)(2,1)S(1)}, bf16[48,128]{1,0:T(8,128)(2,1)S(1)}, u32[]{:S(2)}, u32[]{:S(2)}) collective-permute-start(bf16[48,128]{1,0:T(8,128)(2,1)S(1)} %get-tuple-element.20), channel_id=1, source_target_pairs={{1,0},{2,1},{3,2},{4,3},{5,4},{6,5},{7,6},{8,7},{9,8},{10,9},{11,1... | collective-permute-start | bytes 36872 | tf_op jit(solution)/shard_map/ppermute | solution.py:286
  2.6 4.5 %collective-permute-start = (bf16[48,128]{1,0:T(8,128)(2,1)S(1)}, bf16[48,128]{1,0:T(8,128)(2,1)S(1)}, u32[]{:S(2)}, u32[]{:S(2)}) collective-permute-start(bf16[48,128]{1,0:T(8,128)(2,1)S(1)} %get-tuple-element.21), channel_id=1, source_target_pairs={{0,1},{1,2},{2,3},{3,4},{4,5},{5,6},{6,7},{7,8},{8,9},{9,10},{10,1... | collective-permute-start | bytes 36872 | tf_op jit(solution)/shard_map/ppermute | solution.py:283
  7.2 1.4 %collective-permute-done.left_ref = bf16[48,128]{1,0:T(8,128)(2,1)S(1)} collective-permute-done((bf16[48,128]{1,0:T(8,128)(2,1)S(1)}, bf16[48,128]{1,0:T(8,128)(2,1)S(1)}, u32[]{:S(2)}, u32[]{:S(2)}) %collective-permute-start) | collective-permute-done | bytes 12320 | tf_op jit(solution)/shard_map/ppermute | solution.py:283
  10.2 1.0 copy-done.8
  11.2 0.9 copy-done.9
  12.1 0.9 copy-done.10
  14.6 4.7 %shard_map.122 = (f32[384,128]{1,0:T(8,128)S(1)}, f32[48,768]{1,0:T(8,128)S(1)}, bf16[48,768]{1,0:T(8,128)(2,1)S(1)}) custom-call(bf16[48,128]{1,0:T(8,128)(2,1)S(1)} %collective-permute-done.left_ref, bf16[384,128]{1,0:T(8,128)(2,1)S(1)} %copy-done.4, bf16[48,128]{1,0:T(8,128)(2,1)S(1)} %collective-permute-done.1.right_ref, bf16[48,768]{1,0:T(8,128)(2,1)S(1)} %copy-done.11, ...), custom_call_target="tpu_custom_call" | custom-call | flops 400000000 | bytes 2000000 | tf_op jit(solution)/shard_map/pallas_call | solution.py:287
  19.4 11.0 %collective-permute-start.3 = (bf16[48,768]{1,0:T(8,128)(2,1)S(1)}, bf16[48,768]{1,0:T(8,128)(2,1)S(1)}, u32[]{:S(2)}, u32[]{:S(2)}) collective-permute-start(bf16[48,768]{1,0:T(8,128)(2,1)S(1)} %get-tuple-element.11.norm_ref), channel_id=1, source_target_pairs={{0,4},{1,5},{2,6},{3,7},{4,0},{5,1},{6,2},{7,3},{8,12},{9,13},{10,... | collective-permute-start | bytes 221192 | tf_op jit(solution)/shard_map/ppermute | solution.py:307
  30.4 3.2 %collective-permute-start.2 = (bf16[48,768]{1,0:T(8,128)(2,1)S(1)}, bf16[48,768]{1,0:T(8,128)(2,1)S(1)}, u32[]{:S(2)}, u32[]{:S(2)}) collective-permute-start(bf16[48,768]{1,0:T(8,128)(2,1)S(1)} %get-tuple-element.11.norm_ref), channel_id=1, source_target_pairs={{0,32},{1,48},{2,0},{3,16},{4,96},{5,112},{6,64},{7,80},{8,40},{9,... | collective-permute-start | bytes 221192 | tf_op jit(solution)/shard_map/ppermute | solution.py:306
  33.6 3.2 %collective-permute-done.2 = bf16[48,768]{1,0:T(8,128)(2,1)S(1)} collective-permute-done((bf16[48,768]{1,0:T(8,128)(2,1)S(1)}, bf16[48,768]{1,0:T(8,128)(2,1)S(1)}, u32[]{:S(2)}, u32[]{:S(2)}) %collective-permute-start.2) | collective-permute-done | bytes 73760 | tf_op jit(solution)/shard_map/ppermute | solution.py:306
  36.9 15.1 %all_to_all.10.blocks_ref = bf16[8,48,768]{2,1,0:T(8,128)(2,1)S(1)} all-to-all(bf16[8,48,768]{2,1,0:T(8,128)(2,1)S(1)} %broadcast_in_dim.2), channel_id=1, replica_groups={{0,16,32,48,64,80,96,112},{8,24,40,56,72,88,104,120},{1,17,33,49,65,81,..., dimensions={0} | all-to-all | bytes 1179648 | tf_op jit(solution)/shard_map/all_to_all | solution.py:311
  52.0 2.2 %collective-permute-start.6 = (bf16[96,768]{1,0:T(8,128)(2,1)S(1)}, bf16[96,768]{1,0:T(8,128)(2,1)S(1)}, u32[]{:S(2)}, u32[]{:S(2)}) collective-permute-start(bf16[96,768]{1,0:T(8,128)(2,1)S(1)} %pad_maximum_fusion.own_ref), channel_id=1, source_target_pairs={{0,2},{1,3},{2,0},{3,1},{4,6},{5,7},{6,4},{7,5},{8,10},{9,11},{10,... | collective-permute-start | bytes 442376 | tf_op jit(solution)/shard_map/ppermute | solution.py:316
  54.2 1.1 collective-permute-start.5
  55.2 1.0 collective-permute-start.4
  56.2 3.9 %collective-permute-done.6.far_ref = bf16[96,768]{1,0:T(8,128)(2,1)S(1)} collective-permute-done((bf16[96,768]{1,0:T(8,128)(2,1)S(1)}, bf16[96,768]{1,0:T(8,128)(2,1)S(1)}, u32[]{:S(2)}, u32[]{:S(2)}) %collective-permute-start.6) | collective-permute-done | bytes 147488 | tf_op jit(solution)/shard_map/ppermute | solution.py:316
  60.2 1.9 %collective-permute-done.5.before_ref = bf16[96,768]{1,0:T(8,128)(2,1)S(1)} collective-permute-done((bf16[96,768]{1,0:T(8,128)(2,1)S(1)}, bf16[96,768]{1,0:T(8,128)(2,1)S(1)}, u32[]{:S(2)}, u32[]{:S(2)}) %collective-permute-start.5) | collective-permute-done | bytes 147488 | tf_op jit(solution)/shard_map/ppermute | solution.py:316
  62.9 2.3 %copy-done = bf16[4,768,768]{2,1,0:T(8,128)(2,1)S(1)} copy-done((bf16[4,768,768]{2,1,0:T(8,128)(2,1)S(1)}, bf16[4,768,768]{2,1,0:T(8,128)(2,1)}, u32[]{:S(2)}) %copy-start) | copy-done | bytes 4718616
  65.3 1.4 %shard_map.123 = (bf16[8,384,128]{2,1,0:T(8,128)(2,1)S(1)}, f32[48,1024]{1,0:T(8,128)S(1)}) custom-call(bf16[96,768]{1,0:T(8,128)(2,1)S(1)} %pad_maximum_fusion.own_ref, bf16[96,768]{1,0:T(8,128)(2,1)S(1)} %collective-permute-done.4.after_ref, bf16[96,768]{1,0:T(8,128)(2,1)S(1)} %collective-permute-done.5.before_ref, ...), custom_call_target="tpu_custom_call" | custom-call | flops 900000000 | bytes 5000000 | tf_op jit(solution)/shard_map/pallas_call | solution.py:324
  66.7 1.0 copy-done.1
  67.6 1.7 %shard_map.124 = (bf16[8,384,128]{2,1,0:T(8,128)(2,1)S(1)}, bf16[8,384,128]{2,1,0:T(8,128)(2,1)S(1)}) custom-call(bf16[8,48,768]{2,1,0:T(8,128)(2,1)S(1)} %all_to_all.10.blocks_ref, bf16[4,768,768]{2,1,0:T(8,128)(2,1)S(1)} %copy-done.1), custom_call_target="tpu_custom_call" | custom-call | flops 1400000000 | bytes 5000000 | tf_op jit(solution)/shard_map/pallas_call | solution.py:330
  69.3 3.7 %copy-done.7 = bf16[16,384,768]{2,1,0:T(8,128)(2,1)S(1)} copy-done((bf16[16,384,768]{2,1,0:T(8,128)(2,1)S(1)}, bf16[16,384,768]{2,1,0:T(8,128)(2,1)}, u32[]{:S(2)}) %copy-start.7) | copy-done | bytes 9437208
  73.0 17.9 %shard_map.125 = bf16[384,1024]{1,0:T(8,128)(2,1)S(1)} custom-call(bf16[8,384,128]{2,1,0:T(8,128)(2,1)S(1)} %get-tuple-element.13.q_ref, bf16[8,384,128]{2,1,0:T(8,128)(2,1)S(1)} %get-tuple-element.15.k_ref, bf16[8,384,128]{2,1,0:T(8,128)(2,1)S(1)} %get-tuple-element.16.v_ref, bf16[8,48,768]{2,1,0:T(8,128)(2,1)S(1)} %collective-permute-done.7.blocks_ref, ...), custom_call_target="tpu_custom_call" | custom-call | flops 6000000000 | bytes 14000000 | tf_op jit(solution)/shard_map/pallas_call | solution.py:336
  91.0 19.4 %all_to_all.11.part_ref = bf16[8,48,1024]{2,1,0:T(8,128)(2,1)S(1)} all-to-all(bf16[8,48,1024]{2,1,0:T(8,128)(2,1)S(1)} %bitcast.1), channel_id=1, replica_groups=mesh['row'=16,'col'=8] {'col'}, dimensions={0} | all-to-all | bytes 1572864 | tf_op jit(solution)/shard_map/all_to_all | solution.py:350
  110.3 2.3 %shard_map.126 = (bf16[384,128]{1,0:T(8,128)(2,1)}, bf16[48,768]{1,0:T(8,128)(2,1)}) custom-call(bf16[8,48,1024]{2,1,0:T(8,128)(2,1)S(1)} %all_to_all.11.part_ref, f32[48,1024]{1,0:T(8,128)S(1)} %get-tuple-element.17.gate_ref, f32[48,768]{1,0:T(8,128)S(1)} %get-tuple-element.18.single_ref, f32[384,128]{1,0:T(8,128)S(1)} %get-tuple-element.19.mid_ref, ...), custom_call_target="tpu_custom_call" | custom-call | flops 400000000 | bytes 5000000 | tf_op jit(solution)/shard_map/pallas_call | solution.py:351
  (28 shorter events, 4.9 us)
Async XLA Ops:
  1.4 5.8 %collective-permute-start.1 = (bf16[48,128]{1,0:T(8,128)(2,1)S(1)}, bf16[48,128]{1,0:T(8,128)(2,1)S(1)}, u32[]{:S(2)}, u32[]{:S(2)}) collective-permute-start(bf16[48,128]{1,0:T(8,128)(2,1)S(1)} %get-tuple-element.20), channel_id=1, source_target_pairs={{1,0},{2,1},{3,2},{4,3},{5,4},{6,5},{7,6},{8,7},{9,8},{10,9},{11,1... | collective-permute-start | bytes 36872 | tf_op jit(solution)/shard_map/ppermute | solution.py:286
  2.6 5.9 %collective-permute-start = (bf16[48,128]{1,0:T(8,128)(2,1)S(1)}, bf16[48,128]{1,0:T(8,128)(2,1)S(1)}, u32[]{:S(2)}, u32[]{:S(2)}) collective-permute-start(bf16[48,128]{1,0:T(8,128)(2,1)S(1)} %get-tuple-element.21), channel_id=1, source_target_pairs={{0,1},{1,2},{2,3},{3,4},{4,5},{5,6},{6,7},{7,8},{8,9},{9,10},{10,1... | collective-permute-start | bytes 36872 | tf_op jit(solution)/shard_map/ppermute | solution.py:283
  8.6 0.9 copy-start.4
  9.5 0.7 copy-start.5
  10.2 1.0 copy-start.8
  11.2 0.9 copy-start.9
  12.1 0.9 copy-start.10
  13.0 0.9 copy-start.11
  13.9 0.8 copy-start.12
  19.4 14.2 %collective-permute-start.3 = (bf16[48,768]{1,0:T(8,128)(2,1)S(1)}, bf16[48,768]{1,0:T(8,128)(2,1)S(1)}, u32[]{:S(2)}, u32[]{:S(2)}) collective-permute-start(bf16[48,768]{1,0:T(8,128)(2,1)S(1)} %get-tuple-element.11.norm_ref), channel_id=1, source_target_pairs={{0,4},{1,5},{2,6},{3,7},{4,0},{5,1},{6,2},{7,3},{8,12},{9,13},{10,... | collective-permute-start | bytes 221192 | tf_op jit(solution)/shard_map/ppermute | solution.py:307
  30.4 6.5 %collective-permute-start.2 = (bf16[48,768]{1,0:T(8,128)(2,1)S(1)}, bf16[48,768]{1,0:T(8,128)(2,1)S(1)}, u32[]{:S(2)}, u32[]{:S(2)}) collective-permute-start(bf16[48,768]{1,0:T(8,128)(2,1)S(1)} %get-tuple-element.11.norm_ref), channel_id=1, source_target_pairs={{0,32},{1,48},{2,0},{3,16},{4,96},{5,112},{6,64},{7,80},{8,40},{9,... | collective-permute-start | bytes 221192 | tf_op jit(solution)/shard_map/ppermute | solution.py:306
  52.0 17.3 %collective-permute-start.7 = (bf16[8,48,768]{2,1,0:T(8,128)(2,1)S(1)}, bf16[8,48,768]{2,1,0:T(8,128)(2,1)S(1)}, u32[]{:S(2)}, u32[]{:S(2)}) collective-permute-start(bf16[8,48,768]{2,1,0:T(8,128)(2,1)S(1)} %all_to_all.10.blocks_ref), channel_id=1, source_target_pairs={{0,8},{8,0},{16,24},{24,16},{32,40},{40,32},{48,56},{56,48},{64,72... | collective-permute-start | bytes 1769480 | tf_op jit(solution)/shard_map/ppermute | solution.py:321
  52.0 8.1 %collective-permute-start.6 = (bf16[96,768]{1,0:T(8,128)(2,1)S(1)}, bf16[96,768]{1,0:T(8,128)(2,1)S(1)}, u32[]{:S(2)}, u32[]{:S(2)}) collective-permute-start(bf16[96,768]{1,0:T(8,128)(2,1)S(1)} %pad_maximum_fusion.own_ref), channel_id=1, source_target_pairs={{0,2},{1,3},{2,0},{3,1},{4,6},{5,7},{6,4},{7,5},{8,10},{9,11},{10,... | collective-permute-start | bytes 442376 | tf_op jit(solution)/shard_map/ppermute | solution.py:316
  54.2 7.9 %collective-permute-start.5 = (bf16[96,768]{1,0:T(8,128)(2,1)S(1)}, bf16[96,768]{1,0:T(8,128)(2,1)S(1)}, u32[]{:S(2)}, u32[]{:S(2)}) collective-permute-start(bf16[96,768]{1,0:T(8,128)(2,1)S(1)} %pad_maximum_fusion.own_ref), channel_id=1, source_target_pairs={{0,3},{1,0},{2,1},{3,2},{4,7},{5,4},{6,5},{7,6},{8,11},{9,8},{10,9... | collective-permute-start | bytes 442376 | tf_op jit(solution)/shard_map/ppermute | solution.py:316
  55.2 7.7 %collective-permute-start.4 = (bf16[96,768]{1,0:T(8,128)(2,1)S(1)}, bf16[96,768]{1,0:T(8,128)(2,1)S(1)}, u32[]{:S(2)}, u32[]{:S(2)}) collective-permute-start(bf16[96,768]{1,0:T(8,128)(2,1)S(1)} %pad_maximum_fusion.own_ref), channel_id=1, source_target_pairs={{0,1},{1,2},{2,3},{3,0},{4,5},{5,6},{6,7},{7,4},{8,9},{9,10},{10,1... | collective-permute-start | bytes 442376 | tf_op jit(solution)/shard_map/ppermute | solution.py:316
  62.9 2.3 %copy-start = (bf16[4,768,768]{2,1,0:T(8,128)(2,1)S(1)}, bf16[4,768,768]{2,1,0:T(8,128)(2,1)}, u32[]{:S(2)}) copy-start(bf16[4,768,768]{2,1,0:T(8,128)(2,1)} %proj_ref.7) | copy-start | bytes 14155780
  65.3 2.3 %copy-start.1 = (bf16[4,768,768]{2,1,0:T(8,128)(2,1)S(1)}, bf16[4,768,768]{2,1,0:T(8,128)(2,1)}, u32[]{:S(2)}) copy-start(bf16[4,768,768]{2,1,0:T(8,128)(2,1)} %proj_ref.7) | copy-start | bytes 14155780
  69.3 3.7 %copy-start.7 = (bf16[16,384,768]{2,1,0:T(8,128)(2,1)S(1)}, bf16[16,384,768]{2,1,0:T(8,128)(2,1)}, u32[]{:S(2)}) copy-start(bf16[16,384,768]{2,1,0:T(8,128)(2,1)} %bias_hbm.1) | copy-start | bytes 28311556
  73.0 37.3 %copy-start.2 = (bf16[768,768]{1,0:T(8,128)(2,1)S(1)}, bf16[768,768]{1,0:T(8,128)(2,1)}, u32[]{:S(2)}) copy-start(bf16[768,768]{1,0:T(8,128)(2,1)} %output_ref.3) | copy-start | bytes 3538948
  73.0 37.3 %copy-start.3 = (bf16[768,128]{1,0:T(8,128)(2,1)S(1)}, bf16[768,128]{1,0:T(8,128)(2,1)}, u32[]{:S(2)}) copy-start(bf16[768,128]{1,0:T(8,128)(2,1)} %back_ref.1) | copy-start | bytes 589828
  73.0 37.3 %copy-start.6 = (s32[1,384]{1,0:T(1,128)S(1)}, s32[1,384]{1,0:T(1,128)}, u32[]{:S(2)}) copy-start(s32[1,384]{1,0:T(1,128)} %owner_ref.3) | copy-start | bytes 4612

commit v3 on v2

--- a/solution.py
+++ b/solution.py
@@ -20,6 +20,8 @@
 BOTH = ("row", "col")
 F32 = jnp.float32
 BF16 = jnp.bfloat16
+ATOM_MB = 20
+SMALL = (1_000_000, 100_000)
 ORDER = (2, 3, 0, 1, 6, 7, 4, 5)
 
 
@@ -77,10 +79,16 @@
 
 
 def atom_step(
-    left_ref, state_ref, right_ref, input_ref, owner_ref, bias_ref, proj_ref, output_ref,
-    pool_ref, mid_ref, single_ref, norm_ref,
+    left_ref, right_ref, narrow_ref, broad_ref, owner_ref, mid_ref, single_ref, norm_ref,
 ):
-    count = state_ref.shape[0]
+    width = narrow_ref.shape[1]
+    count = owner_ref.shape[1]
+    state_ref = narrow_ref.at[:count]
+    after = (1 + ATOM_HEADS) * count
+    bias_ref = [narrow_ref.at[(1 + h) * count : (2 + h) * count] for h in range(ATOM_HEADS)]
+    proj_ref = [narrow_ref.at[after + i * width : after + (i + 1) * width] for i in range(5)]
+    output_ref = proj_ref[4]
+    pool_ref, input_ref = broad_ref.at[:width], broad_ref.at[width:]
     windows = count // WIN_Q
     rows, cols = lax.axis_size("row"), lax.axis_size("col")
     first = (lax.axis_index("row") * cols + lax.axis_index("col")) * count
@@ -90,12 +98,11 @@
         [left_ref[...].astype(F32), state, right_ref[...].astype(F32)], axis=0
     )
     normed = layer_norm(extended).astype(BF16)
-    keys = dot(normed, proj_ref[1]).astype(BF16)
-    values = dot(normed, proj_ref[2]).astype(BF16)
+    keys = dot(normed, proj_ref[1][...]).astype(BF16)
+    values = dot(normed, proj_ref[2][...]).astype(BF16)
     own = normed[REACH : REACH + count]
-    queries = dot(own, proj_ref[0]).astype(BF16)
-    gates = jax.nn.sigmoid(dot(own, proj_ref[3]))
-    width = state_ref.shape[1]
+    queries = dot(own, proj_ref[0][...]).astype(BF16)
+    gates = jax.nn.sigmoid(dot(own, proj_ref[3][...]))
     head_width = width // ATOM_HEADS
     head_of = lanes((WIN_Q, width), 1) // head_width
     factor = 1.0 / math.sqrt(head_width)
@@ -109,7 +116,7 @@
         )
         scores = dot(stacked, keys[start : start + WIN_K], ((1,), (1,))) * factor
         scores = scores + jnp.concatenate(
-            [bias_ref[h, start : start + WIN_Q, :] for h in range(ATOM_HEADS)], axis=0
+            [bias_ref[h][start : start + WIN_Q, :] for h in range(ATOM_HEADS)], axis=0
         ).astype(F32)
         if start < REACH or start + WIN_K > count + REACH:
             position = first + (start - REACH) + lanes(scores.shape, 1)
@@ -169,16 +176,8 @@
     store_pairs(v_ref, [jnp.where(mass, 1.0, band) for band in bands])
 
 
-def token_step(
-    q_ref, k_ref, v_ref, blocks_ref, proj_ref, bias_hbm, part_ref, bias_ref, other_k, other_v,
-    sems,
-):
-    lane = 2 * SLOT
-    copies = [
-        pltpu.make_async_copy(bias_hbm.at[h], bias_ref.at[h], sems.at[h]) for h in range(HEADS)
-    ]
-    for copy in copies:
-        copy.start()
+def token_step(q_ref, k_ref, v_ref, blocks_ref, proj_ref, bias_ref, part_ref, other_k, other_v):
+    lane = 2 * SLOT
     project(blocks_ref, proj_ref, other_k, other_v)
     core = lax.rem(lax.axis_index("row"), 2)
     count, half = q_ref.shape[1], k_ref.shape[1]
@@ -188,20 +187,18 @@
     factor = 1.0 / math.sqrt(HEAD_DIM)
     for pair in range(PAIRS):
         query = q_ref[pair]
+        key = jnp.concatenate([k_ref[pair], other_k[pair]], axis=0)
+        value = jnp.concatenate([v_ref[pair], other_v[pair]], axis=0)
         result = jnp.zeros((count, lane), F32)
         for a in range(2):
             head = 2 * pair + a
-            copies[head].wait()
             mine = jnp.where(at // SLOT == a, query, jnp.zeros_like(query))
-            near = dot(mine, k_ref[pair], ((1,), (1,))) * factor
-            near = near + bias_ref[head, :, mine_at].astype(F32)
-            far = dot(mine, other_k[pair], ((1,), (1,))) * factor
-            far = far + bias_ref[head, :, other_at].astype(F32)
-            top = jnp.maximum(
-                jnp.max(near, axis=-1, keepdims=True), jnp.max(far, axis=-1, keepdims=True)
+            bias = jnp.concatenate(
+                [bias_ref[head, :, mine_at], bias_ref[head, :, other_at]], axis=1
             )
-            mixed = dot(jnp.exp(near - top).astype(BF16), v_ref[pair])
-            mixed = mixed + dot(jnp.exp(far - top).astype(BF16), other_v[pair])
+            scores = dot(mine, key, ((1,), (1,))) * factor + bias.astype(F32)
+            top = jnp.max(scores, axis=-1, keepdims=True)
+            mixed = dot(jnp.exp(scores - top).astype(BF16), value)
             base = a * SLOT + HEAD_DIM
             mass = mixed[:, base : base + 1]
             level = top + jnp.log(mass)
@@ -284,6 +281,12 @@
         atom_state[count - REACH :], BOTH, [(i, i + 1) for i in range(ends)]
     )
     right = lax.ppermute(atom_state[:REACH], BOTH, [(i + 1, i) for i in range(ends)])
+    narrow = jnp.concatenate(
+        [atom_state]
+        + [array.reshape(-1, width) for array in (atom_bias, atom_proj, atom_output)],
+        axis=0,
+    )
+    broad = jnp.concatenate([pool_weight, token_input], axis=0)
     mid, single, norm = call(
         atom_step,
         (
@@ -291,12 +294,9 @@
             shape((tokens, depth), F32),
             shape((tokens, depth), BF16),
         ),
-        12,
+        ATOM_MB,
         (400_000_000, 2_000_000),
-    )(
-        left, atom_state, right, token_input, atom_owner, atom_bias, atom_proj, atom_output,
-        pool_weight,
-    )
+    )(left, right, narrow, broad, atom_owner)
     ring = cols // 2
     turn = []
     for r in range(rows):
@@ -318,6 +318,7 @@
         )
         for step in (1, ring - 1, 2)
     ]
+    near, *along = lax.optimization_barrier((near, *along))
     far = lax.ppermute(near, "row", [(i, i ^ 1) for i in range(rows)])
     q_count, half = cols * tokens, rows * tokens // 2
     lane = 2 * SLOT
@@ -325,26 +326,22 @@
         query_step,
         (shape((PAIRS, q_count, lane), BF16), shape((tokens, wide), F32)),
         14,
-        (900_000_000, 5_000_000),
+        SMALL,
     )(own, *along, norm, token_proj)
     near_k, near_v = call(
         project,
         (shape((PAIRS, half, lane), BF16), shape((PAIRS, half, lane), BF16)),
         14,
-        (1_400_000_000, 5_000_000),
+        SMALL,
     )(near, token_proj)
     parts = call(
         token_step,
         shape((q_count, wide), BF16),
         32,
         (6_000_000_000, 14_000_000),
-        in_specs=[pl.BlockSpec(memory_space=pltpu.VMEM)] * 5
-        + [pl.BlockSpec(memory_space=pl.ANY)],
         scratch_shapes=[
-            pltpu.VMEM((HEADS, q_count, 2 * half), BF16),
             pltpu.VMEM((PAIRS, half, lane), BF16),
             pltpu.VMEM((PAIRS, half, lane), BF16),
-            pltpu.SemaphoreType.DMA((HEADS,)),
         ],
     )(queries, near_k, near_v, far, token_proj, pair_bias)
     parts = lax.all_to_all(parts.reshape(cols, tokens, wide), "col", 0, 0)

time: 113 us -> 88.3 us (0.78)
  blocking collectives: 34.5 us -> 19.1 us
  Pallas kernels: 28 us -> 19.8 us
  starting transfers between devices: 24.3 us -> 29.9 us
  local copies, waits for them, and re-layouts: 13.8 us -> 8.29 us
  waiting for transfers between devices: 11.4 us -> 8.92 us
  other arithmetic: 0.01 us -> 1.17 us
    all_to_all x1 -> x0, blocking collectives: 15.1 us -> none  [per_device(): lax.all_to_all(jnp.broadcast_to(turned[None], (rows // 2, tokens, depth))...]
    pallas_call x1, Pallas kernels: 17.9 us -> 9.67 us  [per_device(): call(token_step, shape((q_count, wide), BF16), 32, (6000000000, 14000000)...]
    unnamed x26 -> x16, local copies, waits for them, and re-layouts: 13 us -> 6.66 us
    all_to_all x0 -> x1, starting transfers between devices: none -> 6.12 us  [per_device(): lax.all_to_all(jnp.broadcast_to(turned[None], (rows // 2, tokens, depth))...]
    ppermute x3, waiting for transfers between devices: 6.72 us -> 5.48 us  [per_device(): lax.ppermute(own, 'col', [(i, i // ring * ring + (i + step) % ring) for i...]
    ppermute x1, waiting for transfers between devices: 1.38 us -> 0.18 us  [per_device(): lax.ppermute(atom_state[count - REACH:], BOTH, [(i, i + 1) for i in range...]
    concatenate x0 -> x2, other arithmetic: none -> 1.16 us  [the longest x1 1.14 us: per_device(): jnp.concatenate([atom_state] + [array.reshape(-1, width) for array in (at...]
  transfers between devices with their start and end apart: 8 -> 9, of which waited for: 5 -> 5; matrix products, arithmetic and copies ran while one was open for 0% -> 1% of each run, Pallas kernels for 3% -> 3%
where the time goes in v3:
time: 88.3 us; the launch traced here: 87.9 us
  starting transfers between devices  29.9 us (34%)
  Pallas kernels  19.8 us (22%)
  blocking collectives  19.1 us (22%)
  waiting for transfers between devices  8.92 us (10%)
  local copies, waits for them, and re-layouts  8.29 us (9%)
  other arithmetic  1.17 us (1%)
    all_to_all x1, blocking collectives, per_device(): parts = lax.all_to_all(parts.reshape(cols, tokens, wide), 'col', 0, 0)  19.1 us
    ppermute x1, starting transfers between devices, per_device(): lax.ppermute(norm, 'col', [(i, (i + ring) % cols) for i in range(cols)])  11 us
    pallas_call x1, Pallas kernels, per_device(): call(token_step, shape((q_count, wide), BF16), 32, (6000000000, 14000000)...  9.67 us
    unnamed x16, local copies, waits for them, and re-layouts  6.66 us
    all_to_all x1, starting transfers between devices, per_device(): lax.all_to_all(jnp.broadcast_to(turned[None], (rows // 2, tokens, depth))...  6.12 us
    ppermute x3, waiting for transfers between devices, per_device(): lax.ppermute(own, 'col', [(i, i // ring * ring + (i + step) % ring) for i...  5.48 us
    pallas_call x1, Pallas kernels, per_device(): call(atom_step, (shape((count, width), F32), shape((tokens, depth), F32),...  4.74 us
    ppermute x1, starting transfers between devices, per_device(): lax.ppermute(atom_state[count - REACH:], BOTH, [(i, i + 1) for i in range...  4.55 us
  transfers between devices with their start and end apart: 9, of which 5 were waited for; matrix products, arithmetic and copies ran while one was open for 1% of the time, Pallas kernels for 3%

profile of v3, /device:TPU:0, one launch (start us, length us, event | category | flops | bytes accessed | tf_op | source)
XLA Modules:
  0.0 87.9 jit_solution(17121427509619452149)
XLA Ops:
  0.7 0.8 fusion
  1.4 1.3 %collective-permute-start.1 = (bf16[48,128]{1,0:T(8,128)(2,1)S(1)}, bf16[48,128]{1,0:T(8,128)(2,1)S(1)}, u32[]{:S(2)}, u32[]{:S(2)}) collective-permute-start(bf16[48,128]{1,0:T(8,128)(2,1)S(1)} %get-tuple-element.28), channel_id=1, source_target_pairs={{1,0},{2,1},{3,2},{4,3},{5,4},{6,5},{7,6},{8,7},{9,8},{10,9},{11,1... | collective-permute-start | bytes 36872 | tf_op jit(solution)/shard_map/ppermute | solution.py:283
  2.7 4.5 %collective-permute-start = (bf16[48,128]{1,0:T(8,128)(2,1)S(1)}, bf16[48,128]{1,0:T(8,128)(2,1)S(1)}, u32[]{:S(2)}, u32[]{:S(2)}) collective-permute-start(bf16[48,128]{1,0:T(8,128)(2,1)S(1)} %get-tuple-element.29), channel_id=1, source_target_pairs={{0,1},{1,2},{2,3},{3,4},{4,5},{5,6},{6,7},{7,8},{8,9},{9,10},{10,1... | collective-permute-start | bytes 36872 | tf_op jit(solution)/shard_map/ppermute | solution.py:280
  7.3 1.1 %pad_maximum_fusion.narrow_ref = bf16[2560,128]{1,0:T(8,128)(2,1)S(1)} fusion(bf16[128,128]{1,0:T(8,128)(2,1)} %param.17, bf16[512,128]{1,0:T(8,128)(2,1)} %bitcast.5, bf16[1536,128]{1,0:T(8,128)(2,1)} %bitcast.4, bf16[384,128]{1,0:T(8,128)(2,1)} %param.11), kind=kLoop, calls=%fused_computation | loop fusion | flops 2621440 | bytes 1310720 | tf_op jit(solution)/shard_map/concatenate | solution.py:284
  8.7 4.7 %shard_map.122 = (f32[384,128]{1,0:T(8,128)S(1)}, f32[48,768]{1,0:T(8,128)S(1)}, bf16[48,768]{1,0:T(8,128)(2,1)S(1)}) custom-call(bf16[48,128]{1,0:T(8,128)(2,1)S(1)} %collective-permute-done.left_ref, bf16[48,128]{1,0:T(8,128)(2,1)S(1)} %collective-permute-done.1.right_ref, bf16[2560,128]{1,0:T(8,128)(2,1)S(1)} %pad_maximum_fusion.narrow_ref, ...), custom_call_target="tpu_custom_call" | custom-call | flops 400000000 | bytes 2000000 | tf_op jit(solution)/shard_map/pallas_call | solution.py:290
  13.4 11.0 %collective-permute-start.3 = (bf16[48,768]{1,0:T(8,128)(2,1)S(1)}, bf16[48,768]{1,0:T(8,128)(2,1)S(1)}, u32[]{:S(2)}, u32[]{:S(2)}) collective-permute-start(bf16[48,768]{1,0:T(8,128)(2,1)S(1)} %get-tuple-element.15.norm_ref), channel_id=1, source_target_pairs={{0,4},{1,5},{2,6},{3,7},{4,0},{5,1},{6,2},{7,3},{8,12},{9,13},{10,... | collective-permute-start | bytes 221192 | tf_op jit(solution)/shard_map/ppermute | solution.py:307
  24.5 3.2 %collective-permute-start.2 = (bf16[48,768]{1,0:T(8,128)(2,1)S(1)}, bf16[48,768]{1,0:T(8,128)(2,1)S(1)}, u32[]{:S(2)}, u32[]{:S(2)}) collective-permute-start(bf16[48,768]{1,0:T(8,128)(2,1)S(1)} %get-tuple-element.15.norm_ref), channel_id=1, source_target_pairs={{0,32},{1,48},{2,0},{3,16},{4,96},{5,112},{6,64},{7,80},{8,40},{9,... | collective-permute-start | bytes 221192 | tf_op jit(solution)/shard_map/ppermute | solution.py:306
  27.7 3.2 %collective-permute-done.2 = bf16[48,768]{1,0:T(8,128)(2,1)S(1)} collective-permute-done((bf16[48,768]{1,0:T(8,128)(2,1)S(1)}, bf16[48,768]{1,0:T(8,128)(2,1)S(1)}, u32[]{:S(2)}, u32[]{:S(2)}) %collective-permute-start.2) | collective-permute-done | bytes 73760 | tf_op jit(solution)/shard_map/ppermute | solution.py:306
  30.9 0.9 broadcast_in_dim.2
  31.8 6.1 %all-to-all-start = ((bf16[8,48,768]{2,1,0:T(8,128)(2,1)}), bf16[8,48,768]{2,1,0:T(8,128)(2,1)S(1)}, u32[]{:S(2)}, u32[]{:S(2)}) async-start(bf16[8,48,768]{2,1,0:T(8,128)(2,1)} %broadcast_in_dim.2), calls=%async_computation | async-start | bytes 1179648 | tf_op jit(solution)/shard_map/all_to_all | solution.py:311
  37.9 1.6 %collective-permute-start.6 = (bf16[96,768]{1,0:T(8,128)(2,1)S(1)}, bf16[96,768]{1,0:T(8,128)(2,1)S(1)}, u32[]{:S(2)}, u32[]{:S(2)}) collective-permute-start(bf16[96,768]{1,0:T(8,128)(2,1)S(1)} %pad_maximum_fusion.2.own_ref), channel_id=1, source_target_pairs={{0,2},{1,3},{2,0},{3,1},{4,6},{5,7},{6,4},{7,5},{8,10},{9,11},{10,... | collective-permute-start | bytes 442376 | tf_op jit(solution)/shard_map/ppermute | solution.py:316
  39.6 1.2 %collective-permute-start.5 = (bf16[96,768]{1,0:T(8,128)(2,1)S(1)}, bf16[96,768]{1,0:T(8,128)(2,1)S(1)}, u32[]{:S(2)}, u32[]{:S(2)}) collective-permute-start(bf16[96,768]{1,0:T(8,128)(2,1)S(1)} %pad_maximum_fusion.2.own_ref), channel_id=1, source_target_pairs={{0,3},{1,0},{2,1},{3,2},{4,7},{5,4},{6,5},{7,6},{8,11},{9,8},{10,9... | collective-permute-start | bytes 442376 | tf_op jit(solution)/shard_map/ppermute | solution.py:316
  40.7 0.9 collective-permute-start.4
  41.6 3.1 %collective-permute-done.6.far_ref = bf16[96,768]{1,0:T(8,128)(2,1)S(1)} collective-permute-done((bf16[96,768]{1,0:T(8,128)(2,1)S(1)}, bf16[96,768]{1,0:T(8,128)(2,1)S(1)}, u32[]{:S(2)}, u32[]{:S(2)}) %collective-permute-start.6) | collective-permute-done | bytes 147488 | tf_op jit(solution)/shard_map/ppermute | solution.py:316
  44.7 0.6 collective-permute-done.5.before_ref
  45.2 1.8 %collective-permute-done.4.after_ref = bf16[96,768]{1,0:T(8,128)(2,1)S(1)} collective-permute-done((bf16[96,768]{1,0:T(8,128)(2,1)S(1)}, bf16[96,768]{1,0:T(8,128)(2,1)S(1)}, u32[]{:S(2)}, u32[]{:S(2)}) %collective-permute-start.4) | collective-permute-done | bytes 147488 | tf_op jit(solution)/shard_map/ppermute | solution.py:316
  47.1 2.3 %copy-done = bf16[4,768,768]{2,1,0:T(8,128)(2,1)S(1)} copy-done((bf16[4,768,768]{2,1,0:T(8,128)(2,1)S(1)}, bf16[4,768,768]{2,1,0:T(8,128)(2,1)}, u32[]{:S(2)}) %copy-start) | copy-done | bytes 4718616
  49.4 1.7 %shard_map.124 = (bf16[8,384,128]{2,1,0:T(8,128)(2,1)S(1)}, bf16[8,384,128]{2,1,0:T(8,128)(2,1)S(1)}) custom-call(bf16[8,48,768]{2,1,0:T(8,128)(2,1)S(1)} %all-to-all-done.blocks_ref, bf16[4,768,768]{2,1,0:T(8,128)(2,1)S(1)} %copy-done), custom_call_target="tpu_custom_call" | custom-call | flops 1000000 | bytes 100000 | tf_op jit(solution)/shard_map/pallas_call | solution.py:331
  51.1 0.6 copy-done.1
  51.7 1.4 %shard_map.123 = (bf16[8,384,128]{2,1,0:T(8,128)(2,1)S(1)}, f32[48,1024]{1,0:T(8,128)S(1)}) custom-call(bf16[96,768]{1,0:T(8,128)(2,1)S(1)} %pad_maximum_fusion.2.own_ref, bf16[96,768]{1,0:T(8,128)(2,1)S(1)} %collective-permute-done.4.after_ref, bf16[96,768]{1,0:T(8,128)(2,1)S(1)} %collective-permute-done.5.before_ref, ...), custom_call_target="tpu_custom_call" | custom-call | flops 1000000 | bytes 100000 | tf_op jit(solution)/shard_map/pallas_call | solution.py:325
  53.1 3.7 %copy-done.5 = bf16[16,384,768]{2,1,0:T(8,128)(2,1)S(1)} copy-done((bf16[16,384,768]{2,1,0:T(8,128)(2,1)S(1)}, bf16[16,384,768]{2,1,0:T(8,128)(2,1)}, u32[]{:S(2)}) %copy-start.5) | copy-done | bytes 9437208
  56.8 9.7 %shard_map.125 = bf16[384,1024]{1,0:T(8,128)(2,1)S(1)} custom-call(bf16[8,384,128]{2,1,0:T(8,128)(2,1)S(1)} %get-tuple-element.21.q_ref, bf16[8,384,128]{2,1,0:T(8,128)(2,1)S(1)} %get-tuple-element.23.k_ref, bf16[8,384,128]{2,1,0:T(8,128)(2,1)S(1)} %get-tuple-element.24.v_ref, bf16[8,48,768]{2,1,0:T(8,128)(2,1)S(1)} %collective-permute-done.7.blocks_ref, ...), custom_call_target="tpu_custom_call" | custom-call | flops 6000000000 | bytes 14000000 | tf_op jit(solution)/shard_map/pallas_call | solution.py:337
  66.5 19.1 %all_to_all.10.part_ref = bf16[8,48,1024]{2,1,0:T(8,128)(2,1)S(1)} all-to-all(bf16[8,48,1024]{2,1,0:T(8,128)(2,1)S(1)} %bitcast.3), channel_id=1, replica_groups=mesh['row'=16,'col'=8] {'col'}, dimensions={0} | all-to-all | bytes 1572864 | tf_op jit(solution)/shard_map/all_to_all | solution.py:347
  85.6 2.3 %shard_map.126 = (bf16[384,128]{1,0:T(8,128)(2,1)}, bf16[48,768]{1,0:T(8,128)(2,1)}) custom-call(bf16[8,48,1024]{2,1,0:T(8,128)(2,1)S(1)} %all_to_all.10.part_ref, f32[48,1024]{1,0:T(8,128)S(1)} %get-tuple-element.25.gate_ref, f32[48,768]{1,0:T(8,128)S(1)} %get-tuple-element.26.single_ref, f32[384,128]{1,0:T(8,128)S(1)} %get-tuple-element.27.mid_ref, ...), custom_call_target="tpu_custom_call" | custom-call | flops 400000000 | bytes 5000000 | tf_op jit(solution)/shard_map/pallas_call | solution.py:348
  (21 shorter events, 0.3 us)
Async XLA Ops:
  0.6 7.8 %copy-start.6 = (bf16[128,768]{1,0:T(8,128)(2,1)S(1)}, bf16[128,768]{1,0:T(8,128)(2,1)}, u32[]{:S(2)}) copy-start(bf16[128,768]{1,0:T(8,128)(2,1)} %param.18) | copy-start | bytes 589828
  0.6 7.8 %copy-start.7 = (bf16[48,768]{1,0:T(8,128)(2,1)S(1)}, bf16[48,768]{1,0:T(8,128)(2,1)}, u32[]{:S(2)}) copy-start(bf16[48,768]{1,0:T(8,128)(2,1)} %param.12) | copy-start | bytes 221188
  0.7 8.0 %copy-start.4 = (s32[1,384]{1,0:T(1,128)S(1)}, s32[1,384]{1,0:T(1,128)}, u32[]{:S(2)}) copy-start(s32[1,384]{1,0:T(1,128)} %owner_ref.3) | copy-start | bytes 4612
  1.4 7.0 %collective-permute-start.1 = (bf16[48,128]{1,0:T(8,128)(2,1)S(1)}, bf16[48,128]{1,0:T(8,128)(2,1)S(1)}, u32[]{:S(2)}, u32[]{:S(2)}) collective-permute-start(bf16[48,128]{1,0:T(8,128)(2,1)S(1)} %get-tuple-element.28), channel_id=1, source_target_pairs={{1,0},{2,1},{3,2},{4,3},{5,4},{6,5},{7,6},{8,7},{9,8},{10,9},{11,1... | collective-permute-start | bytes 36872 | tf_op jit(solution)/shard_map/ppermute | solution.py:283
  2.7 5.9 %collective-permute-start = (bf16[48,128]{1,0:T(8,128)(2,1)S(1)}, bf16[48,128]{1,0:T(8,128)(2,1)S(1)}, u32[]{:S(2)}, u32[]{:S(2)}) collective-permute-start(bf16[48,128]{1,0:T(8,128)(2,1)S(1)} %get-tuple-element.29), channel_id=1, source_target_pairs={{0,1},{1,2},{2,3},{3,4},{4,5},{5,6},{6,7},{7,8},{8,9},{9,10},{10,1... | collective-permute-start | bytes 36872 | tf_op jit(solution)/shard_map/ppermute | solution.py:280
  13.4 14.2 %collective-permute-start.3 = (bf16[48,768]{1,0:T(8,128)(2,1)S(1)}, bf16[48,768]{1,0:T(8,128)(2,1)S(1)}, u32[]{:S(2)}, u32[]{:S(2)}) collective-permute-start(bf16[48,768]{1,0:T(8,128)(2,1)S(1)} %get-tuple-element.15.norm_ref), channel_id=1, source_target_pairs={{0,4},{1,5},{2,6},{3,7},{4,0},{5,1},{6,2},{7,3},{8,12},{9,13},{10,... | collective-permute-start | bytes 221192 | tf_op jit(solution)/shard_map/ppermute | solution.py:307
  24.5 6.5 %collective-permute-start.2 = (bf16[48,768]{1,0:T(8,128)(2,1)S(1)}, bf16[48,768]{1,0:T(8,128)(2,1)S(1)}, u32[]{:S(2)}, u32[]{:S(2)}) collective-permute-start(bf16[48,768]{1,0:T(8,128)(2,1)S(1)} %get-tuple-element.15.norm_ref), channel_id=1, source_target_pairs={{0,32},{1,48},{2,0},{3,16},{4,96},{5,112},{6,64},{7,80},{8,40},{9,... | collective-permute-start | bytes 221192 | tf_op jit(solution)/shard_map/ppermute | solution.py:306
  31.8 15.3 %all-to-all-start = ((bf16[8,48,768]{2,1,0:T(8,128)(2,1)}), bf16[8,48,768]{2,1,0:T(8,128)(2,1)S(1)}, u32[]{:S(2)}, u32[]{:S(2)}) async-start(bf16[8,48,768]{2,1,0:T(8,128)(2,1)} %broadcast_in_dim.2), calls=%async_computation | async-start | bytes 1179648 | tf_op jit(solution)/shard_map/all_to_all | solution.py:311
  37.9 6.8 %collective-permute-start.6 = (bf16[96,768]{1,0:T(8,128)(2,1)S(1)}, bf16[96,768]{1,0:T(8,128)(2,1)S(1)}, u32[]{:S(2)}, u32[]{:S(2)}) collective-permute-start(bf16[96,768]{1,0:T(8,128)(2,1)S(1)} %pad_maximum_fusion.2.own_ref), channel_id=1, source_target_pairs={{0,2},{1,3},{2,0},{3,1},{4,6},{5,7},{6,4},{7,5},{8,10},{9,11},{10,... | collective-permute-start | bytes 442376 | tf_op jit(solution)/shard_map/ppermute | solution.py:316
  39.6 5.7 %collective-permute-start.5 = (bf16[96,768]{1,0:T(8,128)(2,1)S(1)}, bf16[96,768]{1,0:T(8,128)(2,1)S(1)}, u32[]{:S(2)}, u32[]{:S(2)}) collective-permute-start(bf16[96,768]{1,0:T(8,128)(2,1)S(1)} %pad_maximum_fusion.2.own_ref), channel_id=1, source_target_pairs={{0,3},{1,0},{2,1},{3,2},{4,7},{5,4},{6,5},{7,6},{8,11},{9,8},{10,9... | collective-permute-start | bytes 442376 | tf_op jit(solution)/shard_map/ppermute | solution.py:316
  40.7 6.4 %collective-permute-start.4 = (bf16[96,768]{1,0:T(8,128)(2,1)S(1)}, bf16[96,768]{1,0:T(8,128)(2,1)S(1)}, u32[]{:S(2)}, u32[]{:S(2)}) collective-permute-start(bf16[96,768]{1,0:T(8,128)(2,1)S(1)} %pad_maximum_fusion.2.own_ref), channel_id=1, source_target_pairs={{0,1},{1,2},{2,3},{3,0},{4,5},{5,6},{6,7},{7,4},{8,9},{9,10},{10,1... | collective-permute-start | bytes 442376 | tf_op jit(solution)/shard_map/ppermute | solution.py:316
  47.1 6.0 %collective-permute-start.7 = (bf16[8,48,768]{2,1,0:T(8,128)(2,1)S(1)}, bf16[8,48,768]{2,1,0:T(8,128)(2,1)S(1)}, u32[]{:S(2)}, u32[]{:S(2)}) collective-permute-start(bf16[8,48,768]{2,1,0:T(8,128)(2,1)S(1)} %all-to-all-done.blocks_ref), channel_id=1, source_target_pairs={{0,8},{8,0},{16,24},{24,16},{32,40},{40,32},{48,56},{56,48},{64,72... | collective-permute-start | bytes 1769480 | tf_op jit(solution)/shard_map/ppermute | solution.py:322
  47.1 2.3 %copy-start = (bf16[4,768,768]{2,1,0:T(8,128)(2,1)S(1)}, bf16[4,768,768]{2,1,0:T(8,128)(2,1)}, u32[]{:S(2)}) copy-start(bf16[4,768,768]{2,1,0:T(8,128)(2,1)} %proj_ref.5) | copy-start | bytes 14155780
  49.4 2.3 %copy-start.1 = (bf16[4,768,768]{2,1,0:T(8,128)(2,1)S(1)}, bf16[4,768,768]{2,1,0:T(8,128)(2,1)}, u32[]{:S(2)}) copy-start(bf16[4,768,768]{2,1,0:T(8,128)(2,1)} %proj_ref.5) | copy-start | bytes 14155780
  53.1 3.7 %copy-start.5 = (bf16[16,384,768]{2,1,0:T(8,128)(2,1)S(1)}, bf16[16,384,768]{2,1,0:T(8,128)(2,1)}, u32[]{:S(2)}) copy-start(bf16[16,384,768]{2,1,0:T(8,128)(2,1)} %bias_ref.1) | copy-start | bytes 28311556
  66.5 19.1 %copy-start.2 = (bf16[768,768]{1,0:T(8,128)(2,1)S(1)}, bf16[768,768]{1,0:T(8,128)(2,1)}, u32[]{:S(2)}) copy-start(bf16[768,768]{1,0:T(8,128)(2,1)} %output_ref.1) | copy-start | bytes 3538948
  66.5 19.1 %copy-start.3 = (bf16[768,128]{1,0:T(8,128)(2,1)S(1)}, bf16[768,128]{1,0:T(8,128)(2,1)}, u32[]{:S(2)}) copy-start(bf16[768,128]{1,0:T(8,128)(2,1)} %back_ref.1) | copy-start | bytes 589828

commit v4 on v3

--- a/solution.py
+++ b/solution.py
@@ -21,6 +21,7 @@
 F32 = jnp.float32
 BF16 = jnp.bfloat16
 ATOM_MB = 20
+MOST = 47
 SMALL = (1_000_000, 100_000)
 ORDER = (2, 3, 0, 1, 6, 7, 4, 5)
 
@@ -142,12 +143,20 @@
     norm_ref[...] = layer_norm(single).astype(BF16)
 
 
-def query_step(own_ref, after_ref, before_ref, far_ref, norm_ref, proj_ref, q_ref, gate_ref):
+def query_step(
+    own_ref, after_ref, before_ref, far_ref, norm_ref, proj_hbm, q_ref, gate_ref, proj_ref, sems
+):
+    copies = [
+        pltpu.make_async_copy(proj_hbm.at[3 * i], proj_ref.at[i], sems.at[i]) for i in range(2)
+    ]
+    for copy in copies:
+        copy.start()
     tokens = norm_ref.shape[0]
     lane = 2 * SLOT
     rows = jnp.concatenate(
         [own_ref[...], after_ref[...], before_ref[...], far_ref[...]], axis=0
     )
+    copies[0].wait()
     bands = spread(dot(rows, proj_ref[0]).astype(BF16))
     ring = lax.axis_size("col") // 2
     me = lax.axis_index("col")
@@ -161,24 +170,51 @@
                 block = band[first : first + tokens].astype(BF16)
                 q_ref[2 * g, at, :] = block[:, :lane]
                 q_ref[2 * g + 1, at, :] = block[:, lane:]
-    gates = jax.nn.sigmoid(dot(norm_ref[...], proj_ref[3]))
+    copies[1].wait()
+    gates = jax.nn.sigmoid(dot(norm_ref[...], proj_ref[1]))
     top = gates.astype(BF16)
     rest = (gates - top.astype(F32)).astype(BF16)
     for g, (a, b) in enumerate(zip(spread(top), spread(rest))):
         gate_ref[:, g * BAND : (g + 1) * BAND] = a + b
 
 
-def project(blocks_ref, proj_ref, k_ref, v_ref):
+def key_rows(blocks_ref, weight, k_ref):
     rows = jnp.concatenate([blocks_ref[i] for i in ORDER], axis=0)
-    store_pairs(k_ref, spread(dot(rows, proj_ref[1]).astype(BF16)))
+    store_pairs(k_ref, spread(dot(rows, weight).astype(BF16)))
+
+
+def value_rows(blocks_ref, weight, v_ref):
+    rows = jnp.concatenate([blocks_ref[i] for i in ORDER], axis=0)
     mass = lanes((1, BAND), 1) % SLOT == HEAD_DIM
-    bands = spread(dot(rows, proj_ref[2]).astype(BF16))
+    bands = spread(dot(rows, weight).astype(BF16))
     store_pairs(v_ref, [jnp.where(mass, 1.0, band) for band in bands])
 
 
-def token_step(q_ref, k_ref, v_ref, blocks_ref, proj_ref, bias_ref, part_ref, other_k, other_v):
-    lane = 2 * SLOT
-    project(blocks_ref, proj_ref, other_k, other_v)
+def near_step(blocks_ref, proj_hbm, k_ref, v_ref, proj_ref, sems):
+    copies = [
+        pltpu.make_async_copy(proj_hbm.at[1 + i], proj_ref.at[i], sems.at[i]) for i in range(2)
+    ]
+    for copy in copies:
+        copy.start()
+    copies[0].wait()
+    key_rows(blocks_ref, proj_ref[0], k_ref)
+    copies[1].wait()
+    value_rows(blocks_ref, proj_ref[1], v_ref)
+
+
+def token_step(
+    q_ref, k_ref, v_ref, blocks_ref, proj_ref, bias_hbm, part_ref, bias_ref, other_k, other_v, sems
+):
+    lane = 2 * SLOT
+    heads = (slice(0, 4), slice(4, HEADS))
+    copies = [
+        pltpu.make_async_copy(bias_hbm.at[span], bias_ref.at[span], sems.at[i])
+        for i, span in enumerate(heads)
+    ]
+    for copy in copies:
+        copy.start()
+    key_rows(blocks_ref, proj_ref[0], other_k)
+    value_rows(blocks_ref, proj_ref[1], other_v)
     core = lax.rem(lax.axis_index("row"), 2)
     count, half = q_ref.shape[1], k_ref.shape[1]
     mine_at = pl.ds(pl.multiple_of(core * half, lane), half)
@@ -186,6 +222,10 @@
     at = lanes((count, lane), 1)
     factor = 1.0 / math.sqrt(HEAD_DIM)
     for pair in range(PAIRS):
+        if pair == 0:
+            copies[0].wait()
+        if pair == 2:
+            copies[1].wait()
         query = q_ref[pair]
         key = jnp.concatenate([k_ref[pair], other_k[pair]], axis=0)
         value = jnp.concatenate([v_ref[pair], other_v[pair]], axis=0)
@@ -322,28 +362,40 @@
     far = lax.ppermute(near, "row", [(i, i ^ 1) for i in range(rows)])
     q_count, half = cols * tokens, rows * tokens // 2
     lane = 2 * SLOT
+    in_vmem, in_hbm = (pl.BlockSpec(memory_space=space) for space in (pltpu.VMEM, pltpu.HBM))
     queries, gates = call(
         query_step,
         (shape((PAIRS, q_count, lane), BF16), shape((tokens, wide), F32)),
-        14,
+        MOST,
         SMALL,
+        in_specs=[in_vmem] * 5 + [in_hbm],
+        scratch_shapes=[pltpu.VMEM((2, depth, depth), BF16), pltpu.SemaphoreType.DMA((2,))],
     )(own, *along, norm, token_proj)
-    near_k, near_v = call(
-        project,
-        (shape((PAIRS, half, lane), BF16), shape((PAIRS, half, lane), BF16)),
-        14,
+    near_k, near_v, key_weights = call(
+        near_step,
+        (
+            shape((PAIRS, half, lane), BF16),
+            shape((PAIRS, half, lane), BF16),
+            shape((2, depth, depth), BF16),
+        ),
+        MOST,
         SMALL,
+        in_specs=[in_vmem, in_hbm],
+        scratch_shapes=[pltpu.SemaphoreType.DMA((2,))],
     )(near, token_proj)
     parts = call(
         token_step,
         shape((q_count, wide), BF16),
-        32,
+        MOST,
         (6_000_000_000, 14_000_000),
+        in_specs=[in_vmem] * 5 + [in_hbm],
         scratch_shapes=[
+            pltpu.VMEM((HEADS, q_count, 2 * half), BF16),
             pltpu.VMEM((PAIRS, half, lane), BF16),
             pltpu.VMEM((PAIRS, half, lane), BF16),
+            pltpu.SemaphoreType.DMA((2,)),
         ],
-    )(queries, near_k, near_v, far, token_proj, pair_bias)
+    )(queries, near_k, near_v, far, key_weights, pair_bias)
     parts = lax.all_to_all(parts.reshape(cols, tokens, wide), "col", 0, 0)
     return call(
         last_step,

time: 88.3 us -> 84.9 us (0.961)
  local copies, waits for them, and re-layouts: 8.29 us -> 1.66 us
  Pallas kernels: 19.8 us -> 23 us
    unnamed x16 -> x12, local copies, waits for them, and re-layouts: 6.66 us -> 0.03 us
    pallas_call x2, Pallas kernels: 11.4 us -> 13.8 us  [the longest x1 10.4 us: per_device(): call(token_step, shape((q_count, wide), BF16), MOST, (6000000000, 1400000...]
    pallas_call x1, Pallas kernels: 1.36 us -> 2.24 us  [per_device(): call(query_step, (shape((PAIRS, q_count, lane), BF16), shape((tokens, wid...]
  transfers between devices with their start and end apart: 9 -> 9, of which waited for: 5 -> 5; matrix products, arithmetic and copies ran while one was open for 1% -> 1% of each run, Pallas kernels for 3% -> 7%
where the time goes in v4:
time: 84.9 us; the launch traced here: 84.5 us
  starting transfers between devices  29.9 us (35%)
  Pallas kernels  23 us (27%)
  blocking collectives  19.1 us (22%)
  waiting for transfers between devices  8.92 us (11%)
  local copies, waits for them, and re-layouts  1.66 us (2%)
  other arithmetic  1.17 us (1%)
    all_to_all x1, blocking collectives, per_device(): parts = lax.all_to_all(parts.reshape(cols, tokens, wide), 'col', 0, 0)  19.1 us
    ppermute x1, starting transfers between devices, per_device(): lax.ppermute(norm, 'col', [(i, (i + ring) % cols) for i in range(cols)])  11 us
    pallas_call x1, Pallas kernels, per_device(): call(token_step, shape((q_count, wide), BF16), MOST, (6000000000, 1400000...  10.4 us
    all_to_all x1, starting transfers between devices, per_device(): lax.all_to_all(jnp.broadcast_to(turned[None], (rows // 2, tokens, depth))...  6.12 us
    ppermute x3, waiting for transfers between devices, per_device(): lax.ppermute(own, 'col', [(i, i // ring * ring + (i + step) % ring) for i...  5.48 us
    pallas_call x1, Pallas kernels, per_device(): call(atom_step, (shape((count, width), F32), shape((tokens, depth), F32),...  4.74 us
    ppermute x1, starting transfers between devices, per_device(): lax.ppermute(atom_state[count - REACH:], BOTH, [(i, i + 1) for i in range...  4.55 us
    ppermute x3, starting transfers between devices, per_device(): lax.ppermute(own, 'col', [(i, i // ring * ring + (i + step) % ring) for i...  3.67 us
  transfers between devices with their start and end apart: 9, of which 5 were waited for; matrix products, arithmetic and copies ran while one was open for 1% of the time, Pallas kernels for 7%

profile of v4, /device:TPU:0, one launch (start us, length us, event | category | flops | bytes accessed | tf_op | source)
XLA Modules:
  0.0 84.5 jit_solution(14542344076518169537)
XLA Ops:
  0.7 0.8 fusion
  1.4 1.3 %collective-permute-start.1 = (bf16[48,128]{1,0:T(8,128)(2,1)S(1)}, bf16[48,128]{1,0:T(8,128)(2,1)S(1)}, u32[]{:S(2)}, u32[]{:S(2)}) collective-permute-start(bf16[48,128]{1,0:T(8,128)(2,1)S(1)} %get-tuple-element.30), channel_id=1, source_target_pairs={{1,0},{2,1},{3,2},{4,3},{5,4},{6,5},{7,6},{8,7},{9,8},{10,9},{11,1... | collective-permute-start | bytes 36872 | tf_op jit(solution)/shard_map/ppermute | solution.py:323
  2.7 4.5 %collective-permute-start = (bf16[48,128]{1,0:T(8,128)(2,1)S(1)}, bf16[48,128]{1,0:T(8,128)(2,1)S(1)}, u32[]{:S(2)}, u32[]{:S(2)}) collective-permute-start(bf16[48,128]{1,0:T(8,128)(2,1)S(1)} %get-tuple-element.31), channel_id=1, source_target_pairs={{0,1},{1,2},{2,3},{3,4},{4,5},{5,6},{6,7},{7,8},{8,9},{9,10},{10,1... | collective-permute-start | bytes 36872 | tf_op jit(solution)/shard_map/ppermute | solution.py:320
  7.3 1.1 %pad_maximum_fusion.narrow_ref = bf16[2560,128]{1,0:T(8,128)(2,1)S(1)} fusion(bf16[128,128]{1,0:T(8,128)(2,1)} %param.17, bf16[512,128]{1,0:T(8,128)(2,1)} %bitcast.5, bf16[1536,128]{1,0:T(8,128)(2,1)} %bitcast.4, bf16[384,128]{1,0:T(8,128)(2,1)} %param.11), kind=kLoop, calls=%fused_computation | loop fusion | flops 2621440 | bytes 1310720 | tf_op jit(solution)/shard_map/concatenate | solution.py:324
  8.5 0.2 collective-permute-done.left_ref
  8.7 4.7 %shard_map.122 = (f32[384,128]{1,0:T(8,128)S(1)}, f32[48,768]{1,0:T(8,128)S(1)}, bf16[48,768]{1,0:T(8,128)(2,1)S(1)}) custom-call(bf16[48,128]{1,0:T(8,128)(2,1)S(1)} %collective-permute-done.left_ref, bf16[48,128]{1,0:T(8,128)(2,1)S(1)} %collective-permute-done.1.right_ref, bf16[2560,128]{1,0:T(8,128)(2,1)S(1)} %pad_maximum_fusion.narrow_ref, ...), custom_call_target="tpu_custom_call" | custom-call | flops 400000000 | bytes 2000000 | tf_op jit(solution)/shard_map/pallas_call | solution.py:330
  13.4 11.0 %collective-permute-start.3 = (bf16[48,768]{1,0:T(8,128)(2,1)S(1)}, bf16[48,768]{1,0:T(8,128)(2,1)S(1)}, u32[]{:S(2)}, u32[]{:S(2)}) collective-permute-start(bf16[48,768]{1,0:T(8,128)(2,1)S(1)} %get-tuple-element.16.norm_ref), channel_id=1, source_target_pairs={{0,4},{1,5},{2,6},{3,7},{4,0},{5,1},{6,2},{7,3},{8,12},{9,13},{10,... | collective-permute-start | bytes 221192 | tf_op jit(solution)/shard_map/ppermute | solution.py:347
  24.5 3.2 %collective-permute-start.2 = (bf16[48,768]{1,0:T(8,128)(2,1)S(1)}, bf16[48,768]{1,0:T(8,128)(2,1)S(1)}, u32[]{:S(2)}, u32[]{:S(2)}) collective-permute-start(bf16[48,768]{1,0:T(8,128)(2,1)S(1)} %get-tuple-element.16.norm_ref), channel_id=1, source_target_pairs={{0,32},{1,48},{2,0},{3,16},{4,96},{5,112},{6,64},{7,80},{8,40},{9,... | collective-permute-start | bytes 221192 | tf_op jit(solution)/shard_map/ppermute | solution.py:346
  27.7 3.2 %collective-permute-done.2 = bf16[48,768]{1,0:T(8,128)(2,1)S(1)} collective-permute-done((bf16[48,768]{1,0:T(8,128)(2,1)S(1)}, bf16[48,768]{1,0:T(8,128)(2,1)S(1)}, u32[]{:S(2)}, u32[]{:S(2)}) %collective-permute-start.2) | collective-permute-done | bytes 73760 | tf_op jit(solution)/shard_map/ppermute | solution.py:346
  30.9 0.9 %broadcast_in_dim.2 = bf16[8,48,768]{2,1,0:T(8,128)(2,1)} broadcast(bf16[48,768]{1,0:T(8,128)(2,1)S(1)} %collective-permute-done.2), dimensions={1,2} | broadcast | bytes 663552 | tf_op jit(solution)/shard_map/broadcast_in_dim | solution.py:352
  31.8 6.1 %all-to-all-start = ((bf16[8,48,768]{2,1,0:T(8,128)(2,1)}), bf16[8,48,768]{2,1,0:T(8,128)(2,1)S(1)}, u32[]{:S(2)}, u32[]{:S(2)}) async-start(bf16[8,48,768]{2,1,0:T(8,128)(2,1)} %broadcast_in_dim.2), calls=%async_computation | async-start | bytes 1179648 | tf_op jit(solution)/shard_map/all_to_all | solution.py:351
  37.9 1.6 %collective-permute-start.6 = (bf16[96,768]{1,0:T(8,128)(2,1)S(1)}, bf16[96,768]{1,0:T(8,128)(2,1)S(1)}, u32[]{:S(2)}, u32[]{:S(2)}) collective-permute-start(bf16[96,768]{1,0:T(8,128)(2,1)S(1)} %pad_maximum_fusion.2.own_ref), channel_id=1, source_target_pairs={{0,2},{1,3},{2,0},{3,1},{4,6},{5,7},{6,4},{7,5},{8,10},{9,11},{10,... | collective-permute-start | bytes 442376 | tf_op jit(solution)/shard_map/ppermute | solution.py:356
  39.5 1.2 %collective-permute-start.5 = (bf16[96,768]{1,0:T(8,128)(2,1)S(1)}, bf16[96,768]{1,0:T(8,128)(2,1)S(1)}, u32[]{:S(2)}, u32[]{:S(2)}) collective-permute-start(bf16[96,768]{1,0:T(8,128)(2,1)S(1)} %pad_maximum_fusion.2.own_ref), channel_id=1, source_target_pairs={{0,3},{1,0},{2,1},{3,2},{4,7},{5,4},{6,5},{7,6},{8,11},{9,8},{10,9... | collective-permute-start | bytes 442376 | tf_op jit(solution)/shard_map/ppermute | solution.py:356
  40.7 0.9 %collective-permute-start.4 = (bf16[96,768]{1,0:T(8,128)(2,1)S(1)}, bf16[96,768]{1,0:T(8,128)(2,1)S(1)}, u32[]{:S(2)}, u32[]{:S(2)}) collective-permute-start(bf16[96,768]{1,0:T(8,128)(2,1)S(1)} %pad_maximum_fusion.2.own_ref), channel_id=1, source_target_pairs={{0,1},{1,2},{2,3},{3,0},{4,5},{5,6},{6,7},{7,4},{8,9},{9,10},{10,1... | collective-permute-start | bytes 442376 | tf_op jit(solution)/shard_map/ppermute | solution.py:356
  41.6 3.1 %collective-permute-done.6.far_ref = bf16[96,768]{1,0:T(8,128)(2,1)S(1)} collective-permute-done((bf16[96,768]{1,0:T(8,128)(2,1)S(1)}, bf16[96,768]{1,0:T(8,128)(2,1)S(1)}, u32[]{:S(2)}, u32[]{:S(2)}) %collective-permute-start.6) | collective-permute-done | bytes 147488 | tf_op jit(solution)/shard_map/ppermute | solution.py:356
  44.7 0.6 collective-permute-done.5.before_ref
  45.2 1.8 %collective-permute-done.4.after_ref = bf16[96,768]{1,0:T(8,128)(2,1)S(1)} collective-permute-done((bf16[96,768]{1,0:T(8,128)(2,1)S(1)}, bf16[96,768]{1,0:T(8,128)(2,1)S(1)}, u32[]{:S(2)}, u32[]{:S(2)}) %collective-permute-start.4) | collective-permute-done | bytes 147488 | tf_op jit(solution)/shard_map/ppermute | solution.py:356
  47.1 3.3 %shard_map.124 = (bf16[8,384,128]{2,1,0:T(8,128)(2,1)S(1)}, bf16[8,384,128]{2,1,0:T(8,128)(2,1)S(1)}, bf16[2,768,768]{2,1,0:T(8,128)(2,1)S(1)}) custom-call(bf16[8,48,768]{2,1,0:T(8,128)(2,1)S(1)} %all-to-all-done.blocks_ref, bf16[4,768,768]{2,1,0:T(8,128)(2,1)} %proj_hbm.3), custom_call_target="tpu_custom_call" | custom-call | flops 1000000 | bytes 100000 | tf_op jit(solution)/shard_map/pallas_call | solution.py:374
  50.4 2.2 %shard_map.123 = (bf16[8,384,128]{2,1,0:T(8,128)(2,1)S(1)}, f32[48,1024]{1,0:T(8,128)S(1)}) custom-call(bf16[96,768]{1,0:T(8,128)(2,1)S(1)} %pad_maximum_fusion.2.own_ref, bf16[96,768]{1,0:T(8,128)(2,1)S(1)} %collective-permute-done.4.after_ref, bf16[96,768]{1,0:T(8,128)(2,1)S(1)} %collective-permute-done.5.before_ref, ...), custom_call_target="tpu_custom_call" | custom-call | flops 1000000 | bytes 100000 | tf_op jit(solution)/shard_map/pallas_call | solution.py:366
  52.7 10.4 %shard_map.125 = bf16[384,1024]{1,0:T(8,128)(2,1)S(1)} custom-call(bf16[8,384,128]{2,1,0:T(8,128)(2,1)S(1)} %get-tuple-element.22.q_ref, bf16[8,384,128]{2,1,0:T(8,128)(2,1)S(1)} %get-tuple-element.24.k_ref, bf16[8,384,128]{2,1,0:T(8,128)(2,1)S(1)} %get-tuple-element.25.v_ref, bf16[8,48,768]{2,1,0:T(8,128)(2,1)S(1)} %collective-permute-done.7.blocks_ref, ...), custom_call_target="tpu_custom_call" | custom-call | flops 6000000000 | bytes 14000000 | tf_op jit(solution)/shard_map/pallas_call | solution.py:386
  63.1 0.0 copy-start.1
  63.1 0.0 copy-start.2
  63.1 19.1 %all_to_all.10.part_ref = bf16[8,48,1024]{2,1,0:T(8,128)(2,1)S(1)} all-to-all(bf16[8,48,1024]{2,1,0:T(8,128)(2,1)S(1)} %bitcast.3), channel_id=1, replica_groups=mesh['row'=16,'col'=8] {'col'}, dimensions={0} | all-to-all | bytes 1572864 | tf_op jit(solution)/shard_map/all_to_all | solution.py:399
  82.2 2.3 %shard_map.126 = (bf16[384,128]{1,0:T(8,128)(2,1)}, bf16[48,768]{1,0:T(8,128)(2,1)}) custom-call(bf16[8,48,1024]{2,1,0:T(8,128)(2,1)S(1)} %all_to_all.10.part_ref, f32[48,1024]{1,0:T(8,128)S(1)} %get-tuple-element.27.gate_ref, f32[48,768]{1,0:T(8,128)S(1)} %get-tuple-element.28.single_ref, f32[384,128]{1,0:T(8,128)S(1)} %get-tuple-element.29.mid_ref, ...), custom_call_target="tpu_custom_call" | custom-call | flops 400000000 | bytes 5000000 | tf_op jit(solution)/shard_map/pallas_call | solution.py:400
  (17 shorter events, 0.1 us)
Async XLA Ops:
  0.6 7.8 %copy-start.4 = (bf16[128,768]{1,0:T(8,128)(2,1)S(1)}, bf16[128,768]{1,0:T(8,128)(2,1)}, u32[]{:S(2)}) copy-start(bf16[128,768]{1,0:T(8,128)(2,1)} %param.18) | copy-start | bytes 589828
  0.6 7.8 %copy-start.5 = (bf16[48,768]{1,0:T(8,128)(2,1)S(1)}, bf16[48,768]{1,0:T(8,128)(2,1)}, u32[]{:S(2)}) copy-start(bf16[48,768]{1,0:T(8,128)(2,1)} %param.12) | copy-start | bytes 221188
  0.7 8.0 %copy-start.3 = (s32[1,384]{1,0:T(1,128)S(1)}, s32[1,384]{1,0:T(1,128)}, u32[]{:S(2)}) copy-start(s32[1,384]{1,0:T(1,128)} %owner_ref.3) | copy-start | bytes 4612
  1.4 7.0 %collective-permute-start.1 = (bf16[48,128]{1,0:T(8,128)(2,1)S(1)}, bf16[48,128]{1,0:T(8,128)(2,1)S(1)}, u32[]{:S(2)}, u32[]{:S(2)}) collective-permute-start(bf16[48,128]{1,0:T(8,128)(2,1)S(1)} %get-tuple-element.30), channel_id=1, source_target_pairs={{1,0},{2,1},{3,2},{4,3},{5,4},{6,5},{7,6},{8,7},{9,8},{10,9},{11,1... | collective-permute-start | bytes 36872 | tf_op jit(solution)/shard_map/ppermute | solution.py:323
  2.7 5.9 %collective-permute-start = (bf16[48,128]{1,0:T(8,128)(2,1)S(1)}, bf16[48,128]{1,0:T(8,128)(2,1)S(1)}, u32[]{:S(2)}, u32[]{:S(2)}) collective-permute-start(bf16[48,128]{1,0:T(8,128)(2,1)S(1)} %get-tuple-element.31), channel_id=1, source_target_pairs={{0,1},{1,2},{2,3},{3,4},{4,5},{5,6},{6,7},{7,8},{8,9},{9,10},{10,1... | collective-permute-start | bytes 36872 | tf_op jit(solution)/shard_map/ppermute | solution.py:320
  13.4 14.2 %collective-permute-start.3 = (bf16[48,768]{1,0:T(8,128)(2,1)S(1)}, bf16[48,768]{1,0:T(8,128)(2,1)S(1)}, u32[]{:S(2)}, u32[]{:S(2)}) collective-permute-start(bf16[48,768]{1,0:T(8,128)(2,1)S(1)} %get-tuple-element.16.norm_ref), channel_id=1, source_target_pairs={{0,4},{1,5},{2,6},{3,7},{4,0},{5,1},{6,2},{7,3},{8,12},{9,13},{10,... | collective-permute-start | bytes 221192 | tf_op jit(solution)/shard_map/ppermute | solution.py:347
  24.5 6.5 %collective-permute-start.2 = (bf16[48,768]{1,0:T(8,128)(2,1)S(1)}, bf16[48,768]{1,0:T(8,128)(2,1)S(1)}, u32[]{:S(2)}, u32[]{:S(2)}) collective-permute-start(bf16[48,768]{1,0:T(8,128)(2,1)S(1)} %get-tuple-element.16.norm_ref), channel_id=1, source_target_pairs={{0,32},{1,48},{2,0},{3,16},{4,96},{5,112},{6,64},{7,80},{8,40},{9,... | collective-permute-start | bytes 221192 | tf_op jit(solution)/shard_map/ppermute | solution.py:346
  31.8 15.3 %all-to-all-start = ((bf16[8,48,768]{2,1,0:T(8,128)(2,1)}), bf16[8,48,768]{2,1,0:T(8,128)(2,1)S(1)}, u32[]{:S(2)}, u32[]{:S(2)}) async-start(bf16[8,48,768]{2,1,0:T(8,128)(2,1)} %broadcast_in_dim.2), calls=%async_computation | async-start | bytes 1179648 | tf_op jit(solution)/shard_map/all_to_all | solution.py:351
  37.9 6.8 %collective-permute-start.6 = (bf16[96,768]{1,0:T(8,128)(2,1)S(1)}, bf16[96,768]{1,0:T(8,128)(2,1)S(1)}, u32[]{:S(2)}, u32[]{:S(2)}) collective-permute-start(bf16[96,768]{1,0:T(8,128)(2,1)S(1)} %pad_maximum_fusion.2.own_ref), channel_id=1, source_target_pairs={{0,2},{1,3},{2,0},{3,1},{4,6},{5,7},{6,4},{7,5},{8,10},{9,11},{10,... | collective-permute-start | bytes 442376 | tf_op jit(solution)/shard_map/ppermute | solution.py:356
  39.5 5.7 %collective-permute-start.5 = (bf16[96,768]{1,0:T(8,128)(2,1)S(1)}, bf16[96,768]{1,0:T(8,128)(2,1)S(1)}, u32[]{:S(2)}, u32[]{:S(2)}) collective-permute-start(bf16[96,768]{1,0:T(8,128)(2,1)S(1)} %pad_maximum_fusion.2.own_ref), channel_id=1, source_target_pairs={{0,3},{1,0},{2,1},{3,2},{4,7},{5,4},{6,5},{7,6},{8,11},{9,8},{10,9... | collective-permute-start | bytes 442376 | tf_op jit(solution)/shard_map/ppermute | solution.py:356
  40.7 6.4 %collective-permute-start.4 = (bf16[96,768]{1,0:T(8,128)(2,1)S(1)}, bf16[96,768]{1,0:T(8,128)(2,1)S(1)}, u32[]{:S(2)}, u32[]{:S(2)}) collective-permute-start(bf16[96,768]{1,0:T(8,128)(2,1)S(1)} %pad_maximum_fusion.2.own_ref), channel_id=1, source_target_pairs={{0,1},{1,2},{2,3},{3,0},{4,5},{5,6},{6,7},{7,4},{8,9},{9,10},{10,1... | collective-permute-start | bytes 442376 | tf_op jit(solution)/shard_map/ppermute | solution.py:356
  47.1 5.6 %collective-permute-start.7 = (bf16[8,48,768]{2,1,0:T(8,128)(2,1)S(1)}, bf16[8,48,768]{2,1,0:T(8,128)(2,1)S(1)}, u32[]{:S(2)}, u32[]{:S(2)}) collective-permute-start(bf16[8,48,768]{2,1,0:T(8,128)(2,1)S(1)} %all-to-all-done.blocks_ref), channel_id=1, source_target_pairs={{0,8},{8,0},{16,24},{24,16},{32,40},{40,32},{48,56},{56,48},{64,72... | collective-permute-start | bytes 1769480 | tf_op jit(solution)/shard_map/ppermute | solution.py:362
  47.1 3.3 %copy-start = (bf16[4,768,768]{2,1,0:T(8,128)(2,1)S(1)}, bf16[4,768,768]{2,1,0:T(8,128)(2,1)}, u32[]{:S(2)}) copy-start(bf16[4,768,768]{2,1,0:T(8,128)(2,1)} %proj_hbm.3) | copy-start | bytes 14155780
  63.1 19.1 %copy-start.1 = (bf16[768,768]{1,0:T(8,128)(2,1)S(1)}, bf16[768,768]{1,0:T(8,128)(2,1)}, u32[]{:S(2)}) copy-start(bf16[768,768]{1,0:T(8,128)(2,1)} %output_ref.1) | copy-start | bytes 3538948
  63.1 19.1 %copy-start.2 = (bf16[768,128]{1,0:T(8,128)(2,1)S(1)}, bf16[768,128]{1,0:T(8,128)(2,1)}, u32[]{:S(2)}) copy-start(bf16[768,128]{1,0:T(8,128)(2,1)} %back_ref.1) | copy-start | bytes 589828

commit v5 on v3

--- a/solution.py
+++ b/solution.py
@@ -306,19 +306,18 @@
     turned = lax.ppermute(norm, BOTH, turn)
     across = lax.ppermute(norm, "col", [(i, (i + ring) % cols) for i in range(cols)])
     own = jnp.concatenate([norm, across], axis=0)
-    turned, own = lax.optimization_barrier((turned, own))
-    same_core = [[i for i in range(rows) if i % 2 == e] for e in range(2)]
-    near = lax.all_to_all(
-        jnp.broadcast_to(turned[None], (rows // 2, tokens, depth)), "row", 0, 0,
-        axis_index_groups=same_core,
-    )
     along = [
         lax.ppermute(
             own, "col", [(i, i // ring * ring + (i + step) % ring) for i in range(cols)]
         )
         for step in (1, ring - 1, 2)
     ]
-    near, *along = lax.optimization_barrier((near, *along))
+    turned, *along = lax.optimization_barrier((turned, *along))
+    same_core = [[i for i in range(rows) if i % 2 == e] for e in range(2)]
+    near = lax.all_to_all(
+        jnp.broadcast_to(turned[None], (rows // 2, tokens, depth)), "row", 0, 0,
+        axis_index_groups=same_core,
+    )
     far = lax.ppermute(near, "row", [(i, i ^ 1) for i in range(rows)])
     q_count, half = cols * tokens, rows * tokens // 2
     lane = 2 * SLOT

time: 88.3 us -> 88.9 us (level)
  blocking collectives: 19.1 us -> 32.3 us
  local copies, waits for them, and re-layouts: 8.29 us -> 1.41 us
  starting transfers between devices: 29.9 us -> 25 us
  waiting for transfers between devices: 8.92 us -> 7.71 us
    all_to_all x0 -> x1, blocking collectives: none -> 14.8 us  [per_device(): lax.all_to_all(jnp.broadcast_to(turned[None], (rows // 2, tokens, depth))...]
    all_to_all x1 -> x0, starting transfers between devices: 6.12 us -> none  [per_device(): lax.all_to_all(jnp.broadcast_to(turned[None], (rows // 2, tokens, depth))...]
    unnamed x16 -> x15, local copies, waits for them, and re-layouts: 6.66 us -> 0.59 us
    ppermute x3, waiting for transfers between devices: 5.48 us -> 0.01 us  [per_device(): lax.ppermute(own, 'col', [(i, i // ring * ring + (i + step) % ring) for i...]
    ppermute x1, starting transfers between devices: 3.19 us -> 5.99 us  [per_device(): turned = lax.ppermute(norm, BOTH, turn)]
    ppermute x1, waiting for transfers between devices: 0.01 us -> 2.33 us  [per_device(): lax.ppermute(norm, 'col', [(i, (i + ring) % cols) for i in range(cols)])]
    ppermute x1, waiting for transfers between devices: 3.25 us -> 5.34 us  [per_device(): turned = lax.ppermute(norm, BOTH, turn)]
    all_to_all x1, blocking collectives: 19.1 us -> 17.5 us  [per_device(): parts = lax.all_to_all(parts.reshape(cols, tokens, wide), 'col', 0, 0)]
  transfers between devices with their start and end apart: 9 -> 8, of which waited for: 5 -> 2; matrix products, arithmetic and copies ran while one was open for 1% -> 1% of each run, Pallas kernels for 3% -> 4%
where the time goes in v5:
time: 88.9 us; the launch traced here: 88.5 us
  blocking collectives  32.3 us (36%)
  starting transfers between devices  25 us (28%)
  Pallas kernels  20.1 us (23%)
  waiting for transfers between devices  7.71 us (9%)
  local copies, waits for them, and re-layouts  1.41 us (2%)
  other arithmetic  1.31 us (1%)
    all_to_all x1, blocking collectives, per_device(): parts = lax.all_to_all(parts.reshape(cols, tokens, wide), 'col', 0, 0)  17.5 us
    all_to_all x1, blocking collectives, per_device(): lax.all_to_all(jnp.broadcast_to(turned[None], (rows // 2, tokens, depth))...  14.8 us
    ppermute x1, starting transfers between devices, per_device(): lax.ppermute(norm, 'col', [(i, (i + ring) % cols) for i in range(cols)])  11 us
    pallas_call x1, Pallas kernels, per_device(): call(token_step, shape((q_count, wide), BF16), 32, (6000000000, 14000000)...  9.91 us
    ppermute x1, starting transfers between devices, per_device(): turned = lax.ppermute(norm, BOTH, turn)  5.99 us
    ppermute x1, waiting for transfers between devices, per_device(): turned = lax.ppermute(norm, BOTH, turn)  5.34 us
    pallas_call x1, Pallas kernels, per_device(): call(atom_step, (shape((count, width), F32), shape((tokens, depth), F32),...  4.74 us
    ppermute x1, starting transfers between devices, per_device(): lax.ppermute(atom_state[count - REACH:], BOTH, [(i, i + 1) for i in range...  4.55 us
  transfers between devices with their start and end apart: 8, of which 2 were waited for; matrix products, arithmetic and copies ran while one was open for 1% of the time, Pallas kernels for 4%

profile of v5, /device:TPU:0, one launch (start us, length us, event | category | flops | bytes accessed | tf_op | source)
XLA Modules:
  0.0 88.5 jit_solution(974382378425113793)
XLA Ops:
  0.7 0.8 fusion
  1.4 1.3 %collective-permute-start.1 = (bf16[48,128]{1,0:T(8,128)(2,1)S(1)}, bf16[48,128]{1,0:T(8,128)(2,1)S(1)}, u32[]{:S(2)}, u32[]{:S(2)}) collective-permute-start(bf16[48,128]{1,0:T(8,128)(2,1)S(1)} %get-tuple-element.24), channel_id=1, source_target_pairs={{1,0},{2,1},{3,2},{4,3},{5,4},{6,5},{7,6},{8,7},{9,8},{10,9},{11,1... | collective-permute-start | bytes 36872 | tf_op jit(solution)/shard_map/ppermute | solution.py:283
  2.7 4.5 %collective-permute-start = (bf16[48,128]{1,0:T(8,128)(2,1)S(1)}, bf16[48,128]{1,0:T(8,128)(2,1)S(1)}, u32[]{:S(2)}, u32[]{:S(2)}) collective-permute-start(bf16[48,128]{1,0:T(8,128)(2,1)S(1)} %get-tuple-element.25), channel_id=1, source_target_pairs={{0,1},{1,2},{2,3},{3,4},{4,5},{5,6},{6,7},{7,8},{8,9},{9,10},{10,1... | collective-permute-start | bytes 36872 | tf_op jit(solution)/shard_map/ppermute | solution.py:280
  7.3 0.0 copy-start
  7.3 1.3 %pad_maximum_fusion.narrow_ref = bf16[2560,128]{1,0:T(8,128)(2,1)S(1)} fusion(bf16[128,128]{1,0:T(8,128)(2,1)} %param.17, bf16[512,128]{1,0:T(8,128)(2,1)} %bitcast.5, bf16[1536,128]{1,0:T(8,128)(2,1)} %bitcast.4, bf16[384,128]{1,0:T(8,128)(2,1)} %param.11), kind=kLoop, calls=%fused_computation | loop fusion | flops 2621440 | bytes 1310720 | tf_op jit(solution)/shard_map/concatenate | solution.py:284
  8.6 0.0 collective-permute-done.left_ref
  8.7 4.7 %shard_map.122 = (f32[384,128]{1,0:T(8,128)S(1)}, f32[48,768]{1,0:T(8,128)S(1)}, bf16[48,768]{1,0:T(8,128)(2,1)S(1)}) custom-call(bf16[48,128]{1,0:T(8,128)(2,1)S(1)} %collective-permute-done.left_ref, bf16[48,128]{1,0:T(8,128)(2,1)S(1)} %collective-permute-done.1.right_ref, bf16[2560,128]{1,0:T(8,128)(2,1)S(1)} %pad_maximum_fusion.narrow_ref, ...), custom_call_target="tpu_custom_call" | custom-call | flops 400000000 | bytes 2000000 | tf_op jit(solution)/shard_map/pallas_call | solution.py:290
  13.4 11.0 %collective-permute-start.2 = (bf16[48,768]{1,0:T(8,128)(2,1)S(1)}, bf16[48,768]{1,0:T(8,128)(2,1)S(1)}, u32[]{:S(2)}, u32[]{:S(2)}) collective-permute-start(bf16[48,768]{1,0:T(8,128)(2,1)S(1)} %get-tuple-element.13.norm_ref), channel_id=1, source_target_pairs={{0,4},{1,5},{2,6},{3,7},{4,0},{5,1},{6,2},{7,3},{8,12},{9,13},{10,... | collective-permute-start | bytes 221192 | tf_op jit(solution)/shard_map/ppermute | solution.py:307
  24.5 2.3 %collective-permute-done.2 = bf16[48,768]{1,0:T(8,128)(2,1)S(1)} collective-permute-done((bf16[48,768]{1,0:T(8,128)(2,1)S(1)}, bf16[48,768]{1,0:T(8,128)(2,1)S(1)}, u32[]{:S(2)}, u32[]{:S(2)}) %collective-permute-start.2) | collective-permute-done | bytes 73760 | tf_op jit(solution)/shard_map/ppermute | solution.py:307
  26.8 0.0 collective-permute-start.6
  26.8 0.4 collective-permute-start.5
  27.2 1.7 %collective-permute-start.4 = (bf16[96,768]{1,0:T(8,128)(2,1)S(1)}, bf16[96,768]{1,0:T(8,128)(2,1)S(1)}, u32[]{:S(2)}, u32[]{:S(2)}) collective-permute-start(bf16[96,768]{1,0:T(8,128)(2,1)S(1)} %constant_dynamic-update-slice_fusion.own_ref), channel_id=1, source_target_pairs={{0,1},{1,2},{2,3},{3,0},{4,5},{5,6},{6,7},{7,4},{8,9},{9,10},{10,1... | collective-permute-start | bytes 442376 | tf_op jit(solution)/shard_map/ppermute | solution.py:310
  28.9 6.0 %collective-permute-start.3 = (bf16[48,768]{1,0:T(8,128)(2,1)S(1)}, bf16[48,768]{1,0:T(8,128)(2,1)S(1)}, u32[]{:S(2)}, u32[]{:S(2)}) collective-permute-start(bf16[48,768]{1,0:T(8,128)(2,1)S(1)} %get-tuple-element.13.norm_ref), channel_id=1, source_target_pairs={{0,32},{1,48},{2,0},{3,16},{4,96},{5,112},{6,64},{7,80},{8,40},{9,... | collective-permute-start | bytes 221192 | tf_op jit(solution)/shard_map/ppermute | solution.py:306
  34.9 5.3 %collective-permute-done.3 = bf16[48,768]{1,0:T(8,128)(2,1)S(1)} collective-permute-done((bf16[48,768]{1,0:T(8,128)(2,1)S(1)}, bf16[48,768]{1,0:T(8,128)(2,1)S(1)}, u32[]{:S(2)}, u32[]{:S(2)}) %collective-permute-start.3) | collective-permute-done | bytes 73760 | tf_op jit(solution)/shard_map/ppermute | solution.py:306
  40.3 14.8 %all_to_all.10.blocks_ref = bf16[8,48,768]{2,1,0:T(8,128)(2,1)S(1)} all-to-all(bf16[8,48,768]{2,1,0:T(8,128)(2,1)S(1)} %broadcast_in_dim.2), channel_id=1, replica_groups={{0,16,32,48,64,80,96,112},{8,24,40,56,72,88,104,120},{1,17,33,49,65,81,..., dimensions={0} | all-to-all | bytes 1179648 | tf_op jit(solution)/shard_map/all_to_all | solution.py:317
  55.1 0.0 collective-permute-start.7
  55.1 1.4 %shard_map.123 = (bf16[8,384,128]{2,1,0:T(8,128)(2,1)S(1)}, f32[48,1024]{1,0:T(8,128)S(1)}) custom-call(bf16[96,768]{1,0:T(8,128)(2,1)S(1)} %constant_dynamic-update-slice_fusion.own_ref, bf16[96,768]{1,0:T(8,128)(2,1)S(1)} %collective-permute-done.4.after_ref, bf16[96,768]{1,0:T(8,128)(2,1)S(1)} %collective-permute-done.5.before_ref, ...), custom_call_target="tpu_custom_call" | custom-call | flops 1000000 | bytes 100000 | tf_op jit(solution)/shard_map/pallas_call | solution.py:324
  56.4 1.7 %shard_map.124 = (bf16[8,384,128]{2,1,0:T(8,128)(2,1)S(1)}, bf16[8,384,128]{2,1,0:T(8,128)(2,1)S(1)}) custom-call(bf16[8,48,768]{2,1,0:T(8,128)(2,1)S(1)} %all_to_all.10.blocks_ref, bf16[4,768,768]{2,1,0:T(8,128)(2,1)S(1)} %copy-done), custom_call_target="tpu_custom_call" | custom-call | flops 1000000 | bytes 100000 | tf_op jit(solution)/shard_map/pallas_call | solution.py:330
  58.2 0.6 copy-done.4
  58.7 9.9 %shard_map.125 = bf16[384,1024]{1,0:T(8,128)(2,1)S(1)} custom-call(bf16[8,384,128]{2,1,0:T(8,128)(2,1)S(1)} %get-tuple-element.17.q_ref, bf16[8,384,128]{2,1,0:T(8,128)(2,1)S(1)} %get-tuple-element.19.k_ref, bf16[8,384,128]{2,1,0:T(8,128)(2,1)S(1)} %get-tuple-element.20.v_ref, bf16[8,48,768]{2,1,0:T(8,128)(2,1)S(1)} %collective-permute-done.7.blocks_ref, ...), custom_call_target="tpu_custom_call" | custom-call | flops 6000000000 | bytes 14000000 | tf_op jit(solution)/shard_map/pallas_call | solution.py:336
  68.7 0.0 copy-start.1
  68.7 0.0 copy-start.2
  68.7 17.5 %all_to_all.11.part_ref = bf16[8,48,1024]{2,1,0:T(8,128)(2,1)S(1)} all-to-all(bf16[8,48,1024]{2,1,0:T(8,128)(2,1)S(1)} %bitcast.3), channel_id=1, replica_groups=mesh['row'=16,'col'=8] {'col'}, dimensions={0} | all-to-all | bytes 1572864 | tf_op jit(solution)/shard_map/all_to_all | solution.py:346
  86.2 2.3 %shard_map.126 = (bf16[384,128]{1,0:T(8,128)(2,1)}, bf16[48,768]{1,0:T(8,128)(2,1)}) custom-call(bf16[8,48,1024]{2,1,0:T(8,128)(2,1)S(1)} %all_to_all.11.part_ref, f32[48,1024]{1,0:T(8,128)S(1)} %get-tuple-element.21.gate_ref, f32[48,768]{1,0:T(8,128)S(1)} %get-tuple-element.22.single_ref, f32[384,128]{1,0:T(8,128)S(1)} %get-tuple-element.23.mid_ref, ...), custom_call_target="tpu_custom_call" | custom-call | flops 400000000 | bytes 5000000 | tf_op jit(solution)/shard_map/pallas_call | solution.py:347
  (19 shorter events, 0.1 us)
Async XLA Ops:
  0.6 8.0 %copy-start.5 = (bf16[128,768]{1,0:T(8,128)(2,1)S(1)}, bf16[128,768]{1,0:T(8,128)(2,1)}, u32[]{:S(2)}) copy-start(bf16[128,768]{1,0:T(8,128)(2,1)} %param.18) | copy-start | bytes 589828
  0.6 8.0 %copy-start.6 = (bf16[48,768]{1,0:T(8,128)(2,1)S(1)}, bf16[48,768]{1,0:T(8,128)(2,1)}, u32[]{:S(2)}) copy-start(bf16[48,768]{1,0:T(8,128)(2,1)} %param.12) | copy-start | bytes 221188
  0.7 8.0 %copy-start.3 = (s32[1,384]{1,0:T(1,128)S(1)}, s32[1,384]{1,0:T(1,128)}, u32[]{:S(2)}) copy-start(s32[1,384]{1,0:T(1,128)} %owner_ref.3) | copy-start | bytes 4612
  1.4 7.2 %collective-permute-start.1 = (bf16[48,128]{1,0:T(8,128)(2,1)S(1)}, bf16[48,128]{1,0:T(8,128)(2,1)S(1)}, u32[]{:S(2)}, u32[]{:S(2)}) collective-permute-start(bf16[48,128]{1,0:T(8,128)(2,1)S(1)} %get-tuple-element.24), channel_id=1, source_target_pairs={{1,0},{2,1},{3,2},{4,3},{5,4},{6,5},{7,6},{8,7},{9,8},{10,9},{11,1... | collective-permute-start | bytes 36872 | tf_op jit(solution)/shard_map/ppermute | solution.py:283
  2.7 5.9 %collective-permute-start = (bf16[48,128]{1,0:T(8,128)(2,1)S(1)}, bf16[48,128]{1,0:T(8,128)(2,1)S(1)}, u32[]{:S(2)}, u32[]{:S(2)}) collective-permute-start(bf16[48,128]{1,0:T(8,128)(2,1)S(1)} %get-tuple-element.25), channel_id=1, source_target_pairs={{0,1},{1,2},{2,3},{3,4},{4,5},{5,6},{6,7},{7,8},{8,9},{9,10},{10,1... | collective-permute-start | bytes 36872 | tf_op jit(solution)/shard_map/ppermute | solution.py:280
  7.3 47.8 %copy-start = (bf16[4,768,768]{2,1,0:T(8,128)(2,1)S(1)}, bf16[4,768,768]{2,1,0:T(8,128)(2,1)}, u32[]{:S(2)}) copy-start(bf16[4,768,768]{2,1,0:T(8,128)(2,1)} %proj_ref.5) | copy-start | bytes 14155780
  13.4 13.4 %collective-permute-start.2 = (bf16[48,768]{1,0:T(8,128)(2,1)S(1)}, bf16[48,768]{1,0:T(8,128)(2,1)S(1)}, u32[]{:S(2)}, u32[]{:S(2)}) collective-permute-start(bf16[48,768]{1,0:T(8,128)(2,1)S(1)} %get-tuple-element.13.norm_ref), channel_id=1, source_target_pairs={{0,4},{1,5},{2,6},{3,7},{4,0},{5,1},{6,2},{7,3},{8,12},{9,13},{10,... | collective-permute-start | bytes 221192 | tf_op jit(solution)/shard_map/ppermute | solution.py:307
  26.8 13.4 %collective-permute-start.6 = (bf16[96,768]{1,0:T(8,128)(2,1)S(1)}, bf16[96,768]{1,0:T(8,128)(2,1)S(1)}, u32[]{:S(2)}, u32[]{:S(2)}) collective-permute-start(bf16[96,768]{1,0:T(8,128)(2,1)S(1)} %constant_dynamic-update-slice_fusion.own_ref), channel_id=1, source_target_pairs={{0,2},{1,3},{2,0},{3,1},{4,6},{5,7},{6,4},{7,5},{8,10},{9,11},{10,... | collective-permute-start | bytes 442376 | tf_op jit(solution)/shard_map/ppermute | solution.py:310
  26.8 13.4 %collective-permute-start.5 = (bf16[96,768]{1,0:T(8,128)(2,1)S(1)}, bf16[96,768]{1,0:T(8,128)(2,1)S(1)}, u32[]{:S(2)}, u32[]{:S(2)}) collective-permute-start(bf16[96,768]{1,0:T(8,128)(2,1)S(1)} %constant_dynamic-update-slice_fusion.own_ref), channel_id=1, source_target_pairs={{0,3},{1,0},{2,1},{3,2},{4,7},{5,4},{6,5},{7,6},{8,11},{9,8},{10,9... | collective-permute-start | bytes 442376 | tf_op jit(solution)/shard_map/ppermute | solution.py:310
  27.2 13.0 %collective-permute-start.4 = (bf16[96,768]{1,0:T(8,128)(2,1)S(1)}, bf16[96,768]{1,0:T(8,128)(2,1)S(1)}, u32[]{:S(2)}, u32[]{:S(2)}) collective-permute-start(bf16[96,768]{1,0:T(8,128)(2,1)S(1)} %constant_dynamic-update-slice_fusion.own_ref), channel_id=1, source_target_pairs={{0,1},{1,2},{2,3},{3,0},{4,5},{5,6},{6,7},{7,4},{8,9},{9,10},{10,1... | collective-permute-start | bytes 442376 | tf_op jit(solution)/shard_map/ppermute | solution.py:310
  28.9 11.3 %collective-permute-start.3 = (bf16[48,768]{1,0:T(8,128)(2,1)S(1)}, bf16[48,768]{1,0:T(8,128)(2,1)S(1)}, u32[]{:S(2)}, u32[]{:S(2)}) collective-permute-start(bf16[48,768]{1,0:T(8,128)(2,1)S(1)} %get-tuple-element.13.norm_ref), channel_id=1, source_target_pairs={{0,32},{1,48},{2,0},{3,16},{4,96},{5,112},{6,64},{7,80},{8,40},{9,... | collective-permute-start | bytes 221192 | tf_op jit(solution)/shard_map/ppermute | solution.py:306
  55.1 3.1 %collective-permute-start.7 = (bf16[8,48,768]{2,1,0:T(8,128)(2,1)S(1)}, bf16[8,48,768]{2,1,0:T(8,128)(2,1)S(1)}, u32[]{:S(2)}, u32[]{:S(2)}) collective-permute-start(bf16[8,48,768]{2,1,0:T(8,128)(2,1)S(1)} %all_to_all.10.blocks_ref), channel_id=1, source_target_pairs={{0,8},{8,0},{16,24},{24,16},{32,40},{40,32},{48,56},{56,48},{64,72... | collective-permute-start | bytes 1769480 | tf_op jit(solution)/shard_map/ppermute | solution.py:321
  55.1 3.7 %copy-start.4 = (bf16[16,384,768]{2,1,0:T(8,128)(2,1)S(1)}, bf16[16,384,768]{2,1,0:T(8,128)(2,1)}, u32[]{:S(2)}) copy-start(bf16[16,384,768]{2,1,0:T(8,128)(2,1)} %bias_ref.1) | copy-start | bytes 28311556
  68.7 17.6 %copy-start.1 = (bf16[768,768]{1,0:T(8,128)(2,1)S(1)}, bf16[768,768]{1,0:T(8,128)(2,1)}, u32[]{:S(2)}) copy-start(bf16[768,768]{1,0:T(8,128)(2,1)} %output_ref.1) | copy-start | bytes 3538948
  68.7 17.5 %copy-start.2 = (bf16[768,128]{1,0:T(8,128)(2,1)S(1)}, bf16[768,128]{1,0:T(8,128)(2,1)}, u32[]{:S(2)}) copy-start(bf16[768,128]{1,0:T(8,128)(2,1)} %back_ref.1) | copy-start | bytes 589828

commit v6 on v4

--- a/solution.py
+++ b/solution.py
@@ -143,21 +143,10 @@
     norm_ref[...] = layer_norm(single).astype(BF16)
 
 
-def query_step(
-    own_ref, after_ref, before_ref, far_ref, norm_ref, proj_hbm, q_ref, gate_ref, proj_ref, sems
-):
-    copies = [
-        pltpu.make_async_copy(proj_hbm.at[3 * i], proj_ref.at[i], sems.at[i]) for i in range(2)
-    ]
-    for copy in copies:
-        copy.start()
-    tokens = norm_ref.shape[0]
-    lane = 2 * SLOT
-    rows = jnp.concatenate(
-        [own_ref[...], after_ref[...], before_ref[...], far_ref[...]], axis=0
-    )
-    copies[0].wait()
-    bands = spread(dot(rows, proj_ref[0]).astype(BF16))
+def query_rows(parts, weight, q_ref):
+    tokens = parts[0].shape[0] // 2
+    lane = 2 * SLOT
+    bands = spread(dot(jnp.concatenate(parts, axis=0), weight).astype(BF16))
     ring = lax.axis_size("col") // 2
     me = lax.axis_index("col")
     high, low = me // ring, me % ring
@@ -170,12 +159,6 @@
                 block = band[first : first + tokens].astype(BF16)
                 q_ref[2 * g, at, :] = block[:, :lane]
                 q_ref[2 * g + 1, at, :] = block[:, lane:]
-    copies[1].wait()
-    gates = jax.nn.sigmoid(dot(norm_ref[...], proj_ref[1]))
-    top = gates.astype(BF16)
-    rest = (gates - top.astype(F32)).astype(BF16)
-    for g, (a, b) in enumerate(zip(spread(top), spread(rest))):
-        gate_ref[:, g * BAND : (g + 1) * BAND] = a + b
 
 
 def key_rows(blocks_ref, weight, k_ref):
@@ -190,16 +173,31 @@
     store_pairs(v_ref, [jnp.where(mass, 1.0, band) for band in bands])
 
 
-def near_step(blocks_ref, proj_hbm, k_ref, v_ref, proj_ref, sems):
+def project_step(
+    own_ref, after_ref, before_ref, far_ref, norm_ref, blocks_ref, proj_hbm, q_ref, gate_ref,
+    k_ref, v_ref, key_ref, edge_ref, sems,
+):
+    targets = (edge_ref.at[0], key_ref.at[0], key_ref.at[1], edge_ref.at[1])
     copies = [
-        pltpu.make_async_copy(proj_hbm.at[1 + i], proj_ref.at[i], sems.at[i]) for i in range(2)
+        pltpu.make_async_copy(proj_hbm.at[i], target, sems.at[i])
+        for i, target in enumerate(targets)
     ]
     for copy in copies:
         copy.start()
     copies[0].wait()
-    key_rows(blocks_ref, proj_ref[0], k_ref)
+    query_rows(
+        [own_ref[...], after_ref[...], before_ref[...], far_ref[...]], edge_ref[0], q_ref
+    )
     copies[1].wait()
-    value_rows(blocks_ref, proj_ref[1], v_ref)
+    key_rows(blocks_ref, key_ref[0], k_ref)
+    copies[2].wait()
+    value_rows(blocks_ref, key_ref[1], v_ref)
+    copies[3].wait()
+    gates = jax.nn.sigmoid(dot(norm_ref[...], edge_ref[1]))
+    top = gates.astype(BF16)
+    rest = (gates - top.astype(F32)).astype(BF16)
+    for g, (a, b) in enumerate(zip(spread(top), spread(rest))):
+        gate_ref[:, g * BAND : (g + 1) * BAND] = a + b
 
 
 def token_step(
@@ -229,7 +227,7 @@
         query = q_ref[pair]
         key = jnp.concatenate([k_ref[pair], other_k[pair]], axis=0)
         value = jnp.concatenate([v_ref[pair], other_v[pair]], axis=0)
-        result = jnp.zeros((count, lane), F32)
+        both = []
         for a in range(2):
             head = 2 * pair + a
             mine = jnp.where(at // SLOT == a, query, jnp.zeros_like(query))
@@ -238,18 +236,16 @@
             )
             scores = dot(mine, key, ((1,), (1,))) * factor + bias.astype(F32)
             top = jnp.max(scores, axis=-1, keepdims=True)
-            mixed = dot(jnp.exp(scores - top).astype(BF16), value)
-            base = a * SLOT + HEAD_DIM
-            mass = mixed[:, base : base + 1]
-            level = top + jnp.log(mass)
-            high = level.astype(BF16).astype(F32)
-            middle = (level - high).astype(BF16).astype(F32)
-            low = level - high - middle
-            part = mixed / mass
-            part = jnp.where(at == base, high, part)
-            part = jnp.where(at == base + 1, middle, part)
-            part = jnp.where(at == base + 2, low, part)
-            result = jnp.where(at // SLOT == a, part, result)
+            both.append((dot(jnp.exp(scores - top).astype(BF16), value), top))
+        result = jnp.where(at < SLOT, both[0][0], both[1][0])
+        top = jnp.where(at < SLOT, both[0][1], both[1][1])
+        place = at % SLOT - HEAD_DIM
+        rest = result - result.astype(BF16).astype(F32)
+        result = jnp.where(place == 1, pltpu.roll(rest, 1, 1), result)
+        for piece in range(3):
+            part = top.astype(BF16).astype(F32)
+            result = jnp.where(place == 2 + piece, part, result)
+            top = top - part
         part_ref[:, pair * lane : (pair + 1) * lane] = result.astype(BF16)
 
 
@@ -260,25 +256,23 @@
     lane = 2 * SLOT
     shares, tokens, _ = part_ref.shape
     here, there = lanes((lane, lane), 0), lanes((lane, lane), 1)
-    level_of = (
-        (here // SLOT == there // SLOT)
-        & (here % SLOT >= HEAD_DIM)
-        & (here % SLOT < HEAD_DIM + 3)
-    ).astype(BF16)
+    same, place = here // SLOT == there // SLOT, here % SLOT - HEAD_DIM
+    mass_of = (same & (place >= 0) & (place < 2)).astype(BF16)
+    top_of = (same & (place >= 2) & (place < 5)).astype(BF16)
     gated = []
     for p in range(PAIRS):
         span = slice(p * lane, (p + 1) * lane)
         parts = [part_ref[c, :, span] for c in range(shares)]
-        levels = [dot(part, level_of) for part in parts]
-        top = levels[0]
-        for level in levels[1:]:
-            top = jnp.maximum(top, level)
-        mass = jnp.zeros((tokens, lane), F32)
+        tops = [dot(part, top_of) for part in parts]
+        most = tops[0]
+        for top in tops[1:]:
+            most = jnp.maximum(most, top)
         mix = jnp.zeros((tokens, lane), F32)
-        for part, level in zip(parts, levels):
-            weight = jnp.exp(level - top)
-            mass = mass + weight
-            mix = mix + weight * part.astype(F32)
+        for part, top in zip(parts, tops):
+            mix = mix + jnp.exp(top - most) * part.astype(F32)
+        high = mix.astype(BF16)
+        low = (mix - high.astype(F32)).astype(BF16)
+        mass = dot(high, mass_of) + dot(low, mass_of)
         gated.append((mix / mass * gate_ref[:, span]).astype(BF16))
     gated = [jnp.concatenate(gated[g : g + 2], axis=1) for g in range(0, PAIRS, 2)]
     update = dot(gather_lanes(gated).astype(BF16), output_ref[...])
@@ -363,26 +357,20 @@
     q_count, half = cols * tokens, rows * tokens // 2
     lane = 2 * SLOT
     in_vmem, in_hbm = (pl.BlockSpec(memory_space=space) for space in (pltpu.VMEM, pltpu.HBM))
-    queries, gates = call(
-        query_step,
-        (shape((PAIRS, q_count, lane), BF16), shape((tokens, wide), F32)),
-        MOST,
-        SMALL,
-        in_specs=[in_vmem] * 5 + [in_hbm],
-        scratch_shapes=[pltpu.VMEM((2, depth, depth), BF16), pltpu.SemaphoreType.DMA((2,))],
-    )(own, *along, norm, token_proj)
-    near_k, near_v, key_weights = call(
-        near_step,
+    queries, gates, near_k, near_v, key_weights = call(
+        project_step,
         (
+            shape((PAIRS, q_count, lane), BF16),
+            shape((tokens, wide), F32),
             shape((PAIRS, half, lane), BF16),
             shape((PAIRS, half, lane), BF16),
             shape((2, depth, depth), BF16),
         ),
         MOST,
         SMALL,
-        in_specs=[in_vmem, in_hbm],
-        scratch_shapes=[pltpu.SemaphoreType.DMA((2,))],
-    )(near, token_proj)
+        in_specs=[in_vmem] * 6 + [in_hbm],
+        scratch_shapes=[pltpu.VMEM((2, depth, depth), BF16), pltpu.SemaphoreType.DMA((4,))],
+    )(own, *along, norm, near, token_proj)
     parts = call(
         token_step,
         shape((q_count, wide), BF16),

time: 84.9 us -> 81.9 us (0.965)
  starting transfers between devices: 29.9 us -> 24.5 us
  waiting for transfers between devices: 8.92 us -> 12.6 us
  blocking collectives: 19.1 us -> 18.2 us
  Pallas kernels: 23 us -> 22.1 us
    ppermute x1, starting transfers between devices: 11 us -> 4.54 us  [per_device(): lax.ppermute(norm, 'col', [(i, (i + ring) % cols) for i in range(cols)])]
    ppermute x1, waiting for transfers between devices: 0.01 us -> 3.09 us  [per_device(): lax.ppermute(atom_state[:REACH], BOTH, [(i + 1, i) for i in range(ends)])]
    ppermute x3, starting transfers between devices: 3.67 us -> 5.25 us  [per_device(): lax.ppermute(own, 'col', [(i, i // ring * ring + (i + step) % ring) for i...]
    ppermute x3, waiting for transfers between devices: 5.48 us -> 6.87 us  [per_device(): lax.ppermute(own, 'col', [(i, i // ring * ring + (i + step) % ring) for i...]
    pallas_call x1, Pallas kernels: 10.4 us -> 9.39 us  [per_device(): call(token_step, shape((q_count, wide), BF16), MOST, (6000000000, 1400000...]
    pallas_call x1, Pallas kernels: 2.3 us -> 3.28 us  [per_device(): call(last_step, (shape((count, width), BF16), shape((tokens, depth), BF16...]
    all_to_all x1, blocking collectives: 19.1 us -> 18.2 us  [per_device(): parts = lax.all_to_all(parts.reshape(cols, tokens, wide), 'col', 0, 0)]
    pallas_call x2 -> x1, Pallas kernels: 5.56 us -> 4.7 us  [per_device(): call(project_step, (shape((PAIRS, q_count, lane), BF16), shape((tokens, w...]
  transfers between devices with their start and end apart: 9 -> 9, of which waited for: 5 -> 5; matrix products, arithmetic and copies ran while one was open for 1% -> 1% of each run, Pallas kernels for 7% -> 6%
where the time goes in v6:
time: 81.9 us; the launch traced here: 81 us
  starting transfers between devices  24.5 us (30%)
  Pallas kernels  22.1 us (27%)
  blocking collectives  18.2 us (22%)
  waiting for transfers between devices  12.6 us (15%)
  local copies, waits for them, and re-layouts  1.66 us (2%)
  other arithmetic  1.17 us (1%)
    all_to_all x1, blocking collectives, per_device(): parts = lax.all_to_all(parts.reshape(cols, tokens, wide), 'col', 0, 0)  18.2 us
    pallas_call x1, Pallas kernels, per_device(): call(token_step, shape((q_count, wide), BF16), MOST, (6000000000, 1400000...  9.39 us
    ppermute x3, waiting for transfers between devices, per_device(): lax.ppermute(own, 'col', [(i, i // ring * ring + (i + step) % ring) for i...  6.87 us
    all_to_all x1, starting transfers between devices, per_device(): lax.all_to_all(jnp.broadcast_to(turned[None], (rows // 2, tokens, depth))...  6.31 us
    ppermute x3, starting transfers between devices, per_device(): lax.ppermute(own, 'col', [(i, i // ring * ring + (i + step) % ring) for i...  5.25 us
    pallas_call x1, Pallas kernels, per_device(): call(atom_step, (shape((count, width), F32), shape((tokens, depth), F32),...  4.75 us
    pallas_call x1, Pallas kernels, per_device(): call(project_step, (shape((PAIRS, q_count, lane), BF16), shape((tokens, w...  4.7 us
    ppermute x1, starting transfers between devices, per_device(): lax.ppermute(norm, 'col', [(i, (i + ring) % cols) for i in range(cols)])  4.54 us
  transfers between devices with their start and end apart: 9, of which 5 were waited for; matrix products, arithmetic and copies ran while one was open for 1% of the time, Pallas kernels for 6%

profile of v6, /device:TPU:0, one launch (start us, length us, event | category | flops | bytes accessed | tf_op | source)
XLA Modules:
  0.0 81.0 jit_solution(3479192655958029593)
XLA Ops:
  0.7 0.8 fusion
  1.4 3.9 %collective-permute-start = (bf16[48,128]{1,0:T(8,128)(2,1)S(1)}, bf16[48,128]{1,0:T(8,128)(2,1)S(1)}, u32[]{:S(2)}, u32[]{:S(2)}) collective-permute-start(bf16[48,128]{1,0:T(8,128)(2,1)S(1)} %get-tuple-element.31), channel_id=1, source_target_pairs={{0,1},{1,2},{2,3},{3,4},{4,5},{5,6},{6,7},{7,8},{8,9},{9,10},{10,1... | collective-permute-start | bytes 36872 | tf_op jit(solution)/shard_map/ppermute | solution.py:314
  5.3 1.3 %collective-permute-start.1 = (bf16[48,128]{1,0:T(8,128)(2,1)S(1)}, bf16[48,128]{1,0:T(8,128)(2,1)S(1)}, u32[]{:S(2)}, u32[]{:S(2)}) collective-permute-start(bf16[48,128]{1,0:T(8,128)(2,1)S(1)} %get-tuple-element.30), channel_id=1, source_target_pairs={{1,0},{2,1},{3,2},{4,3},{5,4},{6,5},{7,6},{8,7},{9,8},{10,9},{11,1... | collective-permute-start | bytes 36872 | tf_op jit(solution)/shard_map/ppermute | solution.py:317
  6.6 1.1 %pad_maximum_fusion.narrow_ref = bf16[2560,128]{1,0:T(8,128)(2,1)S(1)} fusion(bf16[128,128]{1,0:T(8,128)(2,1)} %param.17, bf16[512,128]{1,0:T(8,128)(2,1)} %bitcast.5, bf16[1536,128]{1,0:T(8,128)(2,1)} %bitcast.4, bf16[384,128]{1,0:T(8,128)(2,1)} %param.11), kind=kLoop, calls=%fused_computation | loop fusion | flops 2621440 | bytes 1310720 | tf_op jit(solution)/shard_map/concatenate | solution.py:318
  7.8 3.1 %collective-permute-done.1.right_ref = bf16[48,128]{1,0:T(8,128)(2,1)S(1)} collective-permute-done((bf16[48,128]{1,0:T(8,128)(2,1)S(1)}, bf16[48,128]{1,0:T(8,128)(2,1)S(1)}, u32[]{:S(2)}, u32[]{:S(2)}) %collective-permute-start.1) | collective-permute-done | bytes 12320 | tf_op jit(solution)/shard_map/ppermute | solution.py:317
  10.9 4.7 %shard_map.122 = (f32[384,128]{1,0:T(8,128)S(1)}, f32[48,768]{1,0:T(8,128)S(1)}, bf16[48,768]{1,0:T(8,128)(2,1)S(1)}) custom-call(bf16[48,128]{1,0:T(8,128)(2,1)S(1)} %collective-permute-done.left_ref, bf16[48,128]{1,0:T(8,128)(2,1)S(1)} %collective-permute-done.1.right_ref, bf16[2560,128]{1,0:T(8,128)(2,1)S(1)} %pad_maximum_fusion.narrow_ref, ...), custom_call_target="tpu_custom_call" | custom-call | flops 400000000 | bytes 2000000 | tf_op jit(solution)/shard_map/pallas_call | solution.py:324
  15.7 4.5 %collective-permute-start.3 = (bf16[48,768]{1,0:T(8,128)(2,1)S(1)}, bf16[48,768]{1,0:T(8,128)(2,1)S(1)}, u32[]{:S(2)}, u32[]{:S(2)}) collective-permute-start(bf16[48,768]{1,0:T(8,128)(2,1)S(1)} %get-tuple-element.16.norm_ref), channel_id=1, source_target_pairs={{0,4},{1,5},{2,6},{3,7},{4,0},{5,1},{6,2},{7,3},{8,12},{9,13},{10,... | collective-permute-start | bytes 221192 | tf_op jit(solution)/shard_map/ppermute | solution.py:341
  20.2 3.2 %collective-permute-start.2 = (bf16[48,768]{1,0:T(8,128)(2,1)S(1)}, bf16[48,768]{1,0:T(8,128)(2,1)S(1)}, u32[]{:S(2)}, u32[]{:S(2)}) collective-permute-start(bf16[48,768]{1,0:T(8,128)(2,1)S(1)} %get-tuple-element.16.norm_ref), channel_id=1, source_target_pairs={{0,32},{1,48},{2,0},{3,16},{4,96},{5,112},{6,64},{7,80},{8,40},{9,... | collective-permute-start | bytes 221192 | tf_op jit(solution)/shard_map/ppermute | solution.py:340
  23.4 2.6 %collective-permute-done.2 = bf16[48,768]{1,0:T(8,128)(2,1)S(1)} collective-permute-done((bf16[48,768]{1,0:T(8,128)(2,1)S(1)}, bf16[48,768]{1,0:T(8,128)(2,1)S(1)}, u32[]{:S(2)}, u32[]{:S(2)}) %collective-permute-start.2) | collective-permute-done | bytes 73760 | tf_op jit(solution)/shard_map/ppermute | solution.py:340
  26.1 0.9 %broadcast_in_dim.2 = bf16[8,48,768]{2,1,0:T(8,128)(2,1)} broadcast(bf16[48,768]{1,0:T(8,128)(2,1)S(1)} %collective-permute-done.2), dimensions={1,2} | broadcast | bytes 663552 | tf_op jit(solution)/shard_map/broadcast_in_dim | solution.py:346
  26.9 6.3 %all-to-all-start = ((bf16[8,48,768]{2,1,0:T(8,128)(2,1)}), bf16[8,48,768]{2,1,0:T(8,128)(2,1)S(1)}, u32[]{:S(2)}, u32[]{:S(2)}) async-start(bf16[8,48,768]{2,1,0:T(8,128)(2,1)} %broadcast_in_dim.2), calls=%async_computation | async-start | bytes 1179648 | tf_op jit(solution)/shard_map/all_to_all | solution.py:345
  33.3 0.3 collective-permute-start.4
  33.5 3.6 %collective-permute-start.5 = (bf16[96,768]{1,0:T(8,128)(2,1)S(1)}, bf16[96,768]{1,0:T(8,128)(2,1)S(1)}, u32[]{:S(2)}, u32[]{:S(2)}) collective-permute-start(bf16[96,768]{1,0:T(8,128)(2,1)S(1)} %pad_maximum_fusion.2.own_ref), channel_id=1, source_target_pairs={{0,3},{1,0},{2,1},{3,2},{4,7},{5,4},{6,5},{7,6},{8,11},{9,8},{10,9... | collective-permute-start | bytes 442376 | tf_op jit(solution)/shard_map/ppermute | solution.py:350
  37.1 1.4 %collective-permute-start.6 = (bf16[96,768]{1,0:T(8,128)(2,1)S(1)}, bf16[96,768]{1,0:T(8,128)(2,1)S(1)}, u32[]{:S(2)}, u32[]{:S(2)}) collective-permute-start(bf16[96,768]{1,0:T(8,128)(2,1)S(1)} %pad_maximum_fusion.2.own_ref), channel_id=1, source_target_pairs={{0,2},{1,3},{2,0},{3,1},{4,6},{5,7},{6,4},{7,5},{8,10},{9,11},{10,... | collective-permute-start | bytes 442376 | tf_op jit(solution)/shard_map/ppermute | solution.py:350
  38.5 2.5 %collective-permute-done.4.after_ref = bf16[96,768]{1,0:T(8,128)(2,1)S(1)} collective-permute-done((bf16[96,768]{1,0:T(8,128)(2,1)S(1)}, bf16[96,768]{1,0:T(8,128)(2,1)S(1)}, u32[]{:S(2)}, u32[]{:S(2)}) %collective-permute-start.4) | collective-permute-done | bytes 147488 | tf_op jit(solution)/shard_map/ppermute | solution.py:350
  41.0 2.5 %collective-permute-done.5.before_ref = bf16[96,768]{1,0:T(8,128)(2,1)S(1)} collective-permute-done((bf16[96,768]{1,0:T(8,128)(2,1)S(1)}, bf16[96,768]{1,0:T(8,128)(2,1)S(1)}, u32[]{:S(2)}, u32[]{:S(2)}) %collective-permute-start.5) | collective-permute-done | bytes 147488 | tf_op jit(solution)/shard_map/ppermute | solution.py:350
  43.5 1.8 %collective-permute-done.6.far_ref = bf16[96,768]{1,0:T(8,128)(2,1)S(1)} collective-permute-done((bf16[96,768]{1,0:T(8,128)(2,1)S(1)}, bf16[96,768]{1,0:T(8,128)(2,1)S(1)}, u32[]{:S(2)}, u32[]{:S(2)}) %collective-permute-start.6) | collective-permute-done | bytes 147488 | tf_op jit(solution)/shard_map/ppermute | solution.py:350
  45.4 0.0 collective-permute-start.7
  45.4 4.7 %shard_map.123 = (bf16[8,384,128]{2,1,0:T(8,128)(2,1)S(1)}, f32[48,1024]{1,0:T(8,128)S(1)}, bf16[8,384,128]{2,1,0:T(8,128)(2,1)S(1)}, bf16[8,384,128]{2,1,0:T(8,128)(2,1)S(1)}, bf16[2,768,768]{2,1,0:T(8,128)(2,1)S(1)}) custom-call(bf16[96,768]{1,0:T(8,128)(2,1)S(1)} %pad_maximum_fusion.2.own_ref, bf16[96,768]{1,0:T(8,128)(2,1)S(1)} %collective-permute-done.4.after_ref, ...), custom_call_target="tpu_custom_call" | custom-call | flops 1000000 | bytes 100000 | tf_op jit(solution)/shard_map/pallas_call | solution.py:360
  50.1 9.4 %shard_map.124 = bf16[384,1024]{1,0:T(8,128)(2,1)S(1)} custom-call(bf16[8,384,128]{2,1,0:T(8,128)(2,1)S(1)} %get-tuple-element.23.q_ref, bf16[8,384,128]{2,1,0:T(8,128)(2,1)S(1)} %get-tuple-element.24.k_ref, bf16[8,384,128]{2,1,0:T(8,128)(2,1)S(1)} %get-tuple-element.25.v_ref, bf16[8,48,768]{2,1,0:T(8,128)(2,1)S(1)} %collective-permute-done.7.blocks_ref, ...), custom_call_target="tpu_custom_call" | custom-call | flops 6000000000 | bytes 14000000 | tf_op jit(solution)/shard_map/pallas_call | solution.py:374
  59.5 0.0 copy-start
  59.5 0.0 copy-start.1
  59.5 18.2 %all_to_all.10.part_ref = bf16[8,48,1024]{2,1,0:T(8,128)(2,1)S(1)} all-to-all(bf16[8,48,1024]{2,1,0:T(8,128)(2,1)S(1)} %bitcast.3), channel_id=1, replica_groups=mesh['row'=16,'col'=8] {'col'}, dimensions={0} | all-to-all | bytes 1572864 | tf_op jit(solution)/shard_map/all_to_all | solution.py:387
  77.7 3.3 %shard_map.125 = (bf16[384,128]{1,0:T(8,128)(2,1)}, bf16[48,768]{1,0:T(8,128)(2,1)}) custom-call(bf16[8,48,1024]{2,1,0:T(8,128)(2,1)S(1)} %all_to_all.10.part_ref, f32[48,1024]{1,0:T(8,128)S(1)} %get-tuple-element.27.gate_ref, f32[48,768]{1,0:T(8,128)S(1)} %get-tuple-element.28.single_ref, f32[384,128]{1,0:T(8,128)S(1)} %get-tuple-element.29.mid_ref, ...), custom_call_target="tpu_custom_call" | custom-call | flops 400000000 | bytes 5000000 | tf_op jit(solution)/shard_map/pallas_call | solution.py:388
  (14 shorter events, 0.1 us)
Async XLA Ops:
  0.6 7.2 %copy-start.4 = (bf16[48,768]{1,0:T(8,128)(2,1)S(1)}, bf16[48,768]{1,0:T(8,128)(2,1)}, u32[]{:S(2)}) copy-start(bf16[48,768]{1,0:T(8,128)(2,1)} %param.12) | copy-start | bytes 221188
  0.6 7.2 %copy-start.3 = (bf16[128,768]{1,0:T(8,128)(2,1)S(1)}, bf16[128,768]{1,0:T(8,128)(2,1)}, u32[]{:S(2)}) copy-start(bf16[128,768]{1,0:T(8,128)(2,1)} %param.18) | copy-start | bytes 589828
  0.7 10.3 %copy-start.2 = (s32[1,384]{1,0:T(1,128)S(1)}, s32[1,384]{1,0:T(1,128)}, u32[]{:S(2)}) copy-start(s32[1,384]{1,0:T(1,128)} %owner_ref.3) | copy-start | bytes 4612
  1.4 6.4 %collective-permute-start = (bf16[48,128]{1,0:T(8,128)(2,1)S(1)}, bf16[48,128]{1,0:T(8,128)(2,1)S(1)}, u32[]{:S(2)}, u32[]{:S(2)}) collective-permute-start(bf16[48,128]{1,0:T(8,128)(2,1)S(1)} %get-tuple-element.31), channel_id=1, source_target_pairs={{0,1},{1,2},{2,3},{3,4},{4,5},{5,6},{6,7},{7,8},{8,9},{9,10},{10,1... | collective-permute-start | bytes 36872 | tf_op jit(solution)/shard_map/ppermute | solution.py:314
  5.3 5.6 %collective-permute-start.1 = (bf16[48,128]{1,0:T(8,128)(2,1)S(1)}, bf16[48,128]{1,0:T(8,128)(2,1)S(1)}, u32[]{:S(2)}, u32[]{:S(2)}) collective-permute-start(bf16[48,128]{1,0:T(8,128)(2,1)S(1)} %get-tuple-element.30), channel_id=1, source_target_pairs={{1,0},{2,1},{3,2},{4,3},{5,4},{6,5},{7,6},{8,7},{9,8},{10,9},{11,1... | collective-permute-start | bytes 36872 | tf_op jit(solution)/shard_map/ppermute | solution.py:317
  15.7 7.7 %collective-permute-start.3 = (bf16[48,768]{1,0:T(8,128)(2,1)S(1)}, bf16[48,768]{1,0:T(8,128)(2,1)S(1)}, u32[]{:S(2)}, u32[]{:S(2)}) collective-permute-start(bf16[48,768]{1,0:T(8,128)(2,1)S(1)} %get-tuple-element.16.norm_ref), channel_id=1, source_target_pairs={{0,4},{1,5},{2,6},{3,7},{4,0},{5,1},{6,2},{7,3},{8,12},{9,13},{10,... | collective-permute-start | bytes 221192 | tf_op jit(solution)/shard_map/ppermute | solution.py:341
  20.2 5.9 %collective-permute-start.2 = (bf16[48,768]{1,0:T(8,128)(2,1)S(1)}, bf16[48,768]{1,0:T(8,128)(2,1)S(1)}, u32[]{:S(2)}, u32[]{:S(2)}) collective-permute-start(bf16[48,768]{1,0:T(8,128)(2,1)S(1)} %get-tuple-element.16.norm_ref), channel_id=1, source_target_pairs={{0,32},{1,48},{2,0},{3,16},{4,96},{5,112},{6,64},{7,80},{8,40},{9,... | collective-permute-start | bytes 221192 | tf_op jit(solution)/shard_map/ppermute | solution.py:340
  26.9 18.4 %all-to-all-start = ((bf16[8,48,768]{2,1,0:T(8,128)(2,1)}), bf16[8,48,768]{2,1,0:T(8,128)(2,1)S(1)}, u32[]{:S(2)}, u32[]{:S(2)}) async-start(bf16[8,48,768]{2,1,0:T(8,128)(2,1)} %broadcast_in_dim.2), calls=%async_computation | async-start | bytes 1179648 | tf_op jit(solution)/shard_map/all_to_all | solution.py:345
  33.3 7.8 %collective-permute-start.4 = (bf16[96,768]{1,0:T(8,128)(2,1)S(1)}, bf16[96,768]{1,0:T(8,128)(2,1)S(1)}, u32[]{:S(2)}, u32[]{:S(2)}) collective-permute-start(bf16[96,768]{1,0:T(8,128)(2,1)S(1)} %pad_maximum_fusion.2.own_ref), channel_id=1, source_target_pairs={{0,1},{1,2},{2,3},{3,0},{4,5},{5,6},{6,7},{7,4},{8,9},{9,10},{10,1... | collective-permute-start | bytes 442376 | tf_op jit(solution)/shard_map/ppermute | solution.py:350
  33.5 10.0 %collective-permute-start.5 = (bf16[96,768]{1,0:T(8,128)(2,1)S(1)}, bf16[96,768]{1,0:T(8,128)(2,1)S(1)}, u32[]{:S(2)}, u32[]{:S(2)}) collective-permute-start(bf16[96,768]{1,0:T(8,128)(2,1)S(1)} %pad_maximum_fusion.2.own_ref), channel_id=1, source_target_pairs={{0,3},{1,0},{2,1},{3,2},{4,7},{5,4},{6,5},{7,6},{8,11},{9,8},{10,9... | collective-permute-start | bytes 442376 | tf_op jit(solution)/shard_map/ppermute | solution.py:350
  37.1 8.3 %collective-permute-start.6 = (bf16[96,768]{1,0:T(8,128)(2,1)S(1)}, bf16[96,768]{1,0:T(8,128)(2,1)S(1)}, u32[]{:S(2)}, u32[]{:S(2)}) collective-permute-start(bf16[96,768]{1,0:T(8,128)(2,1)S(1)} %pad_maximum_fusion.2.own_ref), channel_id=1, source_target_pairs={{0,2},{1,3},{2,0},{3,1},{4,6},{5,7},{6,4},{7,5},{8,10},{9,11},{10,... | collective-permute-start | bytes 442376 | tf_op jit(solution)/shard_map/ppermute | solution.py:350
  45.4 4.7 %collective-permute-start.7 = (bf16[8,48,768]{2,1,0:T(8,128)(2,1)S(1)}, bf16[8,48,768]{2,1,0:T(8,128)(2,1)S(1)}, u32[]{:S(2)}, u32[]{:S(2)}) collective-permute-start(bf16[8,48,768]{2,1,0:T(8,128)(2,1)S(1)} %all-to-all-done.blocks_ref), channel_id=1, source_target_pairs={{0,8},{8,0},{16,24},{24,16},{32,40},{40,32},{48,56},{56,48},{64,72... | collective-permute-start | bytes 1769480 | tf_op jit(solution)/shard_map/ppermute | solution.py:356
  59.5 18.2 %copy-start = (bf16[768,768]{1,0:T(8,128)(2,1)S(1)}, bf16[768,768]{1,0:T(8,128)(2,1)}, u32[]{:S(2)}) copy-start(bf16[768,768]{1,0:T(8,128)(2,1)} %output_ref.1) | copy-start | bytes 3538948
  59.5 18.2 %copy-start.1 = (bf16[768,128]{1,0:T(8,128)(2,1)S(1)}, bf16[768,128]{1,0:T(8,128)(2,1)}, u32[]{:S(2)}) copy-start(bf16[768,128]{1,0:T(8,128)(2,1)} %back_ref.1) | copy-start | bytes 589828

commit v7 on v6

--- a/solution.py
+++ b/solution.py
@@ -15,6 +15,7 @@
 WIN_Q = 32
 WIN_K = 128
 REACH = 48
+EDGE = 2
 EPSILON = 1e-05
 
 BOTH = ("row", "col")
@@ -79,59 +80,94 @@
         ref[2 * g + 1] = band[:, lane:].astype(BF16)
 
 
+def narrow_parts(narrow_ref, count):
+    width = narrow_ref.shape[1]
+    after = (1 + ATOM_HEADS) * count
+    biases = [narrow_ref.at[(1 + h) * count : (2 + h) * count] for h in range(ATOM_HEADS)]
+    weights = [narrow_ref.at[after + i * width : after + (i + 1) * width] for i in range(5)]
+    return narrow_ref.at[:count], biases, weights
+
+
+def window(start, query, keys, values, gates, biases, bounds=None):
+    width = query.shape[1]
+    head_width = width // ATOM_HEADS
+    head_of = lanes((WIN_Q, width), 1) // head_width
+    stacked = jnp.concatenate(
+        [jnp.where(head_of == h, query, jnp.zeros_like(query)) for h in range(ATOM_HEADS)],
+        axis=0,
+    )
+    scores = dot(stacked, keys, ((1,), (1,))) * (1.0 / math.sqrt(head_width))
+    scores = scores + jnp.concatenate(
+        [bias[start : start + WIN_Q, :] for bias in biases], axis=0
+    ).astype(F32)
+    if bounds is not None:
+        first, total = bounds
+        position = first + (start - REACH) + lanes(scores.shape, 1)
+        scores = jnp.where((position >= 0) & (position < total), scores, -1e30)
+    top = jnp.max(scores, axis=-1, keepdims=True)
+    weights = jnp.exp(scores - top)
+    weights = (weights / jnp.sum(weights, axis=-1, keepdims=True)).astype(BF16)
+    mixed = dot(weights, values)
+    mix = jnp.zeros((WIN_Q, width), F32)
+    for h in range(ATOM_HEADS):
+        mix = jnp.where(head_of == h, mixed[h * WIN_Q : (h + 1) * WIN_Q], mix)
+    return (mix * gates).astype(BF16)
+
+
+def inner_step(narrow_ref, q_ref, k_ref, v_ref, gate_ref, gated_ref):
+    count = q_ref.shape[0]
+    state_ref, biases, weights = narrow_parts(narrow_ref, count)
+    normed = layer_norm(state_ref[...].astype(F32)).astype(BF16)
+    queries = dot(normed, weights[0][...]).astype(BF16)
+    keys = dot(normed, weights[1][...]).astype(BF16)
+    values = dot(normed, weights[2][...]).astype(BF16)
+    gates = jax.nn.sigmoid(dot(normed, weights[3][...]))
+    q_ref[...], k_ref[...], v_ref[...], gate_ref[...] = queries, keys, values, gates
+    for w in range(EDGE, count // WIN_Q - EDGE):
+        start = w * WIN_Q
+        seen = slice(start - REACH, start - REACH + WIN_K)
+        mine = slice(start, start + WIN_Q)
+        gated_ref[start - EDGE * WIN_Q : start - EDGE * WIN_Q + WIN_Q, :] = window(
+            start, queries[mine], keys[seen], values[seen], gates[mine], biases
+        )
+
+
 def atom_step(
-    left_ref, right_ref, narrow_ref, broad_ref, owner_ref, mid_ref, single_ref, norm_ref,
+    left_ref, right_ref, narrow_ref, broad_ref, owner_ref, q_ref, k_ref, v_ref, gate_ref,
+    gated_ref, mid_ref, single_ref, norm_ref,
 ):
     width = narrow_ref.shape[1]
     count = owner_ref.shape[1]
-    state_ref = narrow_ref.at[:count]
-    after = (1 + ATOM_HEADS) * count
-    bias_ref = [narrow_ref.at[(1 + h) * count : (2 + h) * count] for h in range(ATOM_HEADS)]
-    proj_ref = [narrow_ref.at[after + i * width : after + (i + 1) * width] for i in range(5)]
-    output_ref = proj_ref[4]
+    state_ref, biases, weights = narrow_parts(narrow_ref, count)
     pool_ref, input_ref = broad_ref.at[:width], broad_ref.at[width:]
-    windows = count // WIN_Q
     rows, cols = lax.axis_size("row"), lax.axis_size("col")
     first = (lax.axis_index("row") * cols + lax.axis_index("col")) * count
-    total = count * rows * cols
-    state = state_ref[...].astype(F32)
-    extended = jnp.concatenate(
-        [left_ref[...].astype(F32), state, right_ref[...].astype(F32)], axis=0
-    )
-    normed = layer_norm(extended).astype(BF16)
-    keys = dot(normed, proj_ref[1][...]).astype(BF16)
-    values = dot(normed, proj_ref[2][...]).astype(BF16)
-    own = normed[REACH : REACH + count]
-    queries = dot(own, proj_ref[0][...]).astype(BF16)
-    gates = jax.nn.sigmoid(dot(own, proj_ref[3][...]))
-    head_width = width // ATOM_HEADS
-    head_of = lanes((WIN_Q, width), 1) // head_width
-    factor = 1.0 / math.sqrt(head_width)
-    gated = []
-    for w in range(windows):
-        start = w * WIN_Q
-        query = queries[start : start + WIN_Q]
-        stacked = jnp.concatenate(
-            [jnp.where(head_of == h, query, jnp.zeros_like(query)) for h in range(ATOM_HEADS)],
-            axis=0,
-        )
-        scores = dot(stacked, keys[start : start + WIN_K], ((1,), (1,))) * factor
-        scores = scores + jnp.concatenate(
-            [bias_ref[h][start : start + WIN_Q, :] for h in range(ATOM_HEADS)], axis=0
-        ).astype(F32)
-        if start < REACH or start + WIN_K > count + REACH:
-            position = first + (start - REACH) + lanes(scores.shape, 1)
-            scores = jnp.where((position >= 0) & (position < total), scores, -1e30)
-        top = jnp.max(scores, axis=-1, keepdims=True)
-        weights = jnp.exp(scores - top)
-        weights = (weights / jnp.sum(weights, axis=-1, keepdims=True)).astype(BF16)
-        mixed = dot(weights, values[start : start + WIN_K])
-        mix = jnp.zeros((WIN_Q, width), F32)
-        for h in range(ATOM_HEADS):
-            mix = jnp.where(head_of == h, mixed[h * WIN_Q : (h + 1) * WIN_Q], mix)
-        gated.append((mix * gates[start : start + WIN_Q]).astype(BF16))
-    gated = jnp.concatenate(gated, axis=0)
-    mid = state + dot(gated, output_ref[...])
+    bounds = (first, count * rows * cols)
+    beside = jnp.concatenate([left_ref[...], right_ref[...]], axis=0).astype(F32)
+    normed = layer_norm(beside).astype(BF16)
+    keys = dot(normed, weights[1][...]).astype(BF16)
+    values = dot(normed, weights[2][...]).astype(BF16)
+    reach = WIN_K + WIN_Q - REACH
+    ends = (
+        (jnp.concatenate([keys[:REACH], k_ref[:reach, :]], axis=0),
+         jnp.concatenate([values[:REACH], v_ref[:reach, :]], axis=0)),
+        (jnp.concatenate([k_ref[count - reach :, :], keys[REACH:]], axis=0),
+         jnp.concatenate([v_ref[count - reach :, :], values[REACH:]], axis=0)),
+    )
+    outer = []
+    for side in range(2):
+        for w in range(EDGE):
+            start = w * WIN_Q + side * (count - EDGE * WIN_Q)
+            mine = slice(start, start + WIN_Q)
+            seen = slice(w * WIN_Q, w * WIN_Q + WIN_K)
+            outer.append(
+                window(
+                    start, q_ref[mine, :], ends[side][0][seen], ends[side][1][seen],
+                    gate_ref[mine, :], biases, bounds,
+                )
+            )
+    gated = jnp.concatenate(outer[:EDGE] + [gated_ref[...]] + outer[EDGE:], axis=0)
+    mid = state_ref[...].astype(F32) + dot(gated, weights[4][...])
     mid_ref[...] = mid
     lifted = jnp.maximum(dot(mid.astype(BF16), pool_ref[...]), 0.0).astype(BF16)
     tokens = input_ref.shape[0]
@@ -253,28 +289,22 @@
     part_ref, gate_ref, single_ref, mid_ref, owner_ref, output_ref, back_ref, atom_ref,
     token_ref,
 ):
-    lane = 2 * SLOT
     shares, tokens, _ = part_ref.shape
-    here, there = lanes((lane, lane), 0), lanes((lane, lane), 1)
+    here, there = lanes((BAND, BAND), 0), lanes((BAND, BAND), 1)
     same, place = here // SLOT == there // SLOT, here % SLOT - HEAD_DIM
     mass_of = (same & (place >= 0) & (place < 2)).astype(BF16)
     top_of = (same & (place >= 2) & (place < 5)).astype(BF16)
     gated = []
-    for p in range(PAIRS):
-        span = slice(p * lane, (p + 1) * lane)
-        parts = [part_ref[c, :, span] for c in range(shares)]
-        tops = [dot(part, top_of) for part in parts]
-        most = tops[0]
-        for top in tops[1:]:
-            most = jnp.maximum(most, top)
-        mix = jnp.zeros((tokens, lane), F32)
-        for part, top in zip(parts, tops):
-            mix = mix + jnp.exp(top - most) * part.astype(F32)
+    for g in range(HEADS // 4):
+        span = slice(g * BAND, (g + 1) * BAND)
+        parts = jnp.concatenate([part_ref[c, :, span] for c in range(shares)], axis=0)
+        tops = dot(parts, top_of).reshape(shares, tokens, BAND)
+        weights = jnp.exp(tops - jnp.max(tops, axis=0))
+        mix = jnp.sum(weights * parts.astype(F32).reshape(tops.shape), axis=0)
         high = mix.astype(BF16)
         low = (mix - high.astype(F32)).astype(BF16)
         mass = dot(high, mass_of) + dot(low, mass_of)
         gated.append((mix / mass * gate_ref[:, span]).astype(BF16))
-    gated = [jnp.concatenate(gated[g : g + 2], axis=1) for g in range(0, PAIRS, 2)]
     update = dot(gather_lanes(gated).astype(BF16), output_ref[...])
     token_state = (single_ref[...] + update).astype(BF16)
     token_ref[...] = token_state
@@ -321,6 +351,13 @@
         axis=0,
     )
     broad = jnp.concatenate([pool_weight, token_input], axis=0)
+    inner = call(
+        inner_step,
+        tuple(shape((count, width), kind) for kind in (BF16, BF16, BF16, F32))
+        + (shape((count - 2 * EDGE * WIN_Q, width), BF16),),
+        ATOM_MB,
+        (200_000_000, 1_000_000),
+    )(narrow)
     mid, single, norm = call(
         atom_step,
         (
@@ -329,8 +366,8 @@
             shape((tokens, depth), BF16),
         ),
         ATOM_MB,
-        (400_000_000, 2_000_000),
-    )(left, right, narrow, broad, atom_owner)
+        (200_000_000, 2_000_000),
+    )(left, right, narrow, broad, atom_owner, *inner)
     ring = cols // 2
     turn = []
     for r in range(rows):

time: 81.9 us -> 80.2 us (0.979)
  waiting for transfers between devices: 12.6 us -> 11 us
  other arithmetic: 1.17 us -> 2.14 us
    ppermute x1, waiting for transfers between devices: 3.09 us -> 0.01 us  [per_device(): lax.ppermute(atom_state[:REACH], BOTH, [(i + 1, i) for i in range(ends)])]
    ppermute x1, starting transfers between devices: 4.54 us -> 7.44 us  [per_device(): lax.ppermute(norm, 'col', [(i, (i + ring) % cols) for i in range(cols)])]
    pallas_call x0 -> x1, Pallas kernels: none -> 2.77 us  [per_device(): call(inner_step, tuple((shape((count, width), kind) for kind in (BF16, BF...]
    pallas_call x1, Pallas kernels: 4.75 us -> 2.36 us  [per_device(): call(atom_step, (shape((count, width), F32), shape((tokens, depth), F32),...]
    all_to_all x1, starting transfers between devices: 6.31 us -> 4.24 us  [per_device(): lax.all_to_all(jnp.broadcast_to(turned[None], (rows // 2, tokens, depth))...]
    ppermute x3, starting transfers between devices: 5.25 us -> 3.58 us  [per_device(): lax.ppermute(own, 'col', [(i, i // ring * ring + (i + step) % ring) for i...]
    ppermute x1, waiting for transfers between devices: 2.65 us -> 4.22 us  [per_device(): turned = lax.ppermute(norm, BOTH, turn)]
    concatenate x1, other arithmetic: 0.02 us -> 0.98 us  [per_device(): broad = jnp.concatenate([pool_weight, token_input], axis=0)]
  transfers between devices with their start and end apart: 9 -> 9, of which waited for: 5 -> 4; matrix products, arithmetic and copies ran while one was open for 1% -> 3% of each run, Pallas kernels for 6% -> 9%
where the time goes in v7:
time: 80.2 us; the launch traced here: 79.7 us
  starting transfers between devices  23.8 us (30%)
  Pallas kernels  22 us (27%)
  blocking collectives  18.4 us (23%)
  waiting for transfers between devices  11 us (14%)
  other arithmetic  2.14 us (3%)
  local copies, waits for them, and re-layouts  1.6 us (2%)
    all_to_all x1, blocking collectives, per_device(): parts = lax.all_to_all(parts.reshape(cols, tokens, wide), 'col', 0, 0)  18.4 us
    pallas_call x1, Pallas kernels, per_device(): call(token_step, shape((q_count, wide), BF16), MOST, (6000000000, 1400000...  9.38 us
    ppermute x1, starting transfers between devices, per_device(): lax.ppermute(norm, 'col', [(i, (i + ring) % cols) for i in range(cols)])  7.44 us
    ppermute x3, waiting for transfers between devices, per_device(): lax.ppermute(own, 'col', [(i, i // ring * ring + (i + step) % ring) for i...  6.72 us
    pallas_call x1, Pallas kernels, per_device(): call(project_step, (shape((PAIRS, q_count, lane), BF16), shape((tokens, w...  4.7 us
    all_to_all x1, starting transfers between devices, per_device(): lax.all_to_all(jnp.broadcast_to(turned[None], (rows // 2, tokens, depth))...  4.24 us
    ppermute x1, waiting for transfers between devices, per_device(): turned = lax.ppermute(norm, BOTH, turn)  4.22 us
    ppermute x1, starting transfers between devices, per_device(): lax.ppermute(atom_state[count - REACH:], BOTH, [(i, i + 1) for i in range...  4.02 us
  transfers between devices with their start and end apart: 9, of which 4 were waited for; matrix products, arithmetic and copies ran while one was open for 3% of the time, Pallas kernels for 9%

profile of v7, /device:TPU:0, one launch (start us, length us, event | category | flops | bytes accessed | tf_op | source)
XLA Modules:
  0.0 79.7 jit_solution(12377111547588294198)
XLA Ops:
  0.6 0.7 fusion
  1.4 4.0 %collective-permute-start = (bf16[48,128]{1,0:T(8,128)(2,1)S(1)}, bf16[48,128]{1,0:T(8,128)(2,1)S(1)}, u32[]{:S(2)}, u32[]{:S(2)}) collective-permute-start(bf16[48,128]{1,0:T(8,128)(2,1)S(1)} %get-tuple-element.41), channel_id=1, source_target_pairs={{0,1},{1,2},{2,3},{3,4},{4,5},{5,6},{6,7},{7,8},{8,9},{9,10},{10,1... | collective-permute-start | bytes 36872 | tf_op jit(solution)/shard_map/ppermute | solution.py:344
  5.4 1.3 %collective-permute-start.1 = (bf16[48,128]{1,0:T(8,128)(2,1)S(1)}, bf16[48,128]{1,0:T(8,128)(2,1)S(1)}, u32[]{:S(2)}, u32[]{:S(2)}) collective-permute-start(bf16[48,128]{1,0:T(8,128)(2,1)S(1)} %get-tuple-element.40), channel_id=1, source_target_pairs={{1,0},{2,1},{3,2},{4,3},{5,4},{6,5},{7,6},{8,7},{9,8},{10,9},{11,1... | collective-permute-start | bytes 36872 | tf_op jit(solution)/shard_map/ppermute | solution.py:347
  6.7 1.0 %pad_maximum_fusion.1.broad_ref = bf16[176,768]{1,0:T(8,128)(2,1)S(1)} fusion(bf16[48,768]{1,0:T(8,128)(2,1)} %param.12, bf16[128,768]{1,0:T(8,128)(2,1)} %param.18), kind=kLoop, calls=%fused_computation.1 | loop fusion | flops 540672 | bytes 540672 | tf_op jit(solution)/shard_map/concatenate | solution.py:353
  7.7 1.1 %pad_maximum_fusion.narrow_ref = bf16[2560,128]{1,0:T(8,128)(2,1)S(1)} fusion(bf16[128,128]{1,0:T(8,128)(2,1)} %param.17, bf16[512,128]{1,0:T(8,128)(2,1)} %bitcast.5, bf16[1536,128]{1,0:T(8,128)(2,1)} %bitcast.4, bf16[384,128]{1,0:T(8,128)(2,1)} %param.11), kind=kLoop, calls=%fused_computation | loop fusion | flops 2621440 | bytes 1310720 | tf_op jit(solution)/shard_map/concatenate | solution.py:348
  8.8 2.8 %shard_map.122 = (bf16[384,128]{1,0:T(8,128)(2,1)S(1)}, bf16[384,128]{1,0:T(8,128)(2,1)S(1)}, bf16[384,128]{1,0:T(8,128)(2,1)S(1)}, f32[384,128]{1,0:T(8,128)S(1)}, bf16[256,128]{1,0:T(8,128)(2,1)S(1)}) custom-call(bf16[2560,128]{1,0:T(8,128)(2,1)S(1)} %pad_maximum_fusion.narrow_ref), custom_call_target="tpu_custom_call" | custom-call | flops 200000000 | bytes 1000000 | tf_op jit(solution)/shard_map/pallas_call | solution.py:354
  11.6 2.4 %shard_map.123 = (f32[384,128]{1,0:T(8,128)S(1)}, f32[48,768]{1,0:T(8,128)S(1)}, bf16[48,768]{1,0:T(8,128)(2,1)S(1)}) custom-call(bf16[48,128]{1,0:T(8,128)(2,1)S(1)} %collective-permute-done.left_ref, bf16[48,128]{1,0:T(8,128)(2,1)S(1)} %collective-permute-done.1.right_ref, bf16[2560,128]{1,0:T(8,128)(2,1)S(1)} %pad_maximum_fusion.narrow_ref, ...), custom_call_target="tpu_custom_call" | custom-call | flops 200000000 | bytes 2000000 | tf_op jit(solution)/shard_map/pallas_call | solution.py:361
  14.0 7.4 %collective-permute-start.3 = (bf16[48,768]{1,0:T(8,128)(2,1)S(1)}, bf16[48,768]{1,0:T(8,128)(2,1)S(1)}, u32[]{:S(2)}, u32[]{:S(2)}) collective-permute-start(bf16[48,768]{1,0:T(8,128)(2,1)S(1)} %get-tuple-element.26.norm_ref), channel_id=1, source_target_pairs={{0,4},{1,5},{2,6},{3,7},{4,0},{5,1},{6,2},{7,3},{8,12},{9,13},{10,... | collective-permute-start | bytes 221192 | tf_op jit(solution)/shard_map/ppermute | solution.py:378
  21.4 3.2 %collective-permute-start.2 = (bf16[48,768]{1,0:T(8,128)(2,1)S(1)}, bf16[48,768]{1,0:T(8,128)(2,1)S(1)}, u32[]{:S(2)}, u32[]{:S(2)}) collective-permute-start(bf16[48,768]{1,0:T(8,128)(2,1)S(1)} %get-tuple-element.26.norm_ref), channel_id=1, source_target_pairs={{0,32},{1,48},{2,0},{3,16},{4,96},{5,112},{6,64},{7,80},{8,40},{9,... | collective-permute-start | bytes 221192 | tf_op jit(solution)/shard_map/ppermute | solution.py:377
  24.7 4.2 %collective-permute-done.2 = bf16[48,768]{1,0:T(8,128)(2,1)S(1)} collective-permute-done((bf16[48,768]{1,0:T(8,128)(2,1)S(1)}, bf16[48,768]{1,0:T(8,128)(2,1)S(1)}, u32[]{:S(2)}, u32[]{:S(2)}) %collective-permute-start.2) | collective-permute-done | bytes 73760 | tf_op jit(solution)/shard_map/ppermute | solution.py:377
  28.9 0.9 %broadcast_in_dim.2 = bf16[8,48,768]{2,1,0:T(8,128)(2,1)} broadcast(bf16[48,768]{1,0:T(8,128)(2,1)S(1)} %collective-permute-done.2), dimensions={1,2} | broadcast | bytes 663552 | tf_op jit(solution)/shard_map/broadcast_in_dim | solution.py:383
  29.7 4.2 %all-to-all-start = ((bf16[8,48,768]{2,1,0:T(8,128)(2,1)}), bf16[8,48,768]{2,1,0:T(8,128)(2,1)S(1)}, u32[]{:S(2)}, u32[]{:S(2)}) async-start(bf16[8,48,768]{2,1,0:T(8,128)(2,1)} %broadcast_in_dim.2), calls=%async_computation | async-start | bytes 1179648 | tf_op jit(solution)/shard_map/all_to_all | solution.py:382
  34.0 3.2 %collective-permute-start.5 = (bf16[96,768]{1,0:T(8,128)(2,1)S(1)}, bf16[96,768]{1,0:T(8,128)(2,1)S(1)}, u32[]{:S(2)}, u32[]{:S(2)}) collective-permute-start(bf16[96,768]{1,0:T(8,128)(2,1)S(1)} %pad_maximum_fusion.2.own_ref), channel_id=1, source_target_pairs={{0,3},{1,0},{2,1},{3,2},{4,7},{5,4},{6,5},{7,6},{8,11},{9,8},{10,9... | collective-permute-start | bytes 442376 | tf_op jit(solution)/shard_map/ppermute | solution.py:387
  37.2 0.3 collective-permute-start.6
  37.6 3.1 %collective-permute-done.4.after_ref = bf16[96,768]{1,0:T(8,128)(2,1)S(1)} collective-permute-done((bf16[96,768]{1,0:T(8,128)(2,1)S(1)}, bf16[96,768]{1,0:T(8,128)(2,1)S(1)}, u32[]{:S(2)}, u32[]{:S(2)}) %collective-permute-start.4) | collective-permute-done | bytes 147488 | tf_op jit(solution)/shard_map/ppermute | solution.py:387
  40.7 2.1 %collective-permute-done.5.before_ref = bf16[96,768]{1,0:T(8,128)(2,1)S(1)} collective-permute-done((bf16[96,768]{1,0:T(8,128)(2,1)S(1)}, bf16[96,768]{1,0:T(8,128)(2,1)S(1)}, u32[]{:S(2)}, u32[]{:S(2)}) %collective-permute-start.5) | collective-permute-done | bytes 147488 | tf_op jit(solution)/shard_map/ppermute | solution.py:387
  42.8 1.5 %collective-permute-done.6.far_ref = bf16[96,768]{1,0:T(8,128)(2,1)S(1)} collective-permute-done((bf16[96,768]{1,0:T(8,128)(2,1)S(1)}, bf16[96,768]{1,0:T(8,128)(2,1)S(1)}, u32[]{:S(2)}, u32[]{:S(2)}) %collective-permute-start.6) | collective-permute-done | bytes 147488 | tf_op jit(solution)/shard_map/ppermute | solution.py:387
  44.3 0.0 collective-permute-start.7
  44.3 4.7 %shard_map.124 = (bf16[8,384,128]{2,1,0:T(8,128)(2,1)S(1)}, f32[48,1024]{1,0:T(8,128)S(1)}, bf16[8,384,128]{2,1,0:T(8,128)(2,1)S(1)}, bf16[8,384,128]{2,1,0:T(8,128)(2,1)S(1)}, bf16[2,768,768]{2,1,0:T(8,128)(2,1)S(1)}) custom-call(bf16[96,768]{1,0:T(8,128)(2,1)S(1)} %pad_maximum_fusion.2.own_ref, bf16[96,768]{1,0:T(8,128)(2,1)S(1)} %collective-permute-done.4.after_ref, ...), custom_call_target="tpu_custom_call" | custom-call | flops 1000000 | bytes 100000 | tf_op jit(solution)/shard_map/pallas_call | solution.py:397
  49.0 9.4 %shard_map.125 = bf16[384,1024]{1,0:T(8,128)(2,1)S(1)} custom-call(bf16[8,384,128]{2,1,0:T(8,128)(2,1)S(1)} %get-tuple-element.33.q_ref, bf16[8,384,128]{2,1,0:T(8,128)(2,1)S(1)} %get-tuple-element.34.k_ref, bf16[8,384,128]{2,1,0:T(8,128)(2,1)S(1)} %get-tuple-element.35.v_ref, bf16[8,48,768]{2,1,0:T(8,128)(2,1)S(1)} %collective-permute-done.7.blocks_ref, ...), custom_call_target="tpu_custom_call" | custom-call | flops 6000000000 | bytes 14000000 | tf_op jit(solution)/shard_map/pallas_call | solution.py:411
  58.4 0.0 copy-start
  58.4 0.0 copy-start.1
  58.4 18.4 %all_to_all.10.part_ref = bf16[8,48,1024]{2,1,0:T(8,128)(2,1)S(1)} all-to-all(bf16[8,48,1024]{2,1,0:T(8,128)(2,1)S(1)} %bitcast.3), channel_id=1, replica_groups=mesh['row'=16,'col'=8] {'col'}, dimensions={0} | all-to-all | bytes 1572864 | tf_op jit(solution)/shard_map/all_to_all | solution.py:424
  76.9 2.8 %shard_map.126 = (bf16[384,128]{1,0:T(8,128)(2,1)}, bf16[48,768]{1,0:T(8,128)(2,1)}) custom-call(bf16[8,48,1024]{2,1,0:T(8,128)(2,1)S(1)} %all_to_all.10.part_ref, f32[48,1024]{1,0:T(8,128)S(1)} %get-tuple-element.37.gate_ref, f32[48,768]{1,0:T(8,128)S(1)} %get-tuple-element.38.single_ref, f32[384,128]{1,0:T(8,128)S(1)} %get-tuple-element.39.mid_ref, ...), custom_call_target="tpu_custom_call" | custom-call | flops 400000000 | bytes 5000000 | tf_op jit(solution)/shard_map/pallas_call | solution.py:425
  (11 shorter events, 0.0 us)
Async XLA Ops:
  1.4 10.3 %copy-start.2 = (s32[1,384]{1,0:T(1,128)S(1)}, s32[1,384]{1,0:T(1,128)}, u32[]{:S(2)}) copy-start(s32[1,384]{1,0:T(1,128)} %owner_ref.3) | copy-start | bytes 4612
  1.4 10.2 %collective-permute-start = (bf16[48,128]{1,0:T(8,128)(2,1)S(1)}, bf16[48,128]{1,0:T(8,128)(2,1)S(1)}, u32[]{:S(2)}, u32[]{:S(2)}) collective-permute-start(bf16[48,128]{1,0:T(8,128)(2,1)S(1)} %get-tuple-element.41), channel_id=1, source_target_pairs={{0,1},{1,2},{2,3},{3,4},{4,5},{5,6},{6,7},{7,8},{8,9},{9,10},{10,1... | collective-permute-start | bytes 36872 | tf_op jit(solution)/shard_map/ppermute | solution.py:344
  5.4 6.2 %collective-permute-start.1 = (bf16[48,128]{1,0:T(8,128)(2,1)S(1)}, bf16[48,128]{1,0:T(8,128)(2,1)S(1)}, u32[]{:S(2)}, u32[]{:S(2)}) collective-permute-start(bf16[48,128]{1,0:T(8,128)(2,1)S(1)} %get-tuple-element.40), channel_id=1, source_target_pairs={{1,0},{2,1},{3,2},{4,3},{5,4},{6,5},{7,6},{8,7},{9,8},{10,9},{11,1... | collective-permute-start | bytes 36872 | tf_op jit(solution)/shard_map/ppermute | solution.py:347
  14.0 10.6 %collective-permute-start.3 = (bf16[48,768]{1,0:T(8,128)(2,1)S(1)}, bf16[48,768]{1,0:T(8,128)(2,1)S(1)}, u32[]{:S(2)}, u32[]{:S(2)}) collective-permute-start(bf16[48,768]{1,0:T(8,128)(2,1)S(1)} %get-tuple-element.26.norm_ref), channel_id=1, source_target_pairs={{0,4},{1,5},{2,6},{3,7},{4,0},{5,1},{6,2},{7,3},{8,12},{9,13},{10,... | collective-permute-start | bytes 221192 | tf_op jit(solution)/shard_map/ppermute | solution.py:378
  21.4 7.4 %collective-permute-start.2 = (bf16[48,768]{1,0:T(8,128)(2,1)S(1)}, bf16[48,768]{1,0:T(8,128)(2,1)S(1)}, u32[]{:S(2)}, u32[]{:S(2)}) collective-permute-start(bf16[48,768]{1,0:T(8,128)(2,1)S(1)} %get-tuple-element.26.norm_ref), channel_id=1, source_target_pairs={{0,32},{1,48},{2,0},{3,16},{4,96},{5,112},{6,64},{7,80},{8,40},{9,... | collective-permute-start | bytes 221192 | tf_op jit(solution)/shard_map/ppermute | solution.py:377
  29.7 14.6 %all-to-all-start = ((bf16[8,48,768]{2,1,0:T(8,128)(2,1)}), bf16[8,48,768]{2,1,0:T(8,128)(2,1)S(1)}, u32[]{:S(2)}, u32[]{:S(2)}) async-start(bf16[8,48,768]{2,1,0:T(8,128)(2,1)} %broadcast_in_dim.2), calls=%async_computation | async-start | bytes 1179648 | tf_op jit(solution)/shard_map/all_to_all | solution.py:382
  34.0 6.7 %collective-permute-start.4 = (bf16[96,768]{1,0:T(8,128)(2,1)S(1)}, bf16[96,768]{1,0:T(8,128)(2,1)S(1)}, u32[]{:S(2)}, u32[]{:S(2)}) collective-permute-start(bf16[96,768]{1,0:T(8,128)(2,1)S(1)} %pad_maximum_fusion.2.own_ref), channel_id=1, source_target_pairs={{0,1},{1,2},{2,3},{3,0},{4,5},{5,6},{6,7},{7,4},{8,9},{9,10},{10,1... | collective-permute-start | bytes 442376 | tf_op jit(solution)/shard_map/ppermute | solution.py:387
  34.0 8.8 %collective-permute-start.5 = (bf16[96,768]{1,0:T(8,128)(2,1)S(1)}, bf16[96,768]{1,0:T(8,128)(2,1)S(1)}, u32[]{:S(2)}, u32[]{:S(2)}) collective-permute-start(bf16[96,768]{1,0:T(8,128)(2,1)S(1)} %pad_maximum_fusion.2.own_ref), channel_id=1, source_target_pairs={{0,3},{1,0},{2,1},{3,2},{4,7},{5,4},{6,5},{7,6},{8,11},{9,8},{10,9... | collective-permute-start | bytes 442376 | tf_op jit(solution)/shard_map/ppermute | solution.py:387
  37.2 7.1 %collective-permute-start.6 = (bf16[96,768]{1,0:T(8,128)(2,1)S(1)}, bf16[96,768]{1,0:T(8,128)(2,1)S(1)}, u32[]{:S(2)}, u32[]{:S(2)}) collective-permute-start(bf16[96,768]{1,0:T(8,128)(2,1)S(1)} %pad_maximum_fusion.2.own_ref), channel_id=1, source_target_pairs={{0,2},{1,3},{2,0},{3,1},{4,6},{5,7},{6,4},{7,5},{8,10},{9,11},{10,... | collective-permute-start | bytes 442376 | tf_op jit(solution)/shard_map/ppermute | solution.py:387
  44.3 4.7 %collective-permute-start.7 = (bf16[8,48,768]{2,1,0:T(8,128)(2,1)S(1)}, bf16[8,48,768]{2,1,0:T(8,128)(2,1)S(1)}, u32[]{:S(2)}, u32[]{:S(2)}) collective-permute-start(bf16[8,48,768]{2,1,0:T(8,128)(2,1)S(1)} %all-to-all-done.blocks_ref), channel_id=1, source_target_pairs={{0,8},{8,0},{16,24},{24,16},{32,40},{40,32},{48,56},{56,48},{64,72... | collective-permute-start | bytes 1769480 | tf_op jit(solution)/shard_map/ppermute | solution.py:393
  58.4 18.5 %copy-start = (bf16[768,768]{1,0:T(8,128)(2,1)S(1)}, bf16[768,768]{1,0:T(8,128)(2,1)}, u32[]{:S(2)}) copy-start(bf16[768,768]{1,0:T(8,128)(2,1)} %output_ref.1) | copy-start | bytes 3538948
  58.4 18.5 %copy-start.1 = (bf16[768,128]{1,0:T(8,128)(2,1)S(1)}, bf16[768,128]{1,0:T(8,128)(2,1)}, u32[]{:S(2)}) copy-start(bf16[768,128]{1,0:T(8,128)(2,1)} %back_ref.1) | copy-start | bytes 589828

commit v8 on v7

--- a/solution.py
+++ b/solution.py
@@ -46,19 +46,32 @@
 
 
 def band_place(group, back=False):
-    near = lanes((BAND, BAND), 1 if back else 0) + STARTS[group]
-    far = lanes((BAND, BAND), 0 if back else 1) + group * BAND
-    return ((near // HEAD_DIM == far // SLOT) & (near % HEAD_DIM == far % SLOT)).astype(BF16)
-
-
-def spread(values):
+    far = lanes((BAND, 1) if back else (1, BAND), 0 if back else 1) + group * BAND
+    within = far & (SLOT - 1)
+    source = (far >> 6) * HEAD_DIM + within - STARTS[group]
+    source = jnp.where(within < HEAD_DIM, source, -1)
+    return (lanes((BAND, BAND), 1 if back else 0) == source).astype(BF16)
+
+
+def level_place(first, amount):
+    here, there = lanes((BAND, 1), 0), lanes((1, BAND), 1)
+    within = (here & (SLOT - 1)) - HEAD_DIM - first
+    head = jnp.where((within >= 0) & (within < amount), here >> 6, -1)
+    return (head == there >> 6).astype(BF16)
+
+
+def places(back=False):
+    return [band_place(g, back) for g in range(HEADS // 4)]
+
+
+def spread(values, into):
     return [
-        dot(values[:, STARTS[g] : STARTS[g] + BAND], band_place(g)) for g in range(HEADS // 4)
+        dot(values[:, STARTS[g] : STARTS[g] + BAND], into[g]) for g in range(HEADS // 4)
     ]
 
 
 def gather_lanes(values):
-    parts = [dot(values[g], band_place(g, True)) for g in range(HEADS // 4)]
+    parts = [dot(values[g], place) for g, place in enumerate(places(True))]
     lane = 2 * SLOT
     return jnp.concatenate(
         [
@@ -91,11 +104,9 @@
 def window(start, query, keys, values, gates, biases, bounds=None):
     width = query.shape[1]
     head_width = width // ATOM_HEADS
-    head_of = lanes((WIN_Q, width), 1) // head_width
-    stacked = jnp.concatenate(
-        [jnp.where(head_of == h, query, jnp.zeros_like(query)) for h in range(ATOM_HEADS)],
-        axis=0,
-    )
+    head_of = lanes((1, width), 1) >> 5
+    masks = [(head_of == h).astype(F32) for h in range(ATOM_HEADS)]
+    stacked = jnp.concatenate([query * mask.astype(BF16) for mask in masks], axis=0)
     scores = dot(stacked, keys, ((1,), (1,))) * (1.0 / math.sqrt(head_width))
     scores = scores + jnp.concatenate(
         [bias[start : start + WIN_Q, :] for bias in biases], axis=0
@@ -110,7 +121,7 @@
     mixed = dot(weights, values)
     mix = jnp.zeros((WIN_Q, width), F32)
     for h in range(ATOM_HEADS):
-        mix = jnp.where(head_of == h, mixed[h * WIN_Q : (h + 1) * WIN_Q], mix)
+        mix = mix + mixed[h * WIN_Q : (h + 1) * WIN_Q] * masks[h]
     return (mix * gates).astype(BF16)
 
 
@@ -133,13 +144,11 @@
 
 
 def atom_step(
-    left_ref, right_ref, narrow_ref, broad_ref, owner_ref, q_ref, k_ref, v_ref, gate_ref,
-    gated_ref, mid_ref, single_ref, norm_ref,
+    left_ref, right_ref, narrow_ref, pool_ref, input_ref, owner_ref, q_ref, k_ref, v_ref,
+    gate_ref, gated_ref, mid_ref, single_ref, norm_ref,
 ):
-    width = narrow_ref.shape[1]
     count = owner_ref.shape[1]
     state_ref, biases, weights = narrow_parts(narrow_ref, count)
-    pool_ref, input_ref = broad_ref.at[:width], broad_ref.at[width:]
     rows, cols = lax.axis_size("row"), lax.axis_size("col")
     first = (lax.axis_index("row") * cols + lax.axis_index("col")) * count
     bounds = (first, count * rows * cols)
@@ -179,10 +188,10 @@
     norm_ref[...] = layer_norm(single).astype(BF16)
 
 
-def query_rows(parts, weight, q_ref):
+def query_rows(parts, weight, into, q_ref):
     tokens = parts[0].shape[0] // 2
     lane = 2 * SLOT
-    bands = spread(dot(jnp.concatenate(parts, axis=0), weight).astype(BF16))
+    bands = spread(dot(jnp.concatenate(parts, axis=0), weight).astype(BF16), into)
     ring = lax.axis_size("col") // 2
     me = lax.axis_index("col")
     high, low = me // ring, me % ring
@@ -197,15 +206,15 @@
                 q_ref[2 * g + 1, at, :] = block[:, lane:]
 
 
-def key_rows(blocks_ref, weight, k_ref):
+def key_rows(blocks_ref, weight, into, k_ref):
     rows = jnp.concatenate([blocks_ref[i] for i in ORDER], axis=0)
-    store_pairs(k_ref, spread(dot(rows, weight).astype(BF16)))
-
-
-def value_rows(blocks_ref, weight, v_ref):
+    store_pairs(k_ref, spread(dot(rows, weight).astype(BF16), into))
+
+
+def value_rows(blocks_ref, weight, into, v_ref):
     rows = jnp.concatenate([blocks_ref[i] for i in ORDER], axis=0)
-    mass = lanes((1, BAND), 1) % SLOT == HEAD_DIM
-    bands = spread(dot(rows, weight).astype(BF16))
+    mass = (lanes((1, BAND), 1) & (SLOT - 1)) == HEAD_DIM
+    bands = spread(dot(rows, weight).astype(BF16), into)
     store_pairs(v_ref, [jnp.where(mass, 1.0, band) for band in bands])
 
 
@@ -220,19 +229,20 @@
     ]
     for copy in copies:
         copy.start()
+    into = places()
     copies[0].wait()
     query_rows(
-        [own_ref[...], after_ref[...], before_ref[...], far_ref[...]], edge_ref[0], q_ref
+        [own_ref[...], after_ref[...], before_ref[...], far_ref[...]], edge_ref[0], into, q_ref
     )
     copies[1].wait()
-    key_rows(blocks_ref, key_ref[0], k_ref)
+    key_rows(blocks_ref, key_ref[0], into, k_ref)
     copies[2].wait()
-    value_rows(blocks_ref, key_ref[1], v_ref)
+    value_rows(blocks_ref, key_ref[1], into, v_ref)
     copies[3].wait()
     gates = jax.nn.sigmoid(dot(norm_ref[...], edge_ref[1]))
     top = gates.astype(BF16)
     rest = (gates - top.astype(F32)).astype(BF16)
-    for g, (a, b) in enumerate(zip(spread(top), spread(rest))):
+    for g, (a, b) in enumerate(zip(spread(top, into), spread(rest, into))):
         gate_ref[:, g * BAND : (g + 1) * BAND] = a + b
 
 
@@ -247,13 +257,19 @@
     ]
     for copy in copies:
         copy.start()
-    key_rows(blocks_ref, proj_ref[0], other_k)
-    value_rows(blocks_ref, proj_ref[1], other_v)
+    into = places()
+    key_rows(blocks_ref, proj_ref[0], into, other_k)
+    value_rows(blocks_ref, proj_ref[1], into, other_v)
     core = lax.rem(lax.axis_index("row"), 2)
     count, half = q_ref.shape[1], k_ref.shape[1]
     mine_at = pl.ds(pl.multiple_of(core * half, lane), half)
     other_at = pl.ds(pl.multiple_of((1 - core) * half, lane), half)
     at = lanes((count, lane), 1)
+    first_head = at < SLOT
+    spare = (at & (SLOT - 1)) - HEAD_DIM
+    spares = [spare == i for i in range(5)]
+    row = lanes((1, lane), 1)
+    masks = [(row < SLOT).astype(BF16), (row >= SLOT).astype(BF16)]
     factor = 1.0 / math.sqrt(HEAD_DIM)
     for pair in range(PAIRS):
         if pair == 0:
@@ -266,21 +282,20 @@
         both = []
         for a in range(2):
             head = 2 * pair + a
-            mine = jnp.where(at // SLOT == a, query, jnp.zeros_like(query))
+            mine = query * masks[a]
             bias = jnp.concatenate(
                 [bias_ref[head, :, mine_at], bias_ref[head, :, other_at]], axis=1
             )
             scores = dot(mine, key, ((1,), (1,))) * factor + bias.astype(F32)
             top = jnp.max(scores, axis=-1, keepdims=True)
             both.append((dot(jnp.exp(scores - top).astype(BF16), value), top))
-        result = jnp.where(at < SLOT, both[0][0], both[1][0])
-        top = jnp.where(at < SLOT, both[0][1], both[1][1])
-        place = at % SLOT - HEAD_DIM
+        result = jnp.where(first_head, both[0][0], both[1][0])
+        top = jnp.where(first_head, both[0][1], both[1][1])
         rest = result - result.astype(BF16).astype(F32)
-        result = jnp.where(place == 1, pltpu.roll(rest, 1, 1), result)
+        result = jnp.where(spares[1], pltpu.roll(rest, 1, 1), result)
         for piece in range(3):
             part = top.astype(BF16).astype(F32)
-            result = jnp.where(place == 2 + piece, part, result)
+            result = jnp.where(spares[2 + piece], part, result)
             top = top - part
         part_ref[:, pair * lane : (pair + 1) * lane] = result.astype(BF16)
 
@@ -290,10 +305,7 @@
     token_ref,
 ):
     shares, tokens, _ = part_ref.shape
-    here, there = lanes((BAND, BAND), 0), lanes((BAND, BAND), 1)
-    same, place = here // SLOT == there // SLOT, here % SLOT - HEAD_DIM
-    mass_of = (same & (place >= 0) & (place < 2)).astype(BF16)
-    top_of = (same & (place >= 2) & (place < 5)).astype(BF16)
+    mass_of, top_of = level_place(0, 2), level_place(2, 3)
     gated = []
     for g in range(HEADS // 4):
         span = slice(g * BAND, (g + 1) * BAND)
@@ -350,7 +362,6 @@
         + [array.reshape(-1, width) for array in (atom_bias, atom_proj, atom_output)],
         axis=0,
     )
-    broad = jnp.concatenate([pool_weight, token_input], axis=0)
     inner = call(
         inner_step,
         tuple(shape((count, width), kind) for kind in (BF16, BF16, BF16, F32))
@@ -367,7 +378,7 @@
         ),
         ATOM_MB,
         (200_000_000, 2_000_000),
-    )(left, right, narrow, broad, atom_owner, *inner)
+    )(left, right, narrow, pool_weight, token_input, atom_owner, *inner)
     ring = cols // 2
     turn = []
     for r in range(rows):

time: 80.2 us -> 79.6 us (level)
  waiting for transfers between devices: 11 us -> 9.81 us
  other arithmetic: 2.14 us -> 1.15 us
    all_to_all x1, starting transfers between devices: 4.24 us -> 5.82 us  [per_device(): lax.all_to_all(jnp.broadcast_to(turned[None], (rows // 2, tokens, depth))...]
    ppermute x1, waiting for transfers between devices: 4.22 us -> 2.65 us  [per_device(): turned = lax.ppermute(norm, BOTH, turn)]
    concatenate x1 -> x0, other arithmetic: 0.98 us -> none  [per_device(): broad = jnp.concatenate([pool_weight, token_input], axis=0)]
  transfers between devices with their start and end apart: 9 -> 9, of which waited for: 4 -> 5; matrix products, arithmetic and copies ran while one was open for 3% -> 1% of each run, Pallas kernels for 9% -> 9%
where the time goes in v8:
time: 79.6 us; the launch traced here: 79.2 us
  starting transfers between devices  24.6 us (31%)
  Pallas kernels  22.6 us (28%)
  blocking collectives  18.7 us (23%)
  waiting for transfers between devices  9.81 us (12%)
  local copies, waits for them, and re-layouts  1.67 us (2%)
  other arithmetic  1.15 us (1%)
    all_to_all x1, blocking collectives, per_device(): parts = lax.all_to_all(parts.reshape(cols, tokens, wide), 'col', 0, 0)  18.7 us
    pallas_call x1, Pallas kernels, per_device(): call(token_step, shape((q_count, wide), BF16), MOST, (6000000000, 1400000...  9.89 us
    ppermute x1, starting transfers between devices, per_device(): lax.ppermute(norm, 'col', [(i, (i + ring) % cols) for i in range(cols)])  7.12 us
    ppermute x3, waiting for transfers between devices, per_device(): lax.ppermute(own, 'col', [(i, i // ring * ring + (i + step) % ring) for i...  6.79 us
    all_to_all x1, starting transfers between devices, per_device(): lax.all_to_all(jnp.broadcast_to(turned[None], (rows // 2, tokens, depth))...  5.82 us
    pallas_call x1, Pallas kernels, per_device(): call(project_step, (shape((PAIRS, q_count, lane), BF16), shape((tokens, w...  4.68 us
    ppermute x1, starting transfers between devices, per_device(): lax.ppermute(atom_state[count - REACH:], BOTH, [(i, i + 1) for i in range...  3.89 us
    ppermute x3, starting transfers between devices, per_device(): lax.ppermute(own, 'col', [(i, i // ring * ring + (i + step) % ring) for i...  3.23 us
  transfers between devices with their start and end apart: 9, of which 5 were waited for; matrix products, arithmetic and copies ran while one was open for 1% of the time, Pallas kernels for 9%

profile of v8, /device:TPU:0, one launch (start us, length us, event | category | flops | bytes accessed | tf_op | source)
XLA Modules:
  0.0 79.2 jit_solution(16202521339789243209)
XLA Ops:
  0.7 0.8 fusion
  1.4 3.9 %collective-permute-start = (bf16[48,128]{1,0:T(8,128)(2,1)S(1)}, bf16[48,128]{1,0:T(8,128)(2,1)S(1)}, u32[]{:S(2)}, u32[]{:S(2)}) collective-permute-start(bf16[48,128]{1,0:T(8,128)(2,1)S(1)} %get-tuple-element.41), channel_id=1, source_target_pairs={{0,1},{1,2},{2,3},{3,4},{4,5},{5,6},{6,7},{7,8},{8,9},{9,10},{10,1... | collective-permute-start | bytes 36872 | tf_op jit(solution)/shard_map/ppermute | solution.py:356
  5.3 1.3 %collective-permute-start.1 = (bf16[48,128]{1,0:T(8,128)(2,1)S(1)}, bf16[48,128]{1,0:T(8,128)(2,1)S(1)}, u32[]{:S(2)}, u32[]{:S(2)}) collective-permute-start(bf16[48,128]{1,0:T(8,128)(2,1)S(1)} %get-tuple-element.40), channel_id=1, source_target_pairs={{1,0},{2,1},{3,2},{4,3},{5,4},{6,5},{7,6},{8,7},{9,8},{10,9},{11,1... | collective-permute-start | bytes 36872 | tf_op jit(solution)/shard_map/ppermute | solution.py:359
  6.6 1.1 %pad_maximum_fusion.narrow_ref = bf16[2560,128]{1,0:T(8,128)(2,1)S(1)} fusion(bf16[128,128]{1,0:T(8,128)(2,1)} %param.17, bf16[512,128]{1,0:T(8,128)(2,1)} %bitcast.5, bf16[1536,128]{1,0:T(8,128)(2,1)} %bitcast.4, bf16[384,128]{1,0:T(8,128)(2,1)} %param.11), kind=kLoop, calls=%fused_computation | loop fusion | flops 2621440 | bytes 1310720 | tf_op jit(solution)/shard_map/concatenate | solution.py:360
  7.8 2.8 %shard_map.122 = (bf16[384,128]{1,0:T(8,128)(2,1)S(1)}, bf16[384,128]{1,0:T(8,128)(2,1)S(1)}, bf16[384,128]{1,0:T(8,128)(2,1)S(1)}, f32[384,128]{1,0:T(8,128)S(1)}, bf16[256,128]{1,0:T(8,128)(2,1)S(1)}) custom-call(bf16[2560,128]{1,0:T(8,128)(2,1)S(1)} %pad_maximum_fusion.narrow_ref), custom_call_target="tpu_custom_call" | custom-call | flops 200000000 | bytes 1000000 | tf_op jit(solution)/shard_map/pallas_call | solution.py:365
  10.6 0.0 collective-permute-done.left_ref
  10.6 0.4 collective-permute-done.1.right_ref
  10.9 2.4 %shard_map.123 = (f32[384,128]{1,0:T(8,128)S(1)}, f32[48,768]{1,0:T(8,128)S(1)}, bf16[48,768]{1,0:T(8,128)(2,1)S(1)}) custom-call(bf16[48,128]{1,0:T(8,128)(2,1)S(1)} %collective-permute-done.left_ref, bf16[48,128]{1,0:T(8,128)(2,1)S(1)} %collective-permute-done.1.right_ref, bf16[2560,128]{1,0:T(8,128)(2,1)S(1)} %pad_maximum_fusion.narrow_ref, ...), custom_call_target="tpu_custom_call" | custom-call | flops 200000000 | bytes 2000000 | tf_op jit(solution)/shard_map/pallas_call | solution.py:372
  13.3 7.1 %collective-permute-start.3 = (bf16[48,768]{1,0:T(8,128)(2,1)S(1)}, bf16[48,768]{1,0:T(8,128)(2,1)S(1)}, u32[]{:S(2)}, u32[]{:S(2)}) collective-permute-start(bf16[48,768]{1,0:T(8,128)(2,1)S(1)} %get-tuple-element.26.norm_ref), channel_id=1, source_target_pairs={{0,4},{1,5},{2,6},{3,7},{4,0},{5,1},{6,2},{7,3},{8,12},{9,13},{10,... | collective-permute-start | bytes 221192 | tf_op jit(solution)/shard_map/ppermute | solution.py:389
  20.4 3.2 %collective-permute-start.2 = (bf16[48,768]{1,0:T(8,128)(2,1)S(1)}, bf16[48,768]{1,0:T(8,128)(2,1)S(1)}, u32[]{:S(2)}, u32[]{:S(2)}) collective-permute-start(bf16[48,768]{1,0:T(8,128)(2,1)S(1)} %get-tuple-element.26.norm_ref), channel_id=1, source_target_pairs={{0,32},{1,48},{2,0},{3,16},{4,96},{5,112},{6,64},{7,80},{8,40},{9,... | collective-permute-start | bytes 221192 | tf_op jit(solution)/shard_map/ppermute | solution.py:388
  23.6 2.6 %collective-permute-done.2 = bf16[48,768]{1,0:T(8,128)(2,1)S(1)} collective-permute-done((bf16[48,768]{1,0:T(8,128)(2,1)S(1)}, bf16[48,768]{1,0:T(8,128)(2,1)S(1)}, u32[]{:S(2)}, u32[]{:S(2)}) %collective-permute-start.2) | collective-permute-done | bytes 73760 | tf_op jit(solution)/shard_map/ppermute | solution.py:388
  26.3 0.9 %broadcast_in_dim.2 = bf16[8,48,768]{2,1,0:T(8,128)(2,1)} broadcast(bf16[48,768]{1,0:T(8,128)(2,1)S(1)} %collective-permute-done.2), dimensions={1,2} | broadcast | bytes 663552 | tf_op jit(solution)/shard_map/broadcast_in_dim | solution.py:394
  27.2 5.8 %all-to-all-start = ((bf16[8,48,768]{2,1,0:T(8,128)(2,1)}), bf16[8,48,768]{2,1,0:T(8,128)(2,1)S(1)}, u32[]{:S(2)}, u32[]{:S(2)}) async-start(bf16[8,48,768]{2,1,0:T(8,128)(2,1)} %broadcast_in_dim.2), calls=%async_computation | async-start | bytes 1179648 | tf_op jit(solution)/shard_map/all_to_all | solution.py:393
  33.0 3.2 %collective-permute-start.5 = (bf16[96,768]{1,0:T(8,128)(2,1)S(1)}, bf16[96,768]{1,0:T(8,128)(2,1)S(1)}, u32[]{:S(2)}, u32[]{:S(2)}) collective-permute-start(bf16[96,768]{1,0:T(8,128)(2,1)S(1)} %pad_maximum_fusion.1.own_ref), channel_id=1, source_target_pairs={{0,3},{1,0},{2,1},{3,2},{4,7},{5,4},{6,5},{7,6},{8,11},{9,8},{10,9... | collective-permute-start | bytes 442376 | tf_op jit(solution)/shard_map/ppermute | solution.py:398
  36.2 3.6 %collective-permute-done.4.after_ref = bf16[96,768]{1,0:T(8,128)(2,1)S(1)} collective-permute-done((bf16[96,768]{1,0:T(8,128)(2,1)S(1)}, bf16[96,768]{1,0:T(8,128)(2,1)S(1)}, u32[]{:S(2)}, u32[]{:S(2)}) %collective-permute-start.4) | collective-permute-done | bytes 147488 | tf_op jit(solution)/shard_map/ppermute | solution.py:398
  39.8 1.9 %collective-permute-done.5.before_ref = bf16[96,768]{1,0:T(8,128)(2,1)S(1)} collective-permute-done((bf16[96,768]{1,0:T(8,128)(2,1)S(1)}, bf16[96,768]{1,0:T(8,128)(2,1)S(1)}, u32[]{:S(2)}, u32[]{:S(2)}) %collective-permute-start.5) | collective-permute-done | bytes 147488 | tf_op jit(solution)/shard_map/ppermute | solution.py:398
  41.7 1.3 %collective-permute-done.6.far_ref = bf16[96,768]{1,0:T(8,128)(2,1)S(1)} collective-permute-done((bf16[96,768]{1,0:T(8,128)(2,1)S(1)}, bf16[96,768]{1,0:T(8,128)(2,1)S(1)}, u32[]{:S(2)}, u32[]{:S(2)}) %collective-permute-start.6) | collective-permute-done | bytes 147488 | tf_op jit(solution)/shard_map/ppermute | solution.py:398
  43.0 0.0 collective-permute-start.7
  43.0 4.7 %shard_map.124 = (bf16[8,384,128]{2,1,0:T(8,128)(2,1)S(1)}, f32[48,1024]{1,0:T(8,128)S(1)}, bf16[8,384,128]{2,1,0:T(8,128)(2,1)S(1)}, bf16[8,384,128]{2,1,0:T(8,128)(2,1)S(1)}, bf16[2,768,768]{2,1,0:T(8,128)(2,1)S(1)}) custom-call(bf16[96,768]{1,0:T(8,128)(2,1)S(1)} %pad_maximum_fusion.1.own_ref, bf16[96,768]{1,0:T(8,128)(2,1)S(1)} %collective-permute-done.4.after_ref, ...), custom_call_target="tpu_custom_call" | custom-call | flops 1000000 | bytes 100000 | tf_op jit(solution)/shard_map/pallas_call | solution.py:408
  47.7 9.9 %shard_map.125 = bf16[384,1024]{1,0:T(8,128)(2,1)S(1)} custom-call(bf16[8,384,128]{2,1,0:T(8,128)(2,1)S(1)} %get-tuple-element.33.q_ref, bf16[8,384,128]{2,1,0:T(8,128)(2,1)S(1)} %get-tuple-element.34.k_ref, bf16[8,384,128]{2,1,0:T(8,128)(2,1)S(1)} %get-tuple-element.35.v_ref, bf16[8,48,768]{2,1,0:T(8,128)(2,1)S(1)} %collective-permute-done.7.blocks_ref, ...), custom_call_target="tpu_custom_call" | custom-call | flops 6000000000 | bytes 14000000 | tf_op jit(solution)/shard_map/pallas_call | solution.py:422
  57.6 0.0 copy-start
  57.6 0.0 copy-start.2
  57.6 18.7 %all_to_all.10.part_ref = bf16[8,48,1024]{2,1,0:T(8,128)(2,1)S(1)} all-to-all(bf16[8,48,1024]{2,1,0:T(8,128)(2,1)S(1)} %bitcast.3), channel_id=1, replica_groups=mesh['row'=16,'col'=8] {'col'}, dimensions={0} | all-to-all | bytes 1572864 | tf_op jit(solution)/shard_map/all_to_all | solution.py:435
  76.3 2.9 %shard_map.126 = (bf16[384,128]{1,0:T(8,128)(2,1)}, bf16[48,768]{1,0:T(8,128)(2,1)}) custom-call(bf16[8,48,1024]{2,1,0:T(8,128)(2,1)S(1)} %all_to_all.10.part_ref, f32[48,1024]{1,0:T(8,128)S(1)} %get-tuple-element.37.gate_ref, f32[48,768]{1,0:T(8,128)S(1)} %get-tuple-element.38.single_ref, f32[384,128]{1,0:T(8,128)S(1)} %get-tuple-element.39.mid_ref, ...), custom_call_target="tpu_custom_call" | custom-call | flops 400000000 | bytes 5000000 | tf_op jit(solution)/shard_map/pallas_call | solution.py:436
  (14 shorter events, 0.0 us)
Async XLA Ops:
  0.6 10.3 %copy-start.3 = (bf16[48,768]{1,0:T(8,128)(2,1)S(1)}, bf16[48,768]{1,0:T(8,128)(2,1)}, u32[]{:S(2)}) copy-start(bf16[48,768]{1,0:T(8,128)(2,1)} %input_ref.1) | copy-start | bytes 221188
  0.6 10.3 %copy-start.4 = (s32[1,384]{1,0:T(1,128)S(1)}, s32[1,384]{1,0:T(1,128)}, u32[]{:S(2)}) copy-start(s32[1,384]{1,0:T(1,128)} %owner_ref.3) | copy-start | bytes 4612
  0.7 10.3 %copy-start.1 = (bf16[128,768]{1,0:T(8,128)(2,1)S(1)}, bf16[128,768]{1,0:T(8,128)(2,1)}, u32[]{:S(2)}) copy-start(bf16[128,768]{1,0:T(8,128)(2,1)} %pool_ref.1) | copy-start | bytes 589828
  1.4 9.1 %collective-permute-start = (bf16[48,128]{1,0:T(8,128)(2,1)S(1)}, bf16[48,128]{1,0:T(8,128)(2,1)S(1)}, u32[]{:S(2)}, u32[]{:S(2)}) collective-permute-start(bf16[48,128]{1,0:T(8,128)(2,1)S(1)} %get-tuple-element.41), channel_id=1, source_target_pairs={{0,1},{1,2},{2,3},{3,4},{4,5},{5,6},{6,7},{7,8},{8,9},{9,10},{10,1... | collective-permute-start | bytes 36872 | tf_op jit(solution)/shard_map/ppermute | solution.py:356
  5.3 5.6 %collective-permute-start.1 = (bf16[48,128]{1,0:T(8,128)(2,1)S(1)}, bf16[48,128]{1,0:T(8,128)(2,1)S(1)}, u32[]{:S(2)}, u32[]{:S(2)}) collective-permute-start(bf16[48,128]{1,0:T(8,128)(2,1)S(1)} %get-tuple-element.40), channel_id=1, source_target_pairs={{1,0},{2,1},{3,2},{4,3},{5,4},{6,5},{7,6},{8,7},{9,8},{10,9},{11,1... | collective-permute-start | bytes 36872 | tf_op jit(solution)/shard_map/ppermute | solution.py:359
  13.3 10.3 %collective-permute-start.3 = (bf16[48,768]{1,0:T(8,128)(2,1)S(1)}, bf16[48,768]{1,0:T(8,128)(2,1)S(1)}, u32[]{:S(2)}, u32[]{:S(2)}) collective-permute-start(bf16[48,768]{1,0:T(8,128)(2,1)S(1)} %get-tuple-element.26.norm_ref), channel_id=1, source_target_pairs={{0,4},{1,5},{2,6},{3,7},{4,0},{5,1},{6,2},{7,3},{8,12},{9,13},{10,... | collective-permute-start | bytes 221192 | tf_op jit(solution)/shard_map/ppermute | solution.py:389
  20.4 5.9 %collective-permute-start.2 = (bf16[48,768]{1,0:T(8,128)(2,1)S(1)}, bf16[48,768]{1,0:T(8,128)(2,1)S(1)}, u32[]{:S(2)}, u32[]{:S(2)}) collective-permute-start(bf16[48,768]{1,0:T(8,128)(2,1)S(1)} %get-tuple-element.26.norm_ref), channel_id=1, source_target_pairs={{0,32},{1,48},{2,0},{3,16},{4,96},{5,112},{6,64},{7,80},{8,40},{9,... | collective-permute-start | bytes 221192 | tf_op jit(solution)/shard_map/ppermute | solution.py:388
  27.2 15.9 %all-to-all-start = ((bf16[8,48,768]{2,1,0:T(8,128)(2,1)}), bf16[8,48,768]{2,1,0:T(8,128)(2,1)S(1)}, u32[]{:S(2)}, u32[]{:S(2)}) async-start(bf16[8,48,768]{2,1,0:T(8,128)(2,1)} %broadcast_in_dim.2), calls=%async_computation | async-start | bytes 1179648 | tf_op jit(solution)/shard_map/all_to_all | solution.py:393
  33.0 6.8 %collective-permute-start.4 = (bf16[96,768]{1,0:T(8,128)(2,1)S(1)}, bf16[96,768]{1,0:T(8,128)(2,1)S(1)}, u32[]{:S(2)}, u32[]{:S(2)}) collective-permute-start(bf16[96,768]{1,0:T(8,128)(2,1)S(1)} %pad_maximum_fusion.1.own_ref), channel_id=1, source_target_pairs={{0,1},{1,2},{2,3},{3,0},{4,5},{5,6},{6,7},{7,4},{8,9},{9,10},{10,1... | collective-permute-start | bytes 442376 | tf_op jit(solution)/shard_map/ppermute | solution.py:398
  33.0 8.7 %collective-permute-start.5 = (bf16[96,768]{1,0:T(8,128)(2,1)S(1)}, bf16[96,768]{1,0:T(8,128)(2,1)S(1)}, u32[]{:S(2)}, u32[]{:S(2)}) collective-permute-start(bf16[96,768]{1,0:T(8,128)(2,1)S(1)} %pad_maximum_fusion.1.own_ref), channel_id=1, source_target_pairs={{0,3},{1,0},{2,1},{3,2},{4,7},{5,4},{6,5},{7,6},{8,11},{9,8},{10,9... | collective-permute-start | bytes 442376 | tf_op jit(solution)/shard_map/ppermute | solution.py:398
  36.2 6.8 %collective-permute-start.6 = (bf16[96,768]{1,0:T(8,128)(2,1)S(1)}, bf16[96,768]{1,0:T(8,128)(2,1)S(1)}, u32[]{:S(2)}, u32[]{:S(2)}) collective-permute-start(bf16[96,768]{1,0:T(8,128)(2,1)S(1)} %pad_maximum_fusion.1.own_ref), channel_id=1, source_target_pairs={{0,2},{1,3},{2,0},{3,1},{4,6},{5,7},{6,4},{7,5},{8,10},{9,11},{10,... | collective-permute-start | bytes 442376 | tf_op jit(solution)/shard_map/ppermute | solution.py:398
  43.0 4.7 %collective-permute-start.7 = (bf16[8,48,768]{2,1,0:T(8,128)(2,1)S(1)}, bf16[8,48,768]{2,1,0:T(8,128)(2,1)S(1)}, u32[]{:S(2)}, u32[]{:S(2)}) collective-permute-start(bf16[8,48,768]{2,1,0:T(8,128)(2,1)S(1)} %all-to-all-done.blocks_ref), channel_id=1, source_target_pairs={{0,8},{8,0},{16,24},{24,16},{32,40},{40,32},{48,56},{56,48},{64,72... | collective-permute-start | bytes 1769480 | tf_op jit(solution)/shard_map/ppermute | solution.py:404
  57.6 18.7 %copy-start = (bf16[768,768]{1,0:T(8,128)(2,1)S(1)}, bf16[768,768]{1,0:T(8,128)(2,1)}, u32[]{:S(2)}) copy-start(bf16[768,768]{1,0:T(8,128)(2,1)} %output_ref.1) | copy-start | bytes 3538948
  57.6 18.7 %copy-start.2 = (bf16[768,128]{1,0:T(8,128)(2,1)S(1)}, bf16[768,128]{1,0:T(8,128)(2,1)}, u32[]{:S(2)}) copy-start(bf16[768,128]{1,0:T(8,128)(2,1)} %back_ref.1) | copy-start | bytes 589828

commit v9 on v8

--- a/solution.py
+++ b/solution.py
@@ -41,6 +41,7 @@
     return lax.broadcasted_iota(jnp.int32, shape, axis)
 
 
+META = 8
 BAND = 2 * 2 * SLOT
 STARTS = (0, 128, 384, 512)
 
@@ -53,11 +54,18 @@
     return (lanes((BAND, BAND), 1 if back else 0) == source).astype(BF16)
 
 
-def level_place(first, amount):
-    here, there = lanes((BAND, 1), 0), lanes((1, BAND), 1)
-    within = (here & (SLOT - 1)) - HEAD_DIM - first
-    head = jnp.where((within >= 0) & (within < amount), here >> 6, -1)
-    return (head == there >> 6).astype(BF16)
+def meta_place(group):
+    far = lanes((BAND, 1), 0) + group * BAND
+    within = (far & (SLOT - 1)) - HEAD_DIM
+    target = jnp.where((within >= 0) & (within < 5), (far >> 6) * META + within, -1)
+    return (lanes((BAND, 2 * SLOT), 1) == target).astype(BF16)
+
+
+def level_place(block, first, amount):
+    here, there = lanes((2 * SLOT, 1), 0), lanes((1, BAND), 1) + block * BAND
+    within = (here & (META - 1)) - first
+    head = jnp.where((within >= 0) & (within < amount), here >> 3, -1)
+    return (head == there // HEAD_DIM).astype(BF16)
 
 
 def places(back=False):
@@ -239,11 +247,7 @@
     copies[2].wait()
     value_rows(blocks_ref, key_ref[1], into, v_ref)
     copies[3].wait()
-    gates = jax.nn.sigmoid(dot(norm_ref[...], edge_ref[1]))
-    top = gates.astype(BF16)
-    rest = (gates - top.astype(F32)).astype(BF16)
-    for g, (a, b) in enumerate(zip(spread(top, into), spread(rest, into))):
-        gate_ref[:, g * BAND : (g + 1) * BAND] = a + b
+    gate_ref[...] = jax.nn.sigmoid(dot(norm_ref[...], edge_ref[1]))
 
 
 def token_step(
@@ -268,9 +272,8 @@
     first_head = at < SLOT
     spare = (at & (SLOT - 1)) - HEAD_DIM
     spares = [spare == i for i in range(5)]
-    row = lanes((1, lane), 1)
-    masks = [(row < SLOT).astype(BF16), (row >= SLOT).astype(BF16)]
     factor = 1.0 / math.sqrt(HEAD_DIM)
+    results = []
     for pair in range(PAIRS):
         if pair == 0:
             copies[0].wait()
@@ -282,7 +285,7 @@
         both = []
         for a in range(2):
             head = 2 * pair + a
-            mine = query * masks[a]
+            mine = jnp.where((at < SLOT) if a == 0 else (at >= SLOT), query, jnp.zeros_like(query))
             bias = jnp.concatenate(
                 [bias_ref[head, :, mine_at], bias_ref[head, :, other_at]], axis=1
             )
@@ -297,7 +300,11 @@
             part = top.astype(BF16).astype(F32)
             result = jnp.where(spares[2 + piece], part, result)
             top = top - part
-        part_ref[:, pair * lane : (pair + 1) * lane] = result.astype(BF16)
+        results.append(result.astype(BF16))
+    bands = [jnp.concatenate(results[i : i + 2], axis=1) for i in range(0, PAIRS, 2)]
+    width = HEADS * HEAD_DIM
+    part_ref[:, :width] = gather_lanes(bands).astype(BF16)
+    part_ref[:, width:] = sum(dot(band, meta_place(g)) for g, band in enumerate(bands)).astype(BF16)
 
 
 def last_step(
@@ -305,19 +312,18 @@
     token_ref,
 ):
     shares, tokens, _ = part_ref.shape
-    mass_of, top_of = level_place(0, 2), level_place(2, 3)
+    width = HEADS * HEAD_DIM
+    meta = jnp.concatenate([part_ref[c, :, width:] for c in range(shares)], axis=0)
     gated = []
-    for g in range(HEADS // 4):
-        span = slice(g * BAND, (g + 1) * BAND)
-        parts = jnp.concatenate([part_ref[c, :, span] for c in range(shares)], axis=0)
-        tops = dot(parts, top_of).reshape(shares, tokens, BAND)
+    for block in range(width // BAND):
+        span = slice(block * BAND, (block + 1) * BAND)
+        tops = dot(meta, level_place(block, 2, 3)).reshape(shares, tokens, BAND)
+        masses = dot(meta, level_place(block, 0, 2)).reshape(shares, tokens, BAND)
         weights = jnp.exp(tops - jnp.max(tops, axis=0))
-        mix = jnp.sum(weights * parts.astype(F32).reshape(tops.shape), axis=0)
-        high = mix.astype(BF16)
-        low = (mix - high.astype(F32)).astype(BF16)
-        mass = dot(high, mass_of) + dot(low, mass_of)
+        mix = sum(weights[c] * part_ref[c, :, span].astype(F32) for c in range(shares))
+        mass = jnp.sum(weights * masses, axis=0)
         gated.append((mix / mass * gate_ref[:, span]).astype(BF16))
-    update = dot(gather_lanes(gated).astype(BF16), output_ref[...])
+    update = dot(jnp.concatenate(gated, axis=1), output_ref[...])
     token_state = (single_ref[...] + update).astype(BF16)
     token_ref[...] = token_state
     returned = dot(token_state, back_ref[...])
@@ -351,7 +357,7 @@
     devices = rows * cols
     count, width = atom_state.shape
     tokens, depth = token_input.shape
-    wide = HEADS * SLOT
+    wide = depth + HEADS * META
     ends = devices - 1
     left = lax.ppermute(
         atom_state[count - REACH :], BOTH, [(i, i + 1) for i in range(ends)]
@@ -409,7 +415,7 @@
         project_step,
         (
             shape((PAIRS, q_count, lane), BF16),
-            shape((tokens, wide), F32),
+            shape((tokens, depth), F32),
             shape((PAIRS, half, lane), BF16),
             shape((PAIRS, half, lane), BF16),
             shape((2, depth, depth), BF16),

time: 79.6 us -> 78.1 us (0.981)
  blocking collectives: 18.7 us -> 17.8 us
    pallas_call x1, Pallas kernels: 2.85 us -> 1.93 us  [per_device(): call(last_step, (shape((count, width), BF16), shape((tokens, depth), BF16...]
    all_to_all x1, blocking collectives: 18.7 us -> 17.8 us  [per_device(): parts = lax.all_to_all(parts.reshape(cols, tokens, wide), 'col', 0, 0)]
where the time goes in v9:
time: 78.1 us; the launch traced here: 77.6 us
  starting transfers between devices  24.6 us (31%)
  Pallas kernels  21.9 us (28%)
  blocking collectives  17.8 us (23%)
  waiting for transfers between devices  9.81 us (13%)
  local copies, waits for them, and re-layouts  1.67 us (2%)
  other arithmetic  1.15 us (1%)
    all_to_all x1, blocking collectives, per_device(): parts = lax.all_to_all(parts.reshape(cols, tokens, wide), 'col', 0, 0)  17.8 us
    pallas_call x1, Pallas kernels, per_device(): call(token_step, shape((q_count, wide), BF16), MOST, (6000000000, 1400000...  10.3 us
    ppermute x1, starting transfers between devices, per_device(): lax.ppermute(norm, 'col', [(i, (i + ring) % cols) for i in range(cols)])  7.12 us
    ppermute x3, waiting for transfers between devices, per_device(): lax.ppermute(own, 'col', [(i, i // ring * ring + (i + step) % ring) for i...  6.79 us
    all_to_all x1, starting transfers between devices, per_device(): lax.all_to_all(jnp.broadcast_to(turned[None], (rows // 2, tokens, depth))...  5.82 us
    pallas_call x1, Pallas kernels, per_device(): call(project_step, (shape((PAIRS, q_count, lane), BF16), shape((tokens, d...  4.47 us
    ppermute x1, starting transfers between devices, per_device(): lax.ppermute(atom_state[count - REACH:], BOTH, [(i, i + 1) for i in range...  3.89 us
    ppermute x3, starting transfers between devices, per_device(): lax.ppermute(own, 'col', [(i, i // ring * ring + (i + step) % ring) for i...  3.23 us
  transfers between devices with their start and end apart: 9, of which 5 were waited for; matrix products, arithmetic and copies ran while one was open for 1% of the time, Pallas kernels for 9%

profile of v9, /device:TPU:0, one launch (start us, length us, event | category | flops | bytes accessed | tf_op | source)
XLA Modules:
  0.0 77.6 jit_solution(2718938743626893141)
XLA Ops:
  0.7 0.8 %fusion = (bf16[48,128]{1,0:T(8,128)(2,1)S(1)}, bf16[48,128]{1,0:T(8,128)(2,1)S(1)}) fusion(bf16[384,128]{1,0:T(8,128)(2,1)} %param.11), kind=kLoop, calls=%fused_computation.2 | loop fusion | bytes 49152 | tf_op jit(solution)/shard_map/slice | solution.py:365
  1.4 3.9 %collective-permute-start = (bf16[48,128]{1,0:T(8,128)(2,1)S(1)}, bf16[48,128]{1,0:T(8,128)(2,1)S(1)}, u32[]{:S(2)}, u32[]{:S(2)}) collective-permute-start(bf16[48,128]{1,0:T(8,128)(2,1)S(1)} %get-tuple-element.41), channel_id=1, source_target_pairs={{0,1},{1,2},{2,3},{3,4},{4,5},{5,6},{6,7},{7,8},{8,9},{9,10},{10,1... | collective-permute-start | bytes 36872 | tf_op jit(solution)/shard_map/ppermute | solution.py:362
  5.3 1.3 %collective-permute-start.1 = (bf16[48,128]{1,0:T(8,128)(2,1)S(1)}, bf16[48,128]{1,0:T(8,128)(2,1)S(1)}, u32[]{:S(2)}, u32[]{:S(2)}) collective-permute-start(bf16[48,128]{1,0:T(8,128)(2,1)S(1)} %get-tuple-element.40), channel_id=1, source_target_pairs={{1,0},{2,1},{3,2},{4,3},{5,4},{6,5},{7,6},{8,7},{9,8},{10,9},{11,1... | collective-permute-start | bytes 36872 | tf_op jit(solution)/shard_map/ppermute | solution.py:365
  6.6 1.1 %pad_maximum_fusion.narrow_ref = bf16[2560,128]{1,0:T(8,128)(2,1)S(1)} fusion(bf16[128,128]{1,0:T(8,128)(2,1)} %param.17, bf16[512,128]{1,0:T(8,128)(2,1)} %bitcast.5, bf16[1536,128]{1,0:T(8,128)(2,1)} %bitcast.4, bf16[384,128]{1,0:T(8,128)(2,1)} %param.11), kind=kLoop, calls=%fused_computation | loop fusion | flops 2621440 | bytes 1310720 | tf_op jit(solution)/shard_map/concatenate | solution.py:366
  7.8 2.8 %shard_map.122 = (bf16[384,128]{1,0:T(8,128)(2,1)S(1)}, bf16[384,128]{1,0:T(8,128)(2,1)S(1)}, bf16[384,128]{1,0:T(8,128)(2,1)S(1)}, f32[384,128]{1,0:T(8,128)S(1)}, bf16[256,128]{1,0:T(8,128)(2,1)S(1)}) custom-call(bf16[2560,128]{1,0:T(8,128)(2,1)S(1)} %pad_maximum_fusion.narrow_ref), custom_call_target="tpu_custom_call" | custom-call | flops 200000000 | bytes 1000000 | tf_op jit(solution)/shard_map/pallas_call | solution.py:371
  10.6 0.0 collective-permute-done.left_ref
  10.6 0.4 collective-permute-done.1.right_ref
  10.9 2.4 %shard_map.123 = (f32[384,128]{1,0:T(8,128)S(1)}, f32[48,768]{1,0:T(8,128)S(1)}, bf16[48,768]{1,0:T(8,128)(2,1)S(1)}) custom-call(bf16[48,128]{1,0:T(8,128)(2,1)S(1)} %collective-permute-done.left_ref, bf16[48,128]{1,0:T(8,128)(2,1)S(1)} %collective-permute-done.1.right_ref, bf16[2560,128]{1,0:T(8,128)(2,1)S(1)} %pad_maximum_fusion.narrow_ref, ...), custom_call_target="tpu_custom_call" | custom-call | flops 200000000 | bytes 2000000 | tf_op jit(solution)/shard_map/pallas_call | solution.py:378
  13.3 7.1 %collective-permute-start.3 = (bf16[48,768]{1,0:T(8,128)(2,1)S(1)}, bf16[48,768]{1,0:T(8,128)(2,1)S(1)}, u32[]{:S(2)}, u32[]{:S(2)}) collective-permute-start(bf16[48,768]{1,0:T(8,128)(2,1)S(1)} %get-tuple-element.26.norm_ref), channel_id=1, source_target_pairs={{0,4},{1,5},{2,6},{3,7},{4,0},{5,1},{6,2},{7,3},{8,12},{9,13},{10,... | collective-permute-start | bytes 221192 | tf_op jit(solution)/shard_map/ppermute | solution.py:395
  20.4 3.2 %collective-permute-start.2 = (bf16[48,768]{1,0:T(8,128)(2,1)S(1)}, bf16[48,768]{1,0:T(8,128)(2,1)S(1)}, u32[]{:S(2)}, u32[]{:S(2)}) collective-permute-start(bf16[48,768]{1,0:T(8,128)(2,1)S(1)} %get-tuple-element.26.norm_ref), channel_id=1, source_target_pairs={{0,32},{1,48},{2,0},{3,16},{4,96},{5,112},{6,64},{7,80},{8,40},{9,... | collective-permute-start | bytes 221192 | tf_op jit(solution)/shard_map/ppermute | solution.py:394
  23.6 2.6 %collective-permute-done.2 = bf16[48,768]{1,0:T(8,128)(2,1)S(1)} collective-permute-done((bf16[48,768]{1,0:T(8,128)(2,1)S(1)}, bf16[48,768]{1,0:T(8,128)(2,1)S(1)}, u32[]{:S(2)}, u32[]{:S(2)}) %collective-permute-start.2) | collective-permute-done | bytes 73760 | tf_op jit(solution)/shard_map/ppermute | solution.py:394
  26.3 0.9 %broadcast_in_dim.2 = bf16[8,48,768]{2,1,0:T(8,128)(2,1)} broadcast(bf16[48,768]{1,0:T(8,128)(2,1)S(1)} %collective-permute-done.2), dimensions={1,2} | broadcast | bytes 663552 | tf_op jit(solution)/shard_map/broadcast_in_dim | solution.py:400
  27.2 5.8 %all-to-all-start = ((bf16[8,48,768]{2,1,0:T(8,128)(2,1)}), bf16[8,48,768]{2,1,0:T(8,128)(2,1)S(1)}, u32[]{:S(2)}, u32[]{:S(2)}) async-start(bf16[8,48,768]{2,1,0:T(8,128)(2,1)} %broadcast_in_dim.2), calls=%async_computation | async-start | bytes 1179648 | tf_op jit(solution)/shard_map/all_to_all | solution.py:399
  33.0 3.2 %collective-permute-start.5 = (bf16[96,768]{1,0:T(8,128)(2,1)S(1)}, bf16[96,768]{1,0:T(8,128)(2,1)S(1)}, u32[]{:S(2)}, u32[]{:S(2)}) collective-permute-start(bf16[96,768]{1,0:T(8,128)(2,1)S(1)} %pad_maximum_fusion.1.own_ref), channel_id=1, source_target_pairs={{0,3},{1,0},{2,1},{3,2},{4,7},{5,4},{6,5},{7,6},{8,11},{9,8},{10,9... | collective-permute-start | bytes 442376 | tf_op jit(solution)/shard_map/ppermute | solution.py:404
  36.2 3.6 %collective-permute-done.4.after_ref = bf16[96,768]{1,0:T(8,128)(2,1)S(1)} collective-permute-done((bf16[96,768]{1,0:T(8,128)(2,1)S(1)}, bf16[96,768]{1,0:T(8,128)(2,1)S(1)}, u32[]{:S(2)}, u32[]{:S(2)}) %collective-permute-start.4) | collective-permute-done | bytes 147488 | tf_op jit(solution)/shard_map/ppermute | solution.py:404
  39.8 1.9 %collective-permute-done.5.before_ref = bf16[96,768]{1,0:T(8,128)(2,1)S(1)} collective-permute-done((bf16[96,768]{1,0:T(8,128)(2,1)S(1)}, bf16[96,768]{1,0:T(8,128)(2,1)S(1)}, u32[]{:S(2)}, u32[]{:S(2)}) %collective-permute-start.5) | collective-permute-done | bytes 147488 | tf_op jit(solution)/shard_map/ppermute | solution.py:404
  41.7 1.3 %collective-permute-done.6.far_ref = bf16[96,768]{1,0:T(8,128)(2,1)S(1)} collective-permute-done((bf16[96,768]{1,0:T(8,128)(2,1)S(1)}, bf16[96,768]{1,0:T(8,128)(2,1)S(1)}, u32[]{:S(2)}, u32[]{:S(2)}) %collective-permute-start.6) | collective-permute-done | bytes 147488 | tf_op jit(solution)/shard_map/ppermute | solution.py:404
  43.0 0.0 collective-permute-start.7
  43.0 4.5 %shard_map.124 = (bf16[8,384,128]{2,1,0:T(8,128)(2,1)S(1)}, f32[48,768]{1,0:T(8,128)S(1)}, bf16[8,384,128]{2,1,0:T(8,128)(2,1)S(1)}, bf16[8,384,128]{2,1,0:T(8,128)(2,1)S(1)}, bf16[2,768,768]{2,1,0:T(8,128)(2,1)S(1)}) custom-call(bf16[96,768]{1,0:T(8,128)(2,1)S(1)} %pad_maximum_fusion.1.own_ref, bf16[96,768]{1,0:T(8,128)(2,1)S(1)} %collective-permute-done.4.after_ref, ...), custom_call_target="tpu_custom_call" | custom-call | flops 1000000 | bytes 100000 | tf_op jit(solution)/shard_map/pallas_call | solution.py:414
  47.5 10.3 %shard_map.125 = bf16[384,896]{1,0:T(8,128)(2,1)S(1)} custom-call(bf16[8,384,128]{2,1,0:T(8,128)(2,1)S(1)} %get-tuple-element.33.q_ref, bf16[8,384,128]{2,1,0:T(8,128)(2,1)S(1)} %get-tuple-element.34.k_ref, bf16[8,384,128]{2,1,0:T(8,128)(2,1)S(1)} %get-tuple-element.35.v_ref, bf16[8,48,768]{2,1,0:T(8,128)(2,1)S(1)} %collective-permute-done.7.blocks_ref, ...), custom_call_target="tpu_custom_call" | custom-call | flops 6000000000 | bytes 14000000 | tf_op jit(solution)/shard_map/pallas_call | solution.py:428
  57.8 0.0 copy-start
  57.9 0.0 copy-start.2
  57.9 17.8 %all_to_all.10.part_ref = bf16[8,48,896]{2,1,0:T(8,128)(2,1)S(1)} all-to-all(bf16[8,48,896]{2,1,0:T(8,128)(2,1)S(1)} %bitcast.3), channel_id=1, replica_groups=mesh['row'=16,'col'=8] {'col'}, dimensions={0} | all-to-all | bytes 1376256 | tf_op jit(solution)/shard_map/all_to_all | solution.py:441
  75.7 1.9 %shard_map.126 = (bf16[384,128]{1,0:T(8,128)(2,1)}, bf16[48,768]{1,0:T(8,128)(2,1)}) custom-call(bf16[8,48,896]{2,1,0:T(8,128)(2,1)S(1)} %all_to_all.10.part_ref, f32[48,768]{1,0:T(8,128)S(1)} %get-tuple-element.37.gate_ref, f32[48,768]{1,0:T(8,128)S(1)} %get-tuple-element.38.single_ref, f32[384,128]{1,0:T(8,128)S(1)} %get-tuple-element.39.mid_ref, ...), custom_call_target="tpu_custom_call" | custom-call | flops 400000000 | bytes 5000000 | tf_op jit(solution)/shard_map/pallas_call | solution.py:442
  (14 shorter events, 0.0 us)
Async XLA Ops:
  0.6 10.3 %copy-start.3 = (bf16[48,768]{1,0:T(8,128)(2,1)S(1)}, bf16[48,768]{1,0:T(8,128)(2,1)}, u32[]{:S(2)}) copy-start(bf16[48,768]{1,0:T(8,128)(2,1)} %input_ref.1) | copy-start | bytes 221188
  0.6 10.3 %copy-start.4 = (s32[1,384]{1,0:T(1,128)S(1)}, s32[1,384]{1,0:T(1,128)}, u32[]{:S(2)}) copy-start(s32[1,384]{1,0:T(1,128)} %owner_ref.3) | copy-start | bytes 4612
  0.7 10.3 %copy-start.1 = (bf16[128,768]{1,0:T(8,128)(2,1)S(1)}, bf16[128,768]{1,0:T(8,128)(2,1)}, u32[]{:S(2)}) copy-start(bf16[128,768]{1,0:T(8,128)(2,1)} %pool_ref.1) | copy-start | bytes 589828
  1.4 9.1 %collective-permute-start = (bf16[48,128]{1,0:T(8,128)(2,1)S(1)}, bf16[48,128]{1,0:T(8,128)(2,1)S(1)}, u32[]{:S(2)}, u32[]{:S(2)}) collective-permute-start(bf16[48,128]{1,0:T(8,128)(2,1)S(1)} %get-tuple-element.41), channel_id=1, source_target_pairs={{0,1},{1,2},{2,3},{3,4},{4,5},{5,6},{6,7},{7,8},{8,9},{9,10},{10,1... | collective-permute-start | bytes 36872 | tf_op jit(solution)/shard_map/ppermute | solution.py:362
  5.3 5.6 %collective-permute-start.1 = (bf16[48,128]{1,0:T(8,128)(2,1)S(1)}, bf16[48,128]{1,0:T(8,128)(2,1)S(1)}, u32[]{:S(2)}, u32[]{:S(2)}) collective-permute-start(bf16[48,128]{1,0:T(8,128)(2,1)S(1)} %get-tuple-element.40), channel_id=1, source_target_pairs={{1,0},{2,1},{3,2},{4,3},{5,4},{6,5},{7,6},{8,7},{9,8},{10,9},{11,1... | collective-permute-start | bytes 36872 | tf_op jit(solution)/shard_map/ppermute | solution.py:365
  13.3 10.3 %collective-permute-start.3 = (bf16[48,768]{1,0:T(8,128)(2,1)S(1)}, bf16[48,768]{1,0:T(8,128)(2,1)S(1)}, u32[]{:S(2)}, u32[]{:S(2)}) collective-permute-start(bf16[48,768]{1,0:T(8,128)(2,1)S(1)} %get-tuple-element.26.norm_ref), channel_id=1, source_target_pairs={{0,4},{1,5},{2,6},{3,7},{4,0},{5,1},{6,2},{7,3},{8,12},{9,13},{10,... | collective-permute-start | bytes 221192 | tf_op jit(solution)/shard_map/ppermute | solution.py:395
  20.4 5.9 %collective-permute-start.2 = (bf16[48,768]{1,0:T(8,128)(2,1)S(1)}, bf16[48,768]{1,0:T(8,128)(2,1)S(1)}, u32[]{:S(2)}, u32[]{:S(2)}) collective-permute-start(bf16[48,768]{1,0:T(8,128)(2,1)S(1)} %get-tuple-element.26.norm_ref), channel_id=1, source_target_pairs={{0,32},{1,48},{2,0},{3,16},{4,96},{5,112},{6,64},{7,80},{8,40},{9,... | collective-permute-start | bytes 221192 | tf_op jit(solution)/shard_map/ppermute | solution.py:394
  27.2 15.9 %all-to-all-start = ((bf16[8,48,768]{2,1,0:T(8,128)(2,1)}), bf16[8,48,768]{2,1,0:T(8,128)(2,1)S(1)}, u32[]{:S(2)}, u32[]{:S(2)}) async-start(bf16[8,48,768]{2,1,0:T(8,128)(2,1)} %broadcast_in_dim.2), calls=%async_computation | async-start | bytes 1179648 | tf_op jit(solution)/shard_map/all_to_all | solution.py:399
  33.0 6.8 %collective-permute-start.4 = (bf16[96,768]{1,0:T(8,128)(2,1)S(1)}, bf16[96,768]{1,0:T(8,128)(2,1)S(1)}, u32[]{:S(2)}, u32[]{:S(2)}) collective-permute-start(bf16[96,768]{1,0:T(8,128)(2,1)S(1)} %pad_maximum_fusion.1.own_ref), channel_id=1, source_target_pairs={{0,1},{1,2},{2,3},{3,0},{4,5},{5,6},{6,7},{7,4},{8,9},{9,10},{10,1... | collective-permute-start | bytes 442376 | tf_op jit(solution)/shard_map/ppermute | solution.py:404
  33.0 8.7 %collective-permute-start.5 = (bf16[96,768]{1,0:T(8,128)(2,1)S(1)}, bf16[96,768]{1,0:T(8,128)(2,1)S(1)}, u32[]{:S(2)}, u32[]{:S(2)}) collective-permute-start(bf16[96,768]{1,0:T(8,128)(2,1)S(1)} %pad_maximum_fusion.1.own_ref), channel_id=1, source_target_pairs={{0,3},{1,0},{2,1},{3,2},{4,7},{5,4},{6,5},{7,6},{8,11},{9,8},{10,9... | collective-permute-start | bytes 442376 | tf_op jit(solution)/shard_map/ppermute | solution.py:404
  36.2 6.8 %collective-permute-start.6 = (bf16[96,768]{1,0:T(8,128)(2,1)S(1)}, bf16[96,768]{1,0:T(8,128)(2,1)S(1)}, u32[]{:S(2)}, u32[]{:S(2)}) collective-permute-start(bf16[96,768]{1,0:T(8,128)(2,1)S(1)} %pad_maximum_fusion.1.own_ref), channel_id=1, source_target_pairs={{0,2},{1,3},{2,0},{3,1},{4,6},{5,7},{6,4},{7,5},{8,10},{9,11},{10,... | collective-permute-start | bytes 442376 | tf_op jit(solution)/shard_map/ppermute | solution.py:404
  43.0 4.5 %collective-permute-start.7 = (bf16[8,48,768]{2,1,0:T(8,128)(2,1)S(1)}, bf16[8,48,768]{2,1,0:T(8,128)(2,1)S(1)}, u32[]{:S(2)}, u32[]{:S(2)}) collective-permute-start(bf16[8,48,768]{2,1,0:T(8,128)(2,1)S(1)} %all-to-all-done.blocks_ref), channel_id=1, source_target_pairs={{0,8},{8,0},{16,24},{24,16},{32,40},{40,32},{48,56},{56,48},{64,72... | collective-permute-start | bytes 1769480 | tf_op jit(solution)/shard_map/ppermute | solution.py:410
  57.8 17.8 %copy-start = (bf16[768,768]{1,0:T(8,128)(2,1)S(1)}, bf16[768,768]{1,0:T(8,128)(2,1)}, u32[]{:S(2)}) copy-start(bf16[768,768]{1,0:T(8,128)(2,1)} %output_ref.1) | copy-start | bytes 3538948
  57.9 17.8 %copy-start.2 = (bf16[768,128]{1,0:T(8,128)(2,1)S(1)}, bf16[768,128]{1,0:T(8,128)(2,1)}, u32[]{:S(2)}) copy-start(bf16[768,128]{1,0:T(8,128)(2,1)} %back_ref.1) | copy-start | bytes 589828

commit v10 on v9

--- a/solution.py
+++ b/solution.py
@@ -226,14 +226,24 @@
     store_pairs(v_ref, [jnp.where(mass, 1.0, band) for band in bands])
 
 
-def project_step(
-    own_ref, after_ref, before_ref, far_ref, norm_ref, blocks_ref, proj_hbm, q_ref, gate_ref,
-    k_ref, v_ref, key_ref, edge_ref, sems,
+def near_step(blocks_ref, proj_hbm, k_ref, v_ref, key_ref, sems):
+    copies = [
+        pltpu.make_async_copy(proj_hbm.at[1 + i], key_ref.at[i], sems.at[i]) for i in range(2)
+    ]
+    for copy in copies:
+        copy.start()
+    into = places()
+    copies[0].wait()
+    key_rows(blocks_ref, key_ref[0], into, k_ref)
+    copies[1].wait()
+    value_rows(blocks_ref, key_ref[1], into, v_ref)
+
+
+def query_step(
+    own_ref, after_ref, before_ref, far_ref, norm_ref, proj_hbm, q_ref, gate_ref, edge_ref, sems
 ):
-    targets = (edge_ref.at[0], key_ref.at[0], key_ref.at[1], edge_ref.at[1])
     copies = [
-        pltpu.make_async_copy(proj_hbm.at[i], target, sems.at[i])
-        for i, target in enumerate(targets)
+        pltpu.make_async_copy(proj_hbm.at[3 * i], edge_ref.at[i], sems.at[i]) for i in range(2)
     ]
     for copy in copies:
         copy.start()
@@ -243,10 +253,6 @@
         [own_ref[...], after_ref[...], before_ref[...], far_ref[...]], edge_ref[0], into, q_ref
     )
     copies[1].wait()
-    key_rows(blocks_ref, key_ref[0], into, k_ref)
-    copies[2].wait()
-    value_rows(blocks_ref, key_ref[1], into, v_ref)
-    copies[3].wait()
     gate_ref[...] = jax.nn.sigmoid(dot(norm_ref[...], edge_ref[1]))
 
 
@@ -406,25 +412,31 @@
         )
         for step in (1, ring - 1, 2)
     ]
-    near, *along = lax.optimization_barrier((near, *along))
-    far = lax.ppermute(near, "row", [(i, i ^ 1) for i in range(rows)])
+    in_vmem, in_hbm = (pl.BlockSpec(memory_space=space) for space in (pltpu.VMEM, pltpu.HBM))
     q_count, half = cols * tokens, rows * tokens // 2
     lane = 2 * SLOT
-    in_vmem, in_hbm = (pl.BlockSpec(memory_space=space) for space in (pltpu.VMEM, pltpu.HBM))
-    queries, gates, near_k, near_v, key_weights = call(
-        project_step,
+    near_k, near_v, key_weights = call(
+        near_step,
         (
-            shape((PAIRS, q_count, lane), BF16),
-            shape((tokens, depth), F32),
             shape((PAIRS, half, lane), BF16),
             shape((PAIRS, half, lane), BF16),
             shape((2, depth, depth), BF16),
         ),
         MOST,
         SMALL,
-        in_specs=[in_vmem] * 6 + [in_hbm],
-        scratch_shapes=[pltpu.VMEM((2, depth, depth), BF16), pltpu.SemaphoreType.DMA((4,))],
-    )(own, *along, norm, near, token_proj)
+        in_specs=[in_vmem, in_hbm],
+        scratch_shapes=[pltpu.SemaphoreType.DMA((2,))],
+    )(near, token_proj)
+    near, near_k, near_v, *along = lax.optimization_barrier((near, near_k, near_v, *along))
+    far = lax.ppermute(near, "row", [(i, i ^ 1) for i in range(rows)])
+    queries, gates = call(
+        query_step,
+        (shape((PAIRS, q_count, lane), BF16), shape((tokens, depth), F32)),
+        MOST,
+        SMALL,
+        in_specs=[in_vmem] * 5 + [in_hbm],
+        scratch_shapes=[pltpu.VMEM((2, depth, depth), BF16), pltpu.SemaphoreType.DMA((2,))],
+    )(own, *along, norm, token_proj)
     parts = call(
         token_step,
         shape((q_count, wide), BF16),

time: 78.1 us -> 81.5 us (1.044)
  starting transfers between devices: 24.6 us -> 28.1 us
  waiting for transfers between devices: 9.81 us -> 7.57 us
  blocking collectives: 17.8 us -> 19.1 us
    ppermute x3, waiting for transfers between devices: 6.79 us -> 0.01 us  [per_device(): lax.ppermute(own, 'col', [(i, i // ring * ring + (i + step) % ring) for i...]
    all_to_all x1, waiting for transfers between devices: 0.01 us -> 4.87 us  [per_device(): lax.all_to_all(jnp.broadcast_to(turned[None], (rows // 2, tokens, depth))...]
    ppermute x1, starting transfers between devices: 7.12 us -> 8.46 us  [per_device(): lax.ppermute(norm, 'col', [(i, (i + ring) % cols) for i in range(cols)])]
    all_to_all x1, blocking collectives: 17.8 us -> 19.1 us  [per_device(): parts = lax.all_to_all(parts.reshape(cols, tokens, wide), 'col', 0, 0)]
    all_to_all x1, starting transfers between devices: 5.82 us -> 6.72 us  [per_device(): lax.all_to_all(jnp.broadcast_to(turned[None], (rows // 2, tokens, depth))...]
    pallas_call x1 -> x2, Pallas kernels: 4.47 us -> 5.22 us  [the longest x1 3.29 us: per_device(): call(near_step, (shape((PAIRS, half, lane), BF16), shape((PAIRS, half, la...]
  transfers between devices with their start and end apart: 9 -> 9, of which waited for: 5 -> 2; matrix products, arithmetic and copies ran while one was open for 1% -> 1% of each run, Pallas kernels for 9% -> 10%
where the time goes in v10:
time: 81.5 us; the launch traced here: 81.1 us
  starting transfers between devices  28.1 us (34%)
  Pallas kernels  22.7 us (28%)
  blocking collectives  19.1 us (23%)
  waiting for transfers between devices  7.57 us (9%)
  local copies, waits for them, and re-layouts  1.67 us (2%)
  other arithmetic  1.15 us (1%)
  between operations  0.82 us (1%)
    all_to_all x1, blocking collectives, per_device(): parts = lax.all_to_all(parts.reshape(cols, tokens, wide), 'col', 0, 0)  19.1 us
    pallas_call x1, Pallas kernels, per_device(): call(token_step, shape((q_count, wide), BF16), MOST, (6000000000, 1400000...  10.4 us
    ppermute x1, starting transfers between devices, per_device(): lax.ppermute(norm, 'col', [(i, (i + ring) % cols) for i in range(cols)])  8.46 us
    all_to_all x1, starting transfers between devices, per_device(): lax.all_to_all(jnp.broadcast_to(turned[None], (rows // 2, tokens, depth))...  6.72 us
    all_to_all x1, waiting for transfers between devices, per_device(): lax.all_to_all(jnp.broadcast_to(turned[None], (rows // 2, tokens, depth))...  4.87 us
    ppermute x1, starting transfers between devices, per_device(): lax.ppermute(atom_state[count - REACH:], BOTH, [(i, i + 1) for i in range...  4.55 us
    ppermute x3, starting transfers between devices, per_device(): lax.ppermute(own, 'col', [(i, i // ring * ring + (i + step) % ring) for i...  3.67 us
    pallas_call x1, Pallas kernels, per_device(): call(near_step, (shape((PAIRS, half, lane), BF16), shape((PAIRS, half, la...  3.29 us
  transfers between devices with their start and end apart: 9, of which 2 were waited for; matrix products, arithmetic and copies ran while one was open for 1% of the time, Pallas kernels for 10%

profile of v10, /device:TPU:0, one launch (start us, length us, event | category | flops | bytes accessed | tf_op | source)
XLA Modules:
  0.0 81.1 jit_solution(1078570064003539871)
XLA Ops:
  0.7 0.8 fusion
  1.4 1.3 %collective-permute-start.1 = (bf16[48,128]{1,0:T(8,128)(2,1)S(1)}, bf16[48,128]{1,0:T(8,128)(2,1)S(1)}, u32[]{:S(2)}, u32[]{:S(2)}) collective-permute-start(bf16[48,128]{1,0:T(8,128)(2,1)S(1)} %get-tuple-element.44), channel_id=1, source_target_pairs={{1,0},{2,1},{3,2},{4,3},{5,4},{6,5},{7,6},{8,7},{9,8},{10,9},{11,1... | collective-permute-start | bytes 36872 | tf_op jit(solution)/shard_map/ppermute | solution.py:371
  2.7 4.5 %collective-permute-start = (bf16[48,128]{1,0:T(8,128)(2,1)S(1)}, bf16[48,128]{1,0:T(8,128)(2,1)S(1)}, u32[]{:S(2)}, u32[]{:S(2)}) collective-permute-start(bf16[48,128]{1,0:T(8,128)(2,1)S(1)} %get-tuple-element.45), channel_id=1, source_target_pairs={{0,1},{1,2},{2,3},{3,4},{4,5},{5,6},{6,7},{7,8},{8,9},{9,10},{10,1... | collective-permute-start | bytes 36872 | tf_op jit(solution)/shard_map/ppermute | solution.py:368
  7.3 1.1 %pad_maximum_fusion.narrow_ref = bf16[2560,128]{1,0:T(8,128)(2,1)S(1)} fusion(bf16[128,128]{1,0:T(8,128)(2,1)} %param.17, bf16[512,128]{1,0:T(8,128)(2,1)} %bitcast.5, bf16[1536,128]{1,0:T(8,128)(2,1)} %bitcast.4, bf16[384,128]{1,0:T(8,128)(2,1)} %param.11), kind=kLoop, calls=%fused_computation | loop fusion | flops 2621440 | bytes 1310720 | tf_op jit(solution)/shard_map/concatenate | solution.py:372
  8.4 2.8 %shard_map.122 = (bf16[384,128]{1,0:T(8,128)(2,1)S(1)}, bf16[384,128]{1,0:T(8,128)(2,1)S(1)}, bf16[384,128]{1,0:T(8,128)(2,1)S(1)}, f32[384,128]{1,0:T(8,128)S(1)}, bf16[256,128]{1,0:T(8,128)(2,1)S(1)}) custom-call(bf16[2560,128]{1,0:T(8,128)(2,1)S(1)} %pad_maximum_fusion.narrow_ref), custom_call_target="tpu_custom_call" | custom-call | flops 200000000 | bytes 1000000 | tf_op jit(solution)/shard_map/pallas_call | solution.py:377
  11.2 2.4 %shard_map.123 = (f32[384,128]{1,0:T(8,128)S(1)}, f32[48,768]{1,0:T(8,128)S(1)}, bf16[48,768]{1,0:T(8,128)(2,1)S(1)}) custom-call(bf16[48,128]{1,0:T(8,128)(2,1)S(1)} %collective-permute-done.left_ref, bf16[48,128]{1,0:T(8,128)(2,1)S(1)} %collective-permute-done.1.right_ref, bf16[2560,128]{1,0:T(8,128)(2,1)S(1)} %pad_maximum_fusion.narrow_ref, ...), custom_call_target="tpu_custom_call" | custom-call | flops 200000000 | bytes 2000000 | tf_op jit(solution)/shard_map/pallas_call | solution.py:384
  13.6 8.5 %collective-permute-start.3 = (bf16[48,768]{1,0:T(8,128)(2,1)S(1)}, bf16[48,768]{1,0:T(8,128)(2,1)S(1)}, u32[]{:S(2)}, u32[]{:S(2)}) collective-permute-start(bf16[48,768]{1,0:T(8,128)(2,1)S(1)} %get-tuple-element.28.norm_ref), channel_id=1, source_target_pairs={{0,4},{1,5},{2,6},{3,7},{4,0},{5,1},{6,2},{7,3},{8,12},{9,13},{10,... | collective-permute-start | bytes 221192 | tf_op jit(solution)/shard_map/ppermute | solution.py:401
  22.1 3.2 %collective-permute-start.2 = (bf16[48,768]{1,0:T(8,128)(2,1)S(1)}, bf16[48,768]{1,0:T(8,128)(2,1)S(1)}, u32[]{:S(2)}, u32[]{:S(2)}) collective-permute-start(bf16[48,768]{1,0:T(8,128)(2,1)S(1)} %get-tuple-element.28.norm_ref), channel_id=1, source_target_pairs={{0,32},{1,48},{2,0},{3,16},{4,96},{5,112},{6,64},{7,80},{8,40},{9,... | collective-permute-start | bytes 221192 | tf_op jit(solution)/shard_map/ppermute | solution.py:400
  25.3 2.6 %collective-permute-done.2 = bf16[48,768]{1,0:T(8,128)(2,1)S(1)} collective-permute-done((bf16[48,768]{1,0:T(8,128)(2,1)S(1)}, bf16[48,768]{1,0:T(8,128)(2,1)S(1)}, u32[]{:S(2)}, u32[]{:S(2)}) %collective-permute-start.2) | collective-permute-done | bytes 73760 | tf_op jit(solution)/shard_map/ppermute | solution.py:400
  27.9 0.9 %broadcast_in_dim.2 = bf16[8,48,768]{2,1,0:T(8,128)(2,1)} broadcast(bf16[48,768]{1,0:T(8,128)(2,1)S(1)} %collective-permute-done.2), dimensions={1,2} | broadcast | bytes 663552 | tf_op jit(solution)/shard_map/broadcast_in_dim | solution.py:406
  28.8 6.7 %all-to-all-start = ((bf16[8,48,768]{2,1,0:T(8,128)(2,1)}), bf16[8,48,768]{2,1,0:T(8,128)(2,1)S(1)}, u32[]{:S(2)}, u32[]{:S(2)}) async-start(bf16[8,48,768]{2,1,0:T(8,128)(2,1)} %broadcast_in_dim.2), calls=%async_computation | async-start | bytes 1179648 | tf_op jit(solution)/shard_map/all_to_all | solution.py:405
  35.5 1.6 %collective-permute-start.6 = (bf16[96,768]{1,0:T(8,128)(2,1)S(1)}, bf16[96,768]{1,0:T(8,128)(2,1)S(1)}, u32[]{:S(2)}, u32[]{:S(2)}) collective-permute-start(bf16[96,768]{1,0:T(8,128)(2,1)S(1)} %pad_maximum_fusion.1.own_ref), channel_id=1, source_target_pairs={{0,2},{1,3},{2,0},{3,1},{4,6},{5,7},{6,4},{7,5},{8,10},{9,11},{10,... | collective-permute-start | bytes 442376 | tf_op jit(solution)/shard_map/ppermute | solution.py:410
  37.2 1.2 %collective-permute-start.5 = (bf16[96,768]{1,0:T(8,128)(2,1)S(1)}, bf16[96,768]{1,0:T(8,128)(2,1)S(1)}, u32[]{:S(2)}, u32[]{:S(2)}) collective-permute-start(bf16[96,768]{1,0:T(8,128)(2,1)S(1)} %pad_maximum_fusion.1.own_ref), channel_id=1, source_target_pairs={{0,3},{1,0},{2,1},{3,2},{4,7},{5,4},{6,5},{7,6},{8,11},{9,8},{10,9... | collective-permute-start | bytes 442376 | tf_op jit(solution)/shard_map/ppermute | solution.py:410
  38.3 0.9 %collective-permute-start.4 = (bf16[96,768]{1,0:T(8,128)(2,1)S(1)}, bf16[96,768]{1,0:T(8,128)(2,1)S(1)}, u32[]{:S(2)}, u32[]{:S(2)}) collective-permute-start(bf16[96,768]{1,0:T(8,128)(2,1)S(1)} %pad_maximum_fusion.1.own_ref), channel_id=1, source_target_pairs={{0,1},{1,2},{2,3},{3,0},{4,5},{5,6},{6,7},{7,4},{8,9},{9,10},{10,1... | collective-permute-start | bytes 442376 | tf_op jit(solution)/shard_map/ppermute | solution.py:410
  39.2 4.9 %all-to-all-done.blocks_ref = bf16[8,48,768]{2,1,0:T(8,128)(2,1)S(1)} async-done(((bf16[8,48,768]{2,1,0:T(8,128)(2,1)}), bf16[8,48,768]{2,1,0:T(8,128)(2,1)S(1)}, u32[]{:S(2)}, u32[]{:S(2)}) %all-to-all-start) | async-done | bytes 589856 | tf_op jit(solution)/shard_map/all_to_all | solution.py:405
  44.1 3.3 %shard_map.124 = (bf16[8,384,128]{2,1,0:T(8,128)(2,1)S(1)}, bf16[8,384,128]{2,1,0:T(8,128)(2,1)S(1)}, bf16[2,768,768]{2,1,0:T(8,128)(2,1)S(1)}) custom-call(bf16[8,48,768]{2,1,0:T(8,128)(2,1)S(1)} %all-to-all-done.blocks_ref, bf16[4,768,768]{2,1,0:T(8,128)(2,1)} %proj_hbm.3), custom_call_target="tpu_custom_call" | custom-call | flops 1000000 | bytes 100000 | tf_op jit(solution)/shard_map/pallas_call | solution.py:418
  47.4 0.3 collective-permute-start.7
  47.7 1.9 %shard_map.125 = (bf16[8,384,128]{2,1,0:T(8,128)(2,1)S(1)}, f32[48,768]{1,0:T(8,128)S(1)}) custom-call(bf16[96,768]{1,0:T(8,128)(2,1)S(1)} %pad_maximum_fusion.1.own_ref, bf16[96,768]{1,0:T(8,128)(2,1)S(1)} %collective-permute-done.4.after_ref, bf16[96,768]{1,0:T(8,128)(2,1)S(1)} %collective-permute-done.5.before_ref, ...), custom_call_target="tpu_custom_call" | custom-call | flops 1000000 | bytes 100000 | tf_op jit(solution)/shard_map/pallas_call | solution.py:432
  49.6 0.0 collective-permute-done.7.blocks_ref
  49.7 10.4 %shard_map.126 = bf16[384,896]{1,0:T(8,128)(2,1)S(1)} custom-call(bf16[8,384,128]{2,1,0:T(8,128)(2,1)S(1)} %get-tuple-element.36.q_ref, bf16[8,384,128]{2,1,0:T(8,128)(2,1)S(1)} %get-tuple-element.37.k_ref, bf16[8,384,128]{2,1,0:T(8,128)(2,1)S(1)} %get-tuple-element.38.v_ref, bf16[8,48,768]{2,1,0:T(8,128)(2,1)S(1)} %collective-permute-done.7.blocks_ref, ...), custom_call_target="tpu_custom_call" | custom-call | flops 6000000000 | bytes 14000000 | tf_op jit(solution)/shard_map/pallas_call | solution.py:440
  60.1 0.0 copy-start.1
  60.1 0.0 copy-start.3
  60.1 19.1 %all_to_all.10.part_ref = bf16[8,48,896]{2,1,0:T(8,128)(2,1)S(1)} all-to-all(bf16[8,48,896]{2,1,0:T(8,128)(2,1)S(1)} %bitcast.3), channel_id=1, replica_groups=mesh['row'=16,'col'=8] {'col'}, dimensions={0} | all-to-all | bytes 1376256 | tf_op jit(solution)/shard_map/all_to_all | solution.py:453
  79.2 1.9 %shard_map.127 = (bf16[384,128]{1,0:T(8,128)(2,1)}, bf16[48,768]{1,0:T(8,128)(2,1)}) custom-call(bf16[8,48,896]{2,1,0:T(8,128)(2,1)S(1)} %all_to_all.10.part_ref, f32[48,768]{1,0:T(8,128)S(1)} %get-tuple-element.41.gate_ref, f32[48,768]{1,0:T(8,128)S(1)} %get-tuple-element.42.single_ref, f32[384,128]{1,0:T(8,128)S(1)} %get-tuple-element.43.mid_ref, ...), custom_call_target="tpu_custom_call" | custom-call | flops 400000000 | bytes 5000000 | tf_op jit(solution)/shard_map/pallas_call | solution.py:454
  (17 shorter events, 0.0 us)
Async XLA Ops:
  0.6 10.6 %copy-start.5 = (s32[1,384]{1,0:T(1,128)S(1)}, s32[1,384]{1,0:T(1,128)}, u32[]{:S(2)}) copy-start(s32[1,384]{1,0:T(1,128)} %owner_ref.3) | copy-start | bytes 4612
  0.6 10.6 %copy-start.2 = (bf16[128,768]{1,0:T(8,128)(2,1)S(1)}, bf16[128,768]{1,0:T(8,128)(2,1)}, u32[]{:S(2)}) copy-start(bf16[128,768]{1,0:T(8,128)(2,1)} %pool_ref.1) | copy-start | bytes 589828
  0.7 10.6 %copy-start.4 = (bf16[48,768]{1,0:T(8,128)(2,1)S(1)}, bf16[48,768]{1,0:T(8,128)(2,1)}, u32[]{:S(2)}) copy-start(bf16[48,768]{1,0:T(8,128)(2,1)} %input_ref.1) | copy-start | bytes 221188
  1.4 9.8 %collective-permute-start.1 = (bf16[48,128]{1,0:T(8,128)(2,1)S(1)}, bf16[48,128]{1,0:T(8,128)(2,1)S(1)}, u32[]{:S(2)}, u32[]{:S(2)}) collective-permute-start(bf16[48,128]{1,0:T(8,128)(2,1)S(1)} %get-tuple-element.44), channel_id=1, source_target_pairs={{1,0},{2,1},{3,2},{4,3},{5,4},{6,5},{7,6},{8,7},{9,8},{10,9},{11,1... | collective-permute-start | bytes 36872 | tf_op jit(solution)/shard_map/ppermute | solution.py:371
  2.7 8.5 %collective-permute-start = (bf16[48,128]{1,0:T(8,128)(2,1)S(1)}, bf16[48,128]{1,0:T(8,128)(2,1)S(1)}, u32[]{:S(2)}, u32[]{:S(2)}) collective-permute-start(bf16[48,128]{1,0:T(8,128)(2,1)S(1)} %get-tuple-element.45), channel_id=1, source_target_pairs={{0,1},{1,2},{2,3},{3,4},{4,5},{5,6},{6,7},{7,8},{8,9},{9,10},{10,1... | collective-permute-start | bytes 36872 | tf_op jit(solution)/shard_map/ppermute | solution.py:368
  13.6 11.7 %collective-permute-start.3 = (bf16[48,768]{1,0:T(8,128)(2,1)S(1)}, bf16[48,768]{1,0:T(8,128)(2,1)S(1)}, u32[]{:S(2)}, u32[]{:S(2)}) collective-permute-start(bf16[48,768]{1,0:T(8,128)(2,1)S(1)} %get-tuple-element.28.norm_ref), channel_id=1, source_target_pairs={{0,4},{1,5},{2,6},{3,7},{4,0},{5,1},{6,2},{7,3},{8,12},{9,13},{10,... | collective-permute-start | bytes 221192 | tf_op jit(solution)/shard_map/ppermute | solution.py:401
  22.1 5.9 %collective-permute-start.2 = (bf16[48,768]{1,0:T(8,128)(2,1)S(1)}, bf16[48,768]{1,0:T(8,128)(2,1)S(1)}, u32[]{:S(2)}, u32[]{:S(2)}) collective-permute-start(bf16[48,768]{1,0:T(8,128)(2,1)S(1)} %get-tuple-element.28.norm_ref), channel_id=1, source_target_pairs={{0,32},{1,48},{2,0},{3,16},{4,96},{5,112},{6,64},{7,80},{8,40},{9,... | collective-permute-start | bytes 221192 | tf_op jit(solution)/shard_map/ppermute | solution.py:400
  28.8 15.3 %all-to-all-start = ((bf16[8,48,768]{2,1,0:T(8,128)(2,1)}), bf16[8,48,768]{2,1,0:T(8,128)(2,1)S(1)}, u32[]{:S(2)}, u32[]{:S(2)}) async-start(bf16[8,48,768]{2,1,0:T(8,128)(2,1)} %broadcast_in_dim.2), calls=%async_computation | async-start | bytes 1179648 | tf_op jit(solution)/shard_map/all_to_all | solution.py:405
  35.5 11.8 %collective-permute-start.6 = (bf16[96,768]{1,0:T(8,128)(2,1)S(1)}, bf16[96,768]{1,0:T(8,128)(2,1)S(1)}, u32[]{:S(2)}, u32[]{:S(2)}) collective-permute-start(bf16[96,768]{1,0:T(8,128)(2,1)S(1)} %pad_maximum_fusion.1.own_ref), channel_id=1, source_target_pairs={{0,2},{1,3},{2,0},{3,1},{4,6},{5,7},{6,4},{7,5},{8,10},{9,11},{10,... | collective-permute-start | bytes 442376 | tf_op jit(solution)/shard_map/ppermute | solution.py:410
  37.2 10.2 %collective-permute-start.5 = (bf16[96,768]{1,0:T(8,128)(2,1)S(1)}, bf16[96,768]{1,0:T(8,128)(2,1)S(1)}, u32[]{:S(2)}, u32[]{:S(2)}) collective-permute-start(bf16[96,768]{1,0:T(8,128)(2,1)S(1)} %pad_maximum_fusion.1.own_ref), channel_id=1, source_target_pairs={{0,3},{1,0},{2,1},{3,2},{4,7},{5,4},{6,5},{7,6},{8,11},{9,8},{10,9... | collective-permute-start | bytes 442376 | tf_op jit(solution)/shard_map/ppermute | solution.py:410
  38.3 9.1 %collective-permute-start.4 = (bf16[96,768]{1,0:T(8,128)(2,1)S(1)}, bf16[96,768]{1,0:T(8,128)(2,1)S(1)}, u32[]{:S(2)}, u32[]{:S(2)}) collective-permute-start(bf16[96,768]{1,0:T(8,128)(2,1)S(1)} %pad_maximum_fusion.1.own_ref), channel_id=1, source_target_pairs={{0,1},{1,2},{2,3},{3,0},{4,5},{5,6},{6,7},{7,4},{8,9},{9,10},{10,1... | collective-permute-start | bytes 442376 | tf_op jit(solution)/shard_map/ppermute | solution.py:410
  44.1 3.6 %copy-start = (bf16[4,768,768]{2,1,0:T(8,128)(2,1)S(1)}, bf16[4,768,768]{2,1,0:T(8,128)(2,1)}, u32[]{:S(2)}) copy-start(bf16[4,768,768]{2,1,0:T(8,128)(2,1)} %proj_hbm.3) | copy-start | bytes 14155780
  47.4 2.3 %collective-permute-start.7 = (bf16[8,48,768]{2,1,0:T(8,128)(2,1)S(1)}, bf16[8,48,768]{2,1,0:T(8,128)(2,1)S(1)}, u32[]{:S(2)}, u32[]{:S(2)}) collective-permute-start(bf16[8,48,768]{2,1,0:T(8,128)(2,1)S(1)} %all-to-all-done.blocks_ref), channel_id=1, source_target_pairs={{0,8},{8,0},{16,24},{24,16},{32,40},{40,32},{48,56},{56,48},{64,72... | collective-permute-start | bytes 1769480 | tf_op jit(solution)/shard_map/ppermute | solution.py:431
  60.1 19.1 %copy-start.1 = (bf16[768,768]{1,0:T(8,128)(2,1)S(1)}, bf16[768,768]{1,0:T(8,128)(2,1)}, u32[]{:S(2)}) copy-start(bf16[768,768]{1,0:T(8,128)(2,1)} %output_ref.1) | copy-start | bytes 3538948
  60.1 19.1 %copy-start.3 = (bf16[768,128]{1,0:T(8,128)(2,1)S(1)}, bf16[768,128]{1,0:T(8,128)(2,1)}, u32[]{:S(2)}) copy-start(bf16[768,128]{1,0:T(8,128)(2,1)} %back_ref.1) | copy-start | bytes 589828

commit v11 on v10

--- a/solution.py
+++ b/solution.py
@@ -152,7 +152,7 @@
 
 
 def atom_step(
-    left_ref, right_ref, narrow_ref, pool_ref, input_ref, owner_ref, q_ref, k_ref, v_ref,
+    right_ref, left_ref, narrow_ref, pool_ref, input_ref, owner_ref, q_ref, k_ref, v_ref,
     gate_ref, gated_ref, mid_ref, single_ref, norm_ref,
 ):
     count = owner_ref.shape[1]
@@ -240,7 +240,7 @@
 
 
 def query_step(
-    own_ref, after_ref, before_ref, far_ref, norm_ref, proj_hbm, q_ref, gate_ref, edge_ref, sems
+    own_ref, far_ref, before_ref, after_ref, norm_ref, proj_hbm, q_ref, gate_ref, edge_ref, sems
 ):
     copies = [
         pltpu.make_async_copy(proj_hbm.at[3 * i], edge_ref.at[i], sems.at[i]) for i in range(2)
@@ -390,7 +390,7 @@
         ),
         ATOM_MB,
         (200_000_000, 2_000_000),
-    )(left, right, narrow, pool_weight, token_input, atom_owner, *inner)
+    )(right, left, narrow, pool_weight, token_input, atom_owner, *inner)
     ring = cols // 2
     turn = []
     for r in range(rows):
@@ -427,7 +427,7 @@
         in_specs=[in_vmem, in_hbm],
         scratch_shapes=[pltpu.SemaphoreType.DMA((2,))],
     )(near, token_proj)
-    near, near_k, near_v, *along = lax.optimization_barrier((near, near_k, near_v, *along))
+    near, near_k, near_v, *along = lax.optimization_barrier((near, near_k, near_v, *along[::-1]))
     far = lax.ppermute(near, "row", [(i, i ^ 1) for i in range(rows)])
     queries, gates = call(
         query_step,

time: 81.5 us -> 78.5 us (0.963)
  starting transfers between devices: 28.1 us -> 24.8 us
  waiting for transfers between devices: 7.57 us -> 8.75 us
    ppermute x1, starting transfers between devices: 8.46 us -> 7.12 us  [per_device(): lax.ppermute(norm, 'col', [(i, (i + ring) % cols) for i in range(cols)])]
    all_to_all x1, starting transfers between devices: 6.72 us -> 5.82 us  [per_device(): lax.all_to_all(jnp.broadcast_to(turned[None], (rows // 2, tokens, depth))...]
    all_to_all x1, waiting for transfers between devices: 4.87 us -> 5.7 us  [per_device(): lax.all_to_all(jnp.broadcast_to(turned[None], (rows // 2, tokens, depth))...]
  transfers between devices with their start and end apart: 9 -> 9, of which waited for: 2 -> 3; matrix products, arithmetic and copies ran while one was open for 1% -> 1% of each run, Pallas kernels for 10% -> 10%
where the time goes in v11:
time: 78.5 us; the launch traced here: 78.2 us
  starting transfers between devices  24.8 us (32%)
  Pallas kernels  22.7 us (29%)
  blocking collectives  18.3 us (23%)
  waiting for transfers between devices  8.75 us (11%)
  local copies, waits for them, and re-layouts  1.67 us (2%)
  other arithmetic  1.15 us (1%)
  between operations  0.8 us (1%)
    all_to_all x1, blocking collectives, per_device(): parts = lax.all_to_all(parts.reshape(cols, tokens, wide), 'col', 0, 0)  18.3 us
    pallas_call x1, Pallas kernels, per_device(): call(token_step, shape((q_count, wide), BF16), MOST, (6000000000, 1400000...  10.4 us
    ppermute x1, starting transfers between devices, per_device(): lax.ppermute(norm, 'col', [(i, (i + ring) % cols) for i in range(cols)])  7.12 us
    all_to_all x1, starting transfers between devices, per_device(): lax.all_to_all(jnp.broadcast_to(turned[None], (rows // 2, tokens, depth))...  5.82 us
    all_to_all x1, waiting for transfers between devices, per_device(): lax.all_to_all(jnp.broadcast_to(turned[None], (rows // 2, tokens, depth))...  5.7 us
    ppermute x1, starting transfers between devices, per_device(): lax.ppermute(atom_state[count - REACH:], BOTH, [(i, i + 1) for i in range...  3.89 us
    pallas_call x1, Pallas kernels, per_device(): call(near_step, (shape((PAIRS, half, lane), BF16), shape((PAIRS, half, la...  3.29 us
    ppermute x3, starting transfers between devices, per_device(): lax.ppermute(own, 'col', [(i, i // ring * ring + (i + step) % ring) for i...  3.23 us
  transfers between devices with their start and end apart: 9, of which 3 were waited for; matrix products, arithmetic and copies ran while one was open for 1% of the time, Pallas kernels for 10%

profile of v11, /device:TPU:0, one launch (start us, length us, event | category | flops | bytes accessed | tf_op | source)
XLA Modules:
  0.0 78.2 jit_solution(18030791590988248967)
XLA Ops:
  0.7 0.8 fusion
  1.4 3.9 %collective-permute-start.1 = (bf16[48,128]{1,0:T(8,128)(2,1)S(1)}, bf16[48,128]{1,0:T(8,128)(2,1)S(1)}, u32[]{:S(2)}, u32[]{:S(2)}) collective-permute-start(bf16[48,128]{1,0:T(8,128)(2,1)S(1)} %get-tuple-element.44), channel_id=1, source_target_pairs={{0,1},{1,2},{2,3},{3,4},{4,5},{5,6},{6,7},{7,8},{8,9},{9,10},{10,1... | collective-permute-start | bytes 36872 | tf_op jit(solution)/shard_map/ppermute | solution.py:368
  5.3 1.3 %collective-permute-start = (bf16[48,128]{1,0:T(8,128)(2,1)S(1)}, bf16[48,128]{1,0:T(8,128)(2,1)S(1)}, u32[]{:S(2)}, u32[]{:S(2)}) collective-permute-start(bf16[48,128]{1,0:T(8,128)(2,1)S(1)} %get-tuple-element.45), channel_id=1, source_target_pairs={{1,0},{2,1},{3,2},{4,3},{5,4},{6,5},{7,6},{8,7},{9,8},{10,9},{11,1... | collective-permute-start | bytes 36872 | tf_op jit(solution)/shard_map/ppermute | solution.py:371
  6.6 1.1 %pad_maximum_fusion.narrow_ref = bf16[2560,128]{1,0:T(8,128)(2,1)S(1)} fusion(bf16[128,128]{1,0:T(8,128)(2,1)} %param.17, bf16[512,128]{1,0:T(8,128)(2,1)} %bitcast.5, bf16[1536,128]{1,0:T(8,128)(2,1)} %bitcast.4, bf16[384,128]{1,0:T(8,128)(2,1)} %param.11), kind=kLoop, calls=%fused_computation | loop fusion | flops 2621440 | bytes 1310720 | tf_op jit(solution)/shard_map/concatenate | solution.py:372
  7.8 2.8 %shard_map.122 = (bf16[384,128]{1,0:T(8,128)(2,1)S(1)}, bf16[384,128]{1,0:T(8,128)(2,1)S(1)}, bf16[384,128]{1,0:T(8,128)(2,1)S(1)}, f32[384,128]{1,0:T(8,128)S(1)}, bf16[256,128]{1,0:T(8,128)(2,1)S(1)}) custom-call(bf16[2560,128]{1,0:T(8,128)(2,1)S(1)} %pad_maximum_fusion.narrow_ref), custom_call_target="tpu_custom_call" | custom-call | flops 200000000 | bytes 1000000 | tf_op jit(solution)/shard_map/pallas_call | solution.py:377
  10.6 0.4 collective-permute-done.right_ref
  10.9 2.4 %shard_map.123 = (f32[384,128]{1,0:T(8,128)S(1)}, f32[48,768]{1,0:T(8,128)S(1)}, bf16[48,768]{1,0:T(8,128)(2,1)S(1)}) custom-call(bf16[48,128]{1,0:T(8,128)(2,1)S(1)} %collective-permute-done.right_ref, bf16[48,128]{1,0:T(8,128)(2,1)S(1)} %collective-permute-done.1.left_ref, bf16[2560,128]{1,0:T(8,128)(2,1)S(1)} %pad_maximum_fusion.narrow_ref, ...), custom_call_target="tpu_custom_call" | custom-call | flops 200000000 | bytes 2000000 | tf_op jit(solution)/shard_map/pallas_call | solution.py:384
  13.3 7.1 %collective-permute-start.3 = (bf16[48,768]{1,0:T(8,128)(2,1)S(1)}, bf16[48,768]{1,0:T(8,128)(2,1)S(1)}, u32[]{:S(2)}, u32[]{:S(2)}) collective-permute-start(bf16[48,768]{1,0:T(8,128)(2,1)S(1)} %get-tuple-element.28.norm_ref), channel_id=1, source_target_pairs={{0,4},{1,5},{2,6},{3,7},{4,0},{5,1},{6,2},{7,3},{8,12},{9,13},{10,... | collective-permute-start | bytes 221192 | tf_op jit(solution)/shard_map/ppermute | solution.py:401
  20.4 3.2 %collective-permute-start.2 = (bf16[48,768]{1,0:T(8,128)(2,1)S(1)}, bf16[48,768]{1,0:T(8,128)(2,1)S(1)}, u32[]{:S(2)}, u32[]{:S(2)}) collective-permute-start(bf16[48,768]{1,0:T(8,128)(2,1)S(1)} %get-tuple-element.28.norm_ref), channel_id=1, source_target_pairs={{0,32},{1,48},{2,0},{3,16},{4,96},{5,112},{6,64},{7,80},{8,40},{9,... | collective-permute-start | bytes 221192 | tf_op jit(solution)/shard_map/ppermute | solution.py:400
  23.6 0.0 collective-permute-done.3
  23.6 2.6 %collective-permute-done.2 = bf16[48,768]{1,0:T(8,128)(2,1)S(1)} collective-permute-done((bf16[48,768]{1,0:T(8,128)(2,1)S(1)}, bf16[48,768]{1,0:T(8,128)(2,1)S(1)}, u32[]{:S(2)}, u32[]{:S(2)}) %collective-permute-start.2) | collective-permute-done | bytes 73760 | tf_op jit(solution)/shard_map/ppermute | solution.py:400
  26.3 0.9 %broadcast_in_dim.2 = bf16[8,48,768]{2,1,0:T(8,128)(2,1)} broadcast(bf16[48,768]{1,0:T(8,128)(2,1)S(1)} %collective-permute-done.2), dimensions={1,2} | broadcast | bytes 663552 | tf_op jit(solution)/shard_map/broadcast_in_dim | solution.py:406
  27.1 5.8 %all-to-all-start = ((bf16[8,48,768]{2,1,0:T(8,128)(2,1)}), bf16[8,48,768]{2,1,0:T(8,128)(2,1)S(1)}, u32[]{:S(2)}, u32[]{:S(2)}) async-start(bf16[8,48,768]{2,1,0:T(8,128)(2,1)} %broadcast_in_dim.2), calls=%async_computation | async-start | bytes 1179648 | tf_op jit(solution)/shard_map/all_to_all | solution.py:405
  33.0 3.2 %collective-permute-start.5 = (bf16[96,768]{1,0:T(8,128)(2,1)S(1)}, bf16[96,768]{1,0:T(8,128)(2,1)S(1)}, u32[]{:S(2)}, u32[]{:S(2)}) collective-permute-start(bf16[96,768]{1,0:T(8,128)(2,1)S(1)} %pad_maximum_fusion.1.own_ref), channel_id=1, source_target_pairs={{0,3},{1,0},{2,1},{3,2},{4,7},{5,4},{6,5},{7,6},{8,11},{9,8},{10,9... | collective-permute-start | bytes 442376 | tf_op jit(solution)/shard_map/ppermute | solution.py:410
  36.2 5.7 %all-to-all-done.blocks_ref = bf16[8,48,768]{2,1,0:T(8,128)(2,1)S(1)} async-done(((bf16[8,48,768]{2,1,0:T(8,128)(2,1)}), bf16[8,48,768]{2,1,0:T(8,128)(2,1)S(1)}, u32[]{:S(2)}, u32[]{:S(2)}) %all-to-all-start) | async-done | bytes 589856 | tf_op jit(solution)/shard_map/all_to_all | solution.py:405
  41.9 3.3 %shard_map.124 = (bf16[8,384,128]{2,1,0:T(8,128)(2,1)S(1)}, bf16[8,384,128]{2,1,0:T(8,128)(2,1)S(1)}, bf16[2,768,768]{2,1,0:T(8,128)(2,1)S(1)}) custom-call(bf16[8,48,768]{2,1,0:T(8,128)(2,1)S(1)} %all-to-all-done.blocks_ref, bf16[4,768,768]{2,1,0:T(8,128)(2,1)} %proj_hbm.3), custom_call_target="tpu_custom_call" | custom-call | flops 1000000 | bytes 100000 | tf_op jit(solution)/shard_map/pallas_call | solution.py:418
  45.2 0.3 collective-permute-start.7
  45.5 1.9 %shard_map.125 = (bf16[8,384,128]{2,1,0:T(8,128)(2,1)S(1)}, f32[48,768]{1,0:T(8,128)S(1)}) custom-call(bf16[96,768]{1,0:T(8,128)(2,1)S(1)} %pad_maximum_fusion.1.own_ref, bf16[96,768]{1,0:T(8,128)(2,1)S(1)} %collective-permute-done.4.far_ref, bf16[96,768]{1,0:T(8,128)(2,1)S(1)} %collective-permute-done.5.before_ref, ...), custom_call_target="tpu_custom_call" | custom-call | flops 1000000 | bytes 100000 | tf_op jit(solution)/shard_map/pallas_call | solution.py:432
  47.5 0.0 collective-permute-done.7.blocks_ref
  47.5 10.4 %shard_map.126 = bf16[384,896]{1,0:T(8,128)(2,1)S(1)} custom-call(bf16[8,384,128]{2,1,0:T(8,128)(2,1)S(1)} %get-tuple-element.36.q_ref, bf16[8,384,128]{2,1,0:T(8,128)(2,1)S(1)} %get-tuple-element.37.k_ref, bf16[8,384,128]{2,1,0:T(8,128)(2,1)S(1)} %get-tuple-element.38.v_ref, bf16[8,48,768]{2,1,0:T(8,128)(2,1)S(1)} %collective-permute-done.7.blocks_ref, ...), custom_call_target="tpu_custom_call" | custom-call | flops 6000000000 | bytes 14000000 | tf_op jit(solution)/shard_map/pallas_call | solution.py:440
  57.9 0.0 copy-start.1
  57.9 0.0 copy-start.3
  57.9 18.3 %all_to_all.10.part_ref = bf16[8,48,896]{2,1,0:T(8,128)(2,1)S(1)} all-to-all(bf16[8,48,896]{2,1,0:T(8,128)(2,1)S(1)} %bitcast.3), channel_id=1, replica_groups=mesh['row'=16,'col'=8] {'col'}, dimensions={0} | all-to-all | bytes 1376256 | tf_op jit(solution)/shard_map/all_to_all | solution.py:453
  76.3 1.9 %shard_map.127 = (bf16[384,128]{1,0:T(8,128)(2,1)}, bf16[48,768]{1,0:T(8,128)(2,1)}) custom-call(bf16[8,48,896]{2,1,0:T(8,128)(2,1)S(1)} %all_to_all.10.part_ref, f32[48,768]{1,0:T(8,128)S(1)} %get-tuple-element.41.gate_ref, f32[48,768]{1,0:T(8,128)S(1)} %get-tuple-element.42.single_ref, f32[384,128]{1,0:T(8,128)S(1)} %get-tuple-element.43.mid_ref, ...), custom_call_target="tpu_custom_call" | custom-call | flops 400000000 | bytes 5000000 | tf_op jit(solution)/shard_map/pallas_call | solution.py:454
  (17 shorter events, 0.0 us)
Async XLA Ops:
  0.6 10.3 %copy-start.5 = (s32[1,384]{1,0:T(1,128)S(1)}, s32[1,384]{1,0:T(1,128)}, u32[]{:S(2)}) copy-start(s32[1,384]{1,0:T(1,128)} %owner_ref.3) | copy-start | bytes 4612
  0.6 10.3 %copy-start.2 = (bf16[128,768]{1,0:T(8,128)(2,1)S(1)}, bf16[128,768]{1,0:T(8,128)(2,1)}, u32[]{:S(2)}) copy-start(bf16[128,768]{1,0:T(8,128)(2,1)} %pool_ref.1) | copy-start | bytes 589828
  0.7 10.3 %copy-start.4 = (bf16[48,768]{1,0:T(8,128)(2,1)S(1)}, bf16[48,768]{1,0:T(8,128)(2,1)}, u32[]{:S(2)}) copy-start(bf16[48,768]{1,0:T(8,128)(2,1)} %input_ref.1) | copy-start | bytes 221188
  1.4 9.1 %collective-permute-start.1 = (bf16[48,128]{1,0:T(8,128)(2,1)S(1)}, bf16[48,128]{1,0:T(8,128)(2,1)S(1)}, u32[]{:S(2)}, u32[]{:S(2)}) collective-permute-start(bf16[48,128]{1,0:T(8,128)(2,1)S(1)} %get-tuple-element.44), channel_id=1, source_target_pairs={{0,1},{1,2},{2,3},{3,4},{4,5},{5,6},{6,7},{7,8},{8,9},{9,10},{10,1... | collective-permute-start | bytes 36872 | tf_op jit(solution)/shard_map/ppermute | solution.py:368
  5.3 5.6 %collective-permute-start = (bf16[48,128]{1,0:T(8,128)(2,1)S(1)}, bf16[48,128]{1,0:T(8,128)(2,1)S(1)}, u32[]{:S(2)}, u32[]{:S(2)}) collective-permute-start(bf16[48,128]{1,0:T(8,128)(2,1)S(1)} %get-tuple-element.45), channel_id=1, source_target_pairs={{1,0},{2,1},{3,2},{4,3},{5,4},{6,5},{7,6},{8,7},{9,8},{10,9},{11,1... | collective-permute-start | bytes 36872 | tf_op jit(solution)/shard_map/ppermute | solution.py:371
  13.3 10.3 %collective-permute-start.3 = (bf16[48,768]{1,0:T(8,128)(2,1)S(1)}, bf16[48,768]{1,0:T(8,128)(2,1)S(1)}, u32[]{:S(2)}, u32[]{:S(2)}) collective-permute-start(bf16[48,768]{1,0:T(8,128)(2,1)S(1)} %get-tuple-element.28.norm_ref), channel_id=1, source_target_pairs={{0,4},{1,5},{2,6},{3,7},{4,0},{5,1},{6,2},{7,3},{8,12},{9,13},{10,... | collective-permute-start | bytes 221192 | tf_op jit(solution)/shard_map/ppermute | solution.py:401
  20.4 5.9 %collective-permute-start.2 = (bf16[48,768]{1,0:T(8,128)(2,1)S(1)}, bf16[48,768]{1,0:T(8,128)(2,1)S(1)}, u32[]{:S(2)}, u32[]{:S(2)}) collective-permute-start(bf16[48,768]{1,0:T(8,128)(2,1)S(1)} %get-tuple-element.28.norm_ref), channel_id=1, source_target_pairs={{0,32},{1,48},{2,0},{3,16},{4,96},{5,112},{6,64},{7,80},{8,40},{9,... | collective-permute-start | bytes 221192 | tf_op jit(solution)/shard_map/ppermute | solution.py:400
  27.1 14.8 %all-to-all-start = ((bf16[8,48,768]{2,1,0:T(8,128)(2,1)}), bf16[8,48,768]{2,1,0:T(8,128)(2,1)S(1)}, u32[]{:S(2)}, u32[]{:S(2)}) async-start(bf16[8,48,768]{2,1,0:T(8,128)(2,1)} %broadcast_in_dim.2), calls=%async_computation | async-start | bytes 1179648 | tf_op jit(solution)/shard_map/all_to_all | solution.py:405
  33.0 12.2 %collective-permute-start.6 = (bf16[96,768]{1,0:T(8,128)(2,1)S(1)}, bf16[96,768]{1,0:T(8,128)(2,1)S(1)}, u32[]{:S(2)}, u32[]{:S(2)}) collective-permute-start(bf16[96,768]{1,0:T(8,128)(2,1)S(1)} %pad_maximum_fusion.1.own_ref), channel_id=1, source_target_pairs={{0,1},{1,2},{2,3},{3,0},{4,5},{5,6},{6,7},{7,4},{8,9},{9,10},{10,1... | collective-permute-start | bytes 442376 | tf_op jit(solution)/shard_map/ppermute | solution.py:410
  33.0 12.2 %collective-permute-start.5 = (bf16[96,768]{1,0:T(8,128)(2,1)S(1)}, bf16[96,768]{1,0:T(8,128)(2,1)S(1)}, u32[]{:S(2)}, u32[]{:S(2)}) collective-permute-start(bf16[96,768]{1,0:T(8,128)(2,1)S(1)} %pad_maximum_fusion.1.own_ref), channel_id=1, source_target_pairs={{0,3},{1,0},{2,1},{3,2},{4,7},{5,4},{6,5},{7,6},{8,11},{9,8},{10,9... | collective-permute-start | bytes 442376 | tf_op jit(solution)/shard_map/ppermute | solution.py:410
  36.2 9.0 %collective-permute-start.4 = (bf16[96,768]{1,0:T(8,128)(2,1)S(1)}, bf16[96,768]{1,0:T(8,128)(2,1)S(1)}, u32[]{:S(2)}, u32[]{:S(2)}) collective-permute-start(bf16[96,768]{1,0:T(8,128)(2,1)S(1)} %pad_maximum_fusion.1.own_ref), channel_id=1, source_target_pairs={{0,2},{1,3},{2,0},{3,1},{4,6},{5,7},{6,4},{7,5},{8,10},{9,11},{10,... | collective-permute-start | bytes 442376 | tf_op jit(solution)/shard_map/ppermute | solution.py:410
  41.9 3.6 %copy-start = (bf16[4,768,768]{2,1,0:T(8,128)(2,1)S(1)}, bf16[4,768,768]{2,1,0:T(8,128)(2,1)}, u32[]{:S(2)}) copy-start(bf16[4,768,768]{2,1,0:T(8,128)(2,1)} %proj_hbm.3) | copy-start | bytes 14155780
  45.2 2.3 %collective-permute-start.7 = (bf16[8,48,768]{2,1,0:T(8,128)(2,1)S(1)}, bf16[8,48,768]{2,1,0:T(8,128)(2,1)S(1)}, u32[]{:S(2)}, u32[]{:S(2)}) collective-permute-start(bf16[8,48,768]{2,1,0:T(8,128)(2,1)S(1)} %all-to-all-done.blocks_ref), channel_id=1, source_target_pairs={{0,8},{8,0},{16,24},{24,16},{32,40},{40,32},{48,56},{56,48},{64,72... | collective-permute-start | bytes 1769480 | tf_op jit(solution)/shard_map/ppermute | solution.py:431
  57.9 18.4 %copy-start.1 = (bf16[768,768]{1,0:T(8,128)(2,1)S(1)}, bf16[768,768]{1,0:T(8,128)(2,1)}, u32[]{:S(2)}) copy-start(bf16[768,768]{1,0:T(8,128)(2,1)} %output_ref.1) | copy-start | bytes 3538948
  57.9 18.3 %copy-start.3 = (bf16[768,128]{1,0:T(8,128)(2,1)S(1)}, bf16[768,128]{1,0:T(8,128)(2,1)}, u32[]{:S(2)}) copy-start(bf16[768,128]{1,0:T(8,128)(2,1)} %back_ref.1) | copy-start | bytes 589828

commit v12 on v11

--- a/solution.py
+++ b/solution.py
@@ -230,10 +230,10 @@
     copies = [
         pltpu.make_async_copy(proj_hbm.at[1 + i], key_ref.at[i], sems.at[i]) for i in range(2)
     ]
-    for copy in copies:
-        copy.start()
+    copies[0].start()
     into = places()
     copies[0].wait()
+    copies[1].start()
     key_rows(blocks_ref, key_ref[0], into, k_ref)
     copies[1].wait()
     value_rows(blocks_ref, key_ref[1], into, v_ref)
@@ -245,10 +245,10 @@
     copies = [
         pltpu.make_async_copy(proj_hbm.at[3 * i], edge_ref.at[i], sems.at[i]) for i in range(2)
     ]
-    for copy in copies:
-        copy.start()
+    copies[0].start()
     into = places()
     copies[0].wait()
+    copies[1].start()
     query_rows(
         [own_ref[...], after_ref[...], before_ref[...], far_ref[...]], edge_ref[0], into, q_ref
     )

time: 78.5 us -> 79.2 us (level)
  transfers between devices with their start and end apart: 9 -> 9, of which waited for: 3 -> 3; matrix products, arithmetic and copies ran while one was open for 1% -> 1% of each run, Pallas kernels for 10% -> 11%
where the time goes in v12:
time: 79.2 us; the launch traced here: 78.8 us
  starting transfers between devices  24.8 us (31%)
  Pallas kernels  23.3 us (29%)
  blocking collectives  18.3 us (23%)
  waiting for transfers between devices  8.75 us (11%)
  local copies, waits for them, and re-layouts  1.67 us (2%)
  other arithmetic  1.15 us (1%)
  between operations  0.8 us (1%)
    all_to_all x1, blocking collectives, per_device(): parts = lax.all_to_all(parts.reshape(cols, tokens, wide), 'col', 0, 0)  18.3 us
    pallas_call x1, Pallas kernels, per_device(): call(token_step, shape((q_count, wide), BF16), MOST, (6000000000, 1400000...  10.4 us
    ppermute x1, starting transfers between devices, per_device(): lax.ppermute(norm, 'col', [(i, (i + ring) % cols) for i in range(cols)])  7.12 us
    all_to_all x1, starting transfers between devices, per_device(): lax.all_to_all(jnp.broadcast_to(turned[None], (rows // 2, tokens, depth))...  5.82 us
    all_to_all x1, waiting for transfers between devices, per_device(): lax.all_to_all(jnp.broadcast_to(turned[None], (rows // 2, tokens, depth))...  5.7 us
    pallas_call x1, Pallas kernels, per_device(): call(near_step, (shape((PAIRS, half, lane), BF16), shape((PAIRS, half, la...  3.94 us
    ppermute x1, starting transfers between devices, per_device(): lax.ppermute(atom_state[count - REACH:], BOTH, [(i, i + 1) for i in range...  3.89 us
    ppermute x3, starting transfers between devices, per_device(): lax.ppermute(own, 'col', [(i, i // ring * ring + (i + step) % ring) for i...  3.23 us
  transfers between devices with their start and end apart: 9, of which 3 were waited for; matrix products, arithmetic and copies ran while one was open for 1% of the time, Pallas kernels for 11%

profile of v12, /device:TPU:0, one launch (start us, length us, event | category | flops | bytes accessed | tf_op | source)
XLA Modules:
  0.0 78.8 jit_solution(18446353081029045010)
XLA Ops:
  0.7 0.8 fusion
  1.4 3.9 %collective-permute-start.1 = (bf16[48,128]{1,0:T(8,128)(2,1)S(1)}, bf16[48,128]{1,0:T(8,128)(2,1)S(1)}, u32[]{:S(2)}, u32[]{:S(2)}) collective-permute-start(bf16[48,128]{1,0:T(8,128)(2,1)S(1)} %get-tuple-element.44), channel_id=1, source_target_pairs={{0,1},{1,2},{2,3},{3,4},{4,5},{5,6},{6,7},{7,8},{8,9},{9,10},{10,1... | collective-permute-start | bytes 36872 | tf_op jit(solution)/shard_map/ppermute | solution.py:368
  5.3 1.3 %collective-permute-start = (bf16[48,128]{1,0:T(8,128)(2,1)S(1)}, bf16[48,128]{1,0:T(8,128)(2,1)S(1)}, u32[]{:S(2)}, u32[]{:S(2)}) collective-permute-start(bf16[48,128]{1,0:T(8,128)(2,1)S(1)} %get-tuple-element.45), channel_id=1, source_target_pairs={{1,0},{2,1},{3,2},{4,3},{5,4},{6,5},{7,6},{8,7},{9,8},{10,9},{11,1... | collective-permute-start | bytes 36872 | tf_op jit(solution)/shard_map/ppermute | solution.py:371
  6.6 1.1 %pad_maximum_fusion.narrow_ref = bf16[2560,128]{1,0:T(8,128)(2,1)S(1)} fusion(bf16[128,128]{1,0:T(8,128)(2,1)} %param.17, bf16[512,128]{1,0:T(8,128)(2,1)} %bitcast.5, bf16[1536,128]{1,0:T(8,128)(2,1)} %bitcast.4, bf16[384,128]{1,0:T(8,128)(2,1)} %param.11), kind=kLoop, calls=%fused_computation | loop fusion | flops 2621440 | bytes 1310720 | tf_op jit(solution)/shard_map/concatenate | solution.py:372
  7.8 2.8 %shard_map.122 = (bf16[384,128]{1,0:T(8,128)(2,1)S(1)}, bf16[384,128]{1,0:T(8,128)(2,1)S(1)}, bf16[384,128]{1,0:T(8,128)(2,1)S(1)}, f32[384,128]{1,0:T(8,128)S(1)}, bf16[256,128]{1,0:T(8,128)(2,1)S(1)}) custom-call(bf16[2560,128]{1,0:T(8,128)(2,1)S(1)} %pad_maximum_fusion.narrow_ref), custom_call_target="tpu_custom_call" | custom-call | flops 200000000 | bytes 1000000 | tf_op jit(solution)/shard_map/pallas_call | solution.py:377
  10.6 0.4 collective-permute-done.right_ref
  10.9 2.4 %shard_map.123 = (f32[384,128]{1,0:T(8,128)S(1)}, f32[48,768]{1,0:T(8,128)S(1)}, bf16[48,768]{1,0:T(8,128)(2,1)S(1)}) custom-call(bf16[48,128]{1,0:T(8,128)(2,1)S(1)} %collective-permute-done.right_ref, bf16[48,128]{1,0:T(8,128)(2,1)S(1)} %collective-permute-done.1.left_ref, bf16[2560,128]{1,0:T(8,128)(2,1)S(1)} %pad_maximum_fusion.narrow_ref, ...), custom_call_target="tpu_custom_call" | custom-call | flops 200000000 | bytes 2000000 | tf_op jit(solution)/shard_map/pallas_call | solution.py:384
  13.3 7.1 %collective-permute-start.3 = (bf16[48,768]{1,0:T(8,128)(2,1)S(1)}, bf16[48,768]{1,0:T(8,128)(2,1)S(1)}, u32[]{:S(2)}, u32[]{:S(2)}) collective-permute-start(bf16[48,768]{1,0:T(8,128)(2,1)S(1)} %get-tuple-element.28.norm_ref), channel_id=1, source_target_pairs={{0,4},{1,5},{2,6},{3,7},{4,0},{5,1},{6,2},{7,3},{8,12},{9,13},{10,... | collective-permute-start | bytes 221192 | tf_op jit(solution)/shard_map/ppermute | solution.py:401
  20.4 3.2 %collective-permute-start.2 = (bf16[48,768]{1,0:T(8,128)(2,1)S(1)}, bf16[48,768]{1,0:T(8,128)(2,1)S(1)}, u32[]{:S(2)}, u32[]{:S(2)}) collective-permute-start(bf16[48,768]{1,0:T(8,128)(2,1)S(1)} %get-tuple-element.28.norm_ref), channel_id=1, source_target_pairs={{0,32},{1,48},{2,0},{3,16},{4,96},{5,112},{6,64},{7,80},{8,40},{9,... | collective-permute-start | bytes 221192 | tf_op jit(solution)/shard_map/ppermute | solution.py:400
  23.6 0.0 collective-permute-done.3
  23.6 2.6 %collective-permute-done.2 = bf16[48,768]{1,0:T(8,128)(2,1)S(1)} collective-permute-done((bf16[48,768]{1,0:T(8,128)(2,1)S(1)}, bf16[48,768]{1,0:T(8,128)(2,1)S(1)}, u32[]{:S(2)}, u32[]{:S(2)}) %collective-permute-start.2) | collective-permute-done | bytes 73760 | tf_op jit(solution)/shard_map/ppermute | solution.py:400
  26.3 0.9 %broadcast_in_dim.2 = bf16[8,48,768]{2,1,0:T(8,128)(2,1)} broadcast(bf16[48,768]{1,0:T(8,128)(2,1)S(1)} %collective-permute-done.2), dimensions={1,2} | broadcast | bytes 663552 | tf_op jit(solution)/shard_map/broadcast_in_dim | solution.py:406
  27.1 5.8 %all-to-all-start = ((bf16[8,48,768]{2,1,0:T(8,128)(2,1)}), bf16[8,48,768]{2,1,0:T(8,128)(2,1)S(1)}, u32[]{:S(2)}, u32[]{:S(2)}) async-start(bf16[8,48,768]{2,1,0:T(8,128)(2,1)} %broadcast_in_dim.2), calls=%async_computation | async-start | bytes 1179648 | tf_op jit(solution)/shard_map/all_to_all | solution.py:405
  33.0 3.2 %collective-permute-start.5 = (bf16[96,768]{1,0:T(8,128)(2,1)S(1)}, bf16[96,768]{1,0:T(8,128)(2,1)S(1)}, u32[]{:S(2)}, u32[]{:S(2)}) collective-permute-start(bf16[96,768]{1,0:T(8,128)(2,1)S(1)} %pad_maximum_fusion.1.own_ref), channel_id=1, source_target_pairs={{0,3},{1,0},{2,1},{3,2},{4,7},{5,4},{6,5},{7,6},{8,11},{9,8},{10,9... | collective-permute-start | bytes 442376 | tf_op jit(solution)/shard_map/ppermute | solution.py:410
  36.2 5.7 %all-to-all-done.blocks_ref = bf16[8,48,768]{2,1,0:T(8,128)(2,1)S(1)} async-done(((bf16[8,48,768]{2,1,0:T(8,128)(2,1)}), bf16[8,48,768]{2,1,0:T(8,128)(2,1)S(1)}, u32[]{:S(2)}, u32[]{:S(2)}) %all-to-all-start) | async-done | bytes 589856 | tf_op jit(solution)/shard_map/all_to_all | solution.py:405
  41.9 3.9 %shard_map.124 = (bf16[8,384,128]{2,1,0:T(8,128)(2,1)S(1)}, bf16[8,384,128]{2,1,0:T(8,128)(2,1)S(1)}, bf16[2,768,768]{2,1,0:T(8,128)(2,1)S(1)}) custom-call(bf16[8,48,768]{2,1,0:T(8,128)(2,1)S(1)} %all-to-all-done.blocks_ref, bf16[4,768,768]{2,1,0:T(8,128)(2,1)} %proj_hbm.3), custom_call_target="tpu_custom_call" | custom-call | flops 1000000 | bytes 100000 | tf_op jit(solution)/shard_map/pallas_call | solution.py:418
  45.9 0.3 collective-permute-start.7
  46.2 1.9 %shard_map.125 = (bf16[8,384,128]{2,1,0:T(8,128)(2,1)S(1)}, f32[48,768]{1,0:T(8,128)S(1)}) custom-call(bf16[96,768]{1,0:T(8,128)(2,1)S(1)} %pad_maximum_fusion.1.own_ref, bf16[96,768]{1,0:T(8,128)(2,1)S(1)} %collective-permute-done.4.far_ref, bf16[96,768]{1,0:T(8,128)(2,1)S(1)} %collective-permute-done.5.before_ref, ...), custom_call_target="tpu_custom_call" | custom-call | flops 1000000 | bytes 100000 | tf_op jit(solution)/shard_map/pallas_call | solution.py:432
  48.1 0.0 collective-permute-done.7.blocks_ref
  48.2 10.4 %shard_map.126 = bf16[384,896]{1,0:T(8,128)(2,1)S(1)} custom-call(bf16[8,384,128]{2,1,0:T(8,128)(2,1)S(1)} %get-tuple-element.36.q_ref, bf16[8,384,128]{2,1,0:T(8,128)(2,1)S(1)} %get-tuple-element.37.k_ref, bf16[8,384,128]{2,1,0:T(8,128)(2,1)S(1)} %get-tuple-element.38.v_ref, bf16[8,48,768]{2,1,0:T(8,128)(2,1)S(1)} %collective-permute-done.7.blocks_ref, ...), custom_call_target="tpu_custom_call" | custom-call | flops 6000000000 | bytes 14000000 | tf_op jit(solution)/shard_map/pallas_call | solution.py:440
  58.5 0.0 copy-start.1
  58.6 0.0 copy-start.3
  58.6 18.3 %all_to_all.10.part_ref = bf16[8,48,896]{2,1,0:T(8,128)(2,1)S(1)} all-to-all(bf16[8,48,896]{2,1,0:T(8,128)(2,1)S(1)} %bitcast.3), channel_id=1, replica_groups=mesh['row'=16,'col'=8] {'col'}, dimensions={0} | all-to-all | bytes 1376256 | tf_op jit(solution)/shard_map/all_to_all | solution.py:453
  76.9 1.9 %shard_map.127 = (bf16[384,128]{1,0:T(8,128)(2,1)}, bf16[48,768]{1,0:T(8,128)(2,1)}) custom-call(bf16[8,48,896]{2,1,0:T(8,128)(2,1)S(1)} %all_to_all.10.part_ref, f32[48,768]{1,0:T(8,128)S(1)} %get-tuple-element.41.gate_ref, f32[48,768]{1,0:T(8,128)S(1)} %get-tuple-element.42.single_ref, f32[384,128]{1,0:T(8,128)S(1)} %get-tuple-element.43.mid_ref, ...), custom_call_target="tpu_custom_call" | custom-call | flops 400000000 | bytes 5000000 | tf_op jit(solution)/shard_map/pallas_call | solution.py:454
  (17 shorter events, 0.0 us)
Async XLA Ops:
  0.6 10.3 %copy-start.5 = (s32[1,384]{1,0:T(1,128)S(1)}, s32[1,384]{1,0:T(1,128)}, u32[]{:S(2)}) copy-start(s32[1,384]{1,0:T(1,128)} %owner_ref.3) | copy-start | bytes 4612
  0.6 10.3 %copy-start.2 = (bf16[128,768]{1,0:T(8,128)(2,1)S(1)}, bf16[128,768]{1,0:T(8,128)(2,1)}, u32[]{:S(2)}) copy-start(bf16[128,768]{1,0:T(8,128)(2,1)} %pool_ref.1) | copy-start | bytes 589828
  0.7 10.3 %copy-start.4 = (bf16[48,768]{1,0:T(8,128)(2,1)S(1)}, bf16[48,768]{1,0:T(8,128)(2,1)}, u32[]{:S(2)}) copy-start(bf16[48,768]{1,0:T(8,128)(2,1)} %input_ref.1) | copy-start | bytes 221188
  1.4 9.1 %collective-permute-start.1 = (bf16[48,128]{1,0:T(8,128)(2,1)S(1)}, bf16[48,128]{1,0:T(8,128)(2,1)S(1)}, u32[]{:S(2)}, u32[]{:S(2)}) collective-permute-start(bf16[48,128]{1,0:T(8,128)(2,1)S(1)} %get-tuple-element.44), channel_id=1, source_target_pairs={{0,1},{1,2},{2,3},{3,4},{4,5},{5,6},{6,7},{7,8},{8,9},{9,10},{10,1... | collective-permute-start | bytes 36872 | tf_op jit(solution)/shard_map/ppermute | solution.py:368
  5.3 5.6 %collective-permute-start = (bf16[48,128]{1,0:T(8,128)(2,1)S(1)}, bf16[48,128]{1,0:T(8,128)(2,1)S(1)}, u32[]{:S(2)}, u32[]{:S(2)}) collective-permute-start(bf16[48,128]{1,0:T(8,128)(2,1)S(1)} %get-tuple-element.45), channel_id=1, source_target_pairs={{1,0},{2,1},{3,2},{4,3},{5,4},{6,5},{7,6},{8,7},{9,8},{10,9},{11,1... | collective-permute-start | bytes 36872 | tf_op jit(solution)/shard_map/ppermute | solution.py:371
  13.3 10.3 %collective-permute-start.3 = (bf16[48,768]{1,0:T(8,128)(2,1)S(1)}, bf16[48,768]{1,0:T(8,128)(2,1)S(1)}, u32[]{:S(2)}, u32[]{:S(2)}) collective-permute-start(bf16[48,768]{1,0:T(8,128)(2,1)S(1)} %get-tuple-element.28.norm_ref), channel_id=1, source_target_pairs={{0,4},{1,5},{2,6},{3,7},{4,0},{5,1},{6,2},{7,3},{8,12},{9,13},{10,... | collective-permute-start | bytes 221192 | tf_op jit(solution)/shard_map/ppermute | solution.py:401
  20.4 5.9 %collective-permute-start.2 = (bf16[48,768]{1,0:T(8,128)(2,1)S(1)}, bf16[48,768]{1,0:T(8,128)(2,1)S(1)}, u32[]{:S(2)}, u32[]{:S(2)}) collective-permute-start(bf16[48,768]{1,0:T(8,128)(2,1)S(1)} %get-tuple-element.28.norm_ref), channel_id=1, source_target_pairs={{0,32},{1,48},{2,0},{3,16},{4,96},{5,112},{6,64},{7,80},{8,40},{9,... | collective-permute-start | bytes 221192 | tf_op jit(solution)/shard_map/ppermute | solution.py:400
  27.1 14.8 %all-to-all-start = ((bf16[8,48,768]{2,1,0:T(8,128)(2,1)}), bf16[8,48,768]{2,1,0:T(8,128)(2,1)S(1)}, u32[]{:S(2)}, u32[]{:S(2)}) async-start(bf16[8,48,768]{2,1,0:T(8,128)(2,1)} %broadcast_in_dim.2), calls=%async_computation | async-start | bytes 1179648 | tf_op jit(solution)/shard_map/all_to_all | solution.py:405
  33.0 12.9 %collective-permute-start.6 = (bf16[96,768]{1,0:T(8,128)(2,1)S(1)}, bf16[96,768]{1,0:T(8,128)(2,1)S(1)}, u32[]{:S(2)}, u32[]{:S(2)}) collective-permute-start(bf16[96,768]{1,0:T(8,128)(2,1)S(1)} %pad_maximum_fusion.1.own_ref), channel_id=1, source_target_pairs={{0,1},{1,2},{2,3},{3,0},{4,5},{5,6},{6,7},{7,4},{8,9},{9,10},{10,1... | collective-permute-start | bytes 442376 | tf_op jit(solution)/shard_map/ppermute | solution.py:410
  33.0 12.9 %collective-permute-start.5 = (bf16[96,768]{1,0:T(8,128)(2,1)S(1)}, bf16[96,768]{1,0:T(8,128)(2,1)S(1)}, u32[]{:S(2)}, u32[]{:S(2)}) collective-permute-start(bf16[96,768]{1,0:T(8,128)(2,1)S(1)} %pad_maximum_fusion.1.own_ref), channel_id=1, source_target_pairs={{0,3},{1,0},{2,1},{3,2},{4,7},{5,4},{6,5},{7,6},{8,11},{9,8},{10,9... | collective-permute-start | bytes 442376 | tf_op jit(solution)/shard_map/ppermute | solution.py:410
  36.2 9.7 %collective-permute-start.4 = (bf16[96,768]{1,0:T(8,128)(2,1)S(1)}, bf16[96,768]{1,0:T(8,128)(2,1)S(1)}, u32[]{:S(2)}, u32[]{:S(2)}) collective-permute-start(bf16[96,768]{1,0:T(8,128)(2,1)S(1)} %pad_maximum_fusion.1.own_ref), channel_id=1, source_target_pairs={{0,2},{1,3},{2,0},{3,1},{4,6},{5,7},{6,4},{7,5},{8,10},{9,11},{10,... | collective-permute-start | bytes 442376 | tf_op jit(solution)/shard_map/ppermute | solution.py:410
  41.9 4.3 %copy-start = (bf16[4,768,768]{2,1,0:T(8,128)(2,1)S(1)}, bf16[4,768,768]{2,1,0:T(8,128)(2,1)}, u32[]{:S(2)}) copy-start(bf16[4,768,768]{2,1,0:T(8,128)(2,1)} %proj_hbm.3) | copy-start | bytes 14155780
  45.9 2.3 %collective-permute-start.7 = (bf16[8,48,768]{2,1,0:T(8,128)(2,1)S(1)}, bf16[8,48,768]{2,1,0:T(8,128)(2,1)S(1)}, u32[]{:S(2)}, u32[]{:S(2)}) collective-permute-start(bf16[8,48,768]{2,1,0:T(8,128)(2,1)S(1)} %all-to-all-done.blocks_ref), channel_id=1, source_target_pairs={{0,8},{8,0},{16,24},{24,16},{32,40},{40,32},{48,56},{56,48},{64,72... | collective-permute-start | bytes 1769480 | tf_op jit(solution)/shard_map/ppermute | solution.py:431
  58.5 18.4 %copy-start.1 = (bf16[768,768]{1,0:T(8,128)(2,1)S(1)}, bf16[768,768]{1,0:T(8,128)(2,1)}, u32[]{:S(2)}) copy-start(bf16[768,768]{1,0:T(8,128)(2,1)} %output_ref.1) | copy-start | bytes 3538948
  58.6 18.3 %copy-start.3 = (bf16[768,128]{1,0:T(8,128)(2,1)S(1)}, bf16[768,128]{1,0:T(8,128)(2,1)}, u32[]{:S(2)}) copy-start(bf16[768,128]{1,0:T(8,128)(2,1)} %back_ref.1) | copy-start | bytes 589828
